TPU v7x, 32 devices: a whole 2x2x4 slice. The times are simulated.
32 devices in a mesh: dom: 8 (over z, x), cls: 4 (over y, core).
Axes of the slice: x: 2, y: 2, z: 4, core: 2. Of those that a mesh axis runs over, the one named last changes fastest.
Arguments:
- particles: bfloat16 [256, 16384], P(('dom', 'cls')), may hold values from -6 to 6
- references: bfloat16 [64, 16384], P('cls'), may hold values from -0.046875 to 0.046875
- pose_weights: int32 [256, 24, 64], P(('dom', 'cls')), may hold values from 0 to 4
- class_mask: int32 [256, 64], P(('dom', 'cls')), may hold values 0 or 1
Outputs:
- class_scores: float32 [256, 64], P(('dom', 'cls'))
- class_sums: float32 [64, 16384], P('cls', 'dom')
All inputs are finite; a program needn't handle non-finite values. No bound on the sum of `class_mask` on one device may be relied on, other than what follows from the above.
Results may differ from a plain program's by a relative error of at most 0.0003.
Values may be sent and summed in bfloat16 or wider, within the bound.
No kernel may reach another device: no remote copies, remote signals or barrier semaphores. Data moves between devices by JAX's collectives and lax.ppermute only.
A program may use at most 128 MiB of HBM per device.

v0:
```python
import math

import jax
import jax.numpy as jnp
from jax import lax
from jax.sharding import PartitionSpec as P

CYCLES = 64
ANG = 256
ROT = 24


def turned(images, shift_by):
    shape_in = images.shape
    polar = images.reshape(shape_in[:-1] + (CYCLES, ANG))
    return jnp.roll(polar, shift_by, axis=-1).reshape(shape_in)


def on_device(particles, references, pose_weights, class_mask):
    n_rows = particles.shape[0]
    angle_step = ANG // ROT
    weights = pose_weights * class_mask[:, None, :]
    weights_f = weights.astype(jnp.float32)
    weights_b = weights.astype(jnp.bfloat16)
    rotated = jnp.stack([turned(particles, -r * angle_step) for r in range(ROT)], axis=0)
    rotated_rows = rotated.reshape(ROT * n_rows, rotated.shape[2])
    ref_piece = lax.all_gather(references, "cls", axis=0, tiled=True)
    width_now = ref_piece.shape[0]
    corr = jnp.dot(rotated_rows, ref_piece.T, preferred_element_type=jnp.float32)
    corr = corr.reshape(ROT, n_rows, width_now)
    weight_cols = weights_f
    scored = jnp.einsum("rnk,nrk->nk", corr, weight_cols) / ROT
    weight_cols = weights_b
    local_sums = lax.psum_scatter(
        jnp.einsum("nrk,rnl->kl", weight_cols, rotated, preferred_element_type=jnp.float32),
        "cls",
        scatter_dimension=0,
        tiled=True,
    )
    home_part = lax.psum_scatter(local_sums, "dom", scatter_dimension=1, tiled=True)
    particle_total = n_rows * lax.axis_size("dom") * lax.axis_size("cls")
    class_sums = home_part / math.sqrt(particle_total * ROT)
    return (scored, class_sums)


def solution(mesh):
    return jax.shard_map(
        on_device,
        mesh=mesh,
        in_specs=(
            P(("dom", "cls"), None),
            P("cls", None),
            P(("dom", "cls"), None, None),
            P(("dom", "cls"), None),
        ),
        out_specs=(P(("dom", "cls"), None), P("cls", "dom")),
        check_vma=False,
    )
```

profile of v0, /device:TPU:0, one launch (start us, length us, event | category | flops | bytes accessed | tf_op | source)
XLA Modules:
  0.0 300.9 jit_solution(10851470049415356779)
XLA Ops:
  7.2 1.1 slice.238
  8.4 0.9 slice.239
  9.3 1.1 slice.240
  10.4 0.9 slice.241
  11.3 1.1 slice.242
  13.3 1.1 slice.244
  15.3 1.1 slice.246
  16.4 1.6 slice.247
  18.0 1.1 slice.248
  19.1 1.6 slice.249
  20.6 1.8 slice.250
  22.5 1.6 slice.251
  24.0 1.8 slice.252
  25.8 1.6 slice.253
  42.5 0.9 copy.147
  43.7 0.9 copy.149
  45.5 1.0 stack_reshape.105
  46.5 1.0 copy.150
  47.5 0.9 copy.151
  49.3 1.8 stack_reshape.106
  51.0 1.0 copy.152
  52.0 0.9 copy.153
  53.8 1.8 stack_reshape.107
  55.5 1.0 copy.130
  56.5 0.9 copy.131
  58.3 1.7 stack_reshape.96
  60.0 1.0 copy.132
  61.0 0.9 copy.133
  62.8 1.8 stack_reshape.97
  64.6 1.0 copy.134
  65.6 0.9 copy.135
  67.3 1.8 stack_reshape.98
  69.1 1.0 copy.136
  70.1 0.9 copy.137
  71.8 1.8 stack_reshape.99
  73.6 0.9 copy.154
  75.4 1.7 stack_reshape.108
  77.2 0.9 copy.156
  79.0 1.7 stack_reshape.109
  80.7 0.9 copy.158
  82.6 1.8 stack_reshape.110
  84.3 0.9 copy.160
  86.2 1.8 stack_reshape.111
  87.9 0.9 copy.162
  89.7 1.7 stack_reshape.112
  91.5 0.9 copy.164
  93.3 1.7 stack_reshape.113
  95.1 0.9 copy.166
  96.9 1.8 stack_reshape.114
  98.7 0.9 copy.168
  100.5 1.8 stack_reshape.115
  102.3 0.9 copy.170
  104.1 1.7 stack_reshape.116
  105.8 0.9 copy.172
  107.7 1.7 stack_reshape.117
  110.3 1.8 stack_reshape.118
  112.1 1.2 copy.98
  113.3 34.4 %stack.3 = bf16[24,8,16384]{2,0,1:T(8,128)(2,1)} concatenate(bf16[1,8,16384]{2,0,1:T(2,128)(2,1)} %copy.98, bf16[1,8,16384]{2,0,1:T(2,128)(2,1)} %stack_reshape.96, bf16[1,8,16384]{2,0,1:T(2,128)(2,1)} %stack_reshape.97, bf16[1,8,16384]{2,0,1:T(2,128)(2,1)} %stack_reshape.98, bf16[1,8,16384]{2,0,1:T(2,128)(2,1)} %stack_reshape.99, bf16[1,8,16384]{2,0,1:T(2,128)(2,1)S(1)} %stack_reshape.100, ...), dimensions={0} | concatenate | bytes 12582912 | tf_op jit(solution)/shard_map/stack | solution.py:25
  147.7 6.2 %convolution_bitcast_fusion = f32[64,16384]{1,0:T(8,128)} fusion(bf16[24,8,16384]{2,0,1:T(8,128)(2,1)} %stack.3, s32[8,24,64]{2,1,0:T(8,128)S(1)} %copy-done.2, s32[8,64]{1,0:T(8,128)S(1)} %copy-done.1), kind=kOutput, calls=%fused_computation | convolution fusion | flops 402677760 | bytes 10536960 | tf_op jit(solution)/shard_map/nrk,rnl->kl/dot_general | solution.py:35
  154.7 46.6 %reduce-scatter.3.cloned.1.call-done = f32[16,16384]{1,0:T(8,128)} async-done(((f32[64,16384]{1,0:T(8,128)}), f32[16,16384]{1,0:T(8,128)}) %reduce-scatter.3.cloned.1.call-update) | async-done | bytes 1048592 | tf_op jit(solution)/shard_map/reduce_scatter | solution.py:34
  201.3 24.2 %all-gather.2.cloned.1.call-done = bf16[64,16384]{1,0:T(8,128)(2,1)} async-done(((bf16[16,16384]{1,0:T(8,128)(2,1)}), bf16[64,16384]{1,0:T(8,128)(2,1)}) %all-gather.2.cloned.1.call-update) | async-done | bytes 2097168 | tf_op jit(solution)/shard_map/all_gather | solution.py:27
  225.5 5.2 %fusion.8 = f32[8,64]{1,0:T(8,128)S(1)} fusion(bf16[24,8,16384]{2,0,1:T(8,128)(2,1)} %stack.3, bf16[64,16384]{1,0:T(8,128)(2,1)} %all-gather.2.cloned.1.call-done, s32[8,24,64]{2,1,0:T(8,128)S(1)} %copy-done.2, s32[8,64]{1,0:T(8,128)S(1)} %copy-done.1), kind=kOutput, calls=%fused_computation.5 | convolution fusion | flops 402701824 | bytes 8441856 | tf_op jit(solution)/shard_map/dot_general | solution.py:29
  231.3 61.4 %reduce-scatter.5.cloned.1.call-done = f32[16,2048]{1,0:T(8,128)} async-done(((f32[16,16384]{1,0:T(8,128)}), f32[16,2048]{1,0:T(8,128)}) %reduce-scatter.5.cloned.1.call-update) | async-done | bytes 131088 | tf_op jit(solution)/shard_map/reduce_scatter | solution.py:40
  292.8 1.6 broadcast_multiply_fusion
  (84 shorter events, 34.1 us)
Async XLA Ops:
  7.2 20.2 %copy-start = (bf16[8,16384]{1,0:T(8,128)(2,1)S(1)}, bf16[8,16384]{1,0:T(8,128)(2,1)}, u32[]{:S(2)}) copy-start(bf16[8,16384]{1,0:T(8,128)(2,1)} %param.4) | copy-start | bytes 786436
  7.2 194.1 %reduce-scatter.3.cloned.1.call-start = ((), (), s32[]{:S(2)}) async-start(), calls=%async_computation.3 | async-start | bytes 5242880 | tf_op jit(solution)/shard_map/reduce_scatter | solution.py:34
  113.3 34.4 %copy-start.1 = (s32[8,64]{1,0:T(8,128)S(1)}, s32[8,64]{1,0:T(8,128)}, u32[]{:S(2)}) copy-start(s32[8,64]{1,0:T(8,128)} %param.7) | copy-start | bytes 6148
  113.3 34.4 %copy-start.2 = (s32[8,24,64]{2,1,0:T(8,128)S(1)}, s32[8,24,64]{2,1,0:T(8,128)}, u32[]{:S(2)}) copy-start(s32[8,24,64]{2,1,0:T(8,128)} %param.6) | copy-start | bytes 147460
  153.9 71.6 %all-gather.2.cloned.1.call-start = ((), (), s32[]{:S(2)}) async-start(), calls=%async_computation.2 | async-start | bytes 2621440 | tf_op jit(solution)/shard_map/all_gather | solution.py:27
  154.6 138.1 %reduce-scatter.5.cloned.1.call-start = ((), (), s32[]{:S(2)}) async-start(), calls=%async_computation.4 | async-start | bytes 1179648 | tf_op jit(solution)/shard_map/reduce_scatter | solution.py:40
Sparse Core Ops, SparseCore 0:
  154.0 47.2 reduce-scatter.2
  202.9 22.5 all-gather.1
  229.3 63.4 reduce-scatter.4
where the time goes:
time: 306 us; the launch traced here: 301 us
  waiting for transfers between devices  133 us (43%)
  local copies, waits for them, and re-layouts  125 us (41%)
  other arithmetic  17.7 us (6%)
  between operations  14.2 us (5%)
  matrix products  11.4 us (4%)
    another operation x25, local copies, waits for them, and re-layouts, on_device(): jnp.stack([turned(particles, -r * angle_step) for r in range(ROT)], axis=0)  67.3 us
    reduce_scatter x1, waiting for transfers between devices, on_device(): lax.psum_scatter(local_sums, 'dom', scatter_dimension=1, tiled=True)  61.4 us
    reduce_scatter x1, waiting for transfers between devices, on_device(): lax.psum_scatter(jnp.einsum('nrk,rnl->kl', weight_cols, rotated, preferre...  46.6 us
    slice x35, local copies, waits for them, and re-layouts, turned(): return jnp.roll(polar, shift_by, axis=-1).reshape(shape_in)  33.7 us
    all_gather x1, waiting for transfers between devices, on_device(): ref_piece = lax.all_gather(references, 'cls', axis=0, tiled=True)  24.2 us
    unnamed x52, local copies, waits for them, and re-layouts  23.6 us
    concatenate x23, other arithmetic, turned(): return jnp.roll(polar, shift_by, axis=-1).reshape(shape_in)  15.5 us
    dot_general x1, matrix products, on_device(): jnp.einsum('nrk,rnl->kl', weight_cols, rotated, preferred_element_type=jn...  6.15 us
  transfers between devices with their start and end apart: 3, of which 3 were waited for; matrix products, arithmetic and copies ran while one was open for 2% of the time, Pallas kernels for 0%

commit v1 on v0

v1 whole, which is shorter than its diff:
```python
import math

import jax
import jax.numpy as jnp
from jax import lax
from jax.experimental import pallas as pl
from jax.experimental.pallas import tpu as pltpu
from jax.sharding import PartitionSpec as P

CYCLES = 64
ANG = 256
ROT = 24
STEP = ANG // ROT
FINE = 4
COARSE = ROT // FINE
LANES = 128
VMEM_BYTES = 48 * 1024 * 1024
f32 = jnp.float32
bf16 = jnp.bfloat16


def turn(x, shift):
    shift %= ANG
    if shift == 0:
        return x
    halves, rest = shift // LANES, shift % LANES
    lane = lax.broadcasted_iota(jnp.int32, (x.shape[0], LANES), 1)
    pieces = []
    for c in range(x.shape[1] // ANG):
        lo = x[:, c * ANG : c * ANG + LANES]
        hi = x[:, c * ANG + LANES : (c + 1) * ANG]
        if halves:
            lo, hi = hi, lo
        if rest:
            lo, hi = pltpu.roll(lo, rest, 1), pltpu.roll(hi, rest, 1)
            lo, hi = jnp.where(lane < rest, hi, lo), jnp.where(lane < rest, lo, hi)
        pieces += [lo, hi]
    return jnp.concatenate(pieces, axis=1)


def swap_blocks(x, me, block, blocks):
    lane = lax.broadcasted_iota(jnp.int32, x.shape, 1)
    width = x.shape[1]
    bit = 1
    while bit < blocks:
        g = block * bit
        upper = (lane // g) % 2 == 1
        swapped = jnp.where(upper, pltpu.roll(x, g, 1), pltpu.roll(x, width - g, 1))
        x = jnp.where((me // bit) % 2 == 1, swapped, x)
        bit *= 2
    return x


def pack_kernel(part_ref, pose_ref, mask_ref, out_ref):
    dom, n, _ = out_ref.shape
    cols = part_ref.shape[1] // dom
    mask = mask_ref[...]
    for d in range(dom):
        out_ref[d, :, :cols] = part_ref[:, d * cols : (d + 1) * cols]
    for i in range(COARSE):
        w = jnp.concatenate([pose_ref[:, FINE * i + j, :] * mask for j in range(FINE)], axis=1)
        w = w.astype(f32).astype(bf16)
        wide = w.shape[1]
        for d in range(dom):
            out_ref[d, :, cols + i * wide : cols + (i + 1) * wide] = w


def sums_kernel(me_ref, got_ref, keep_ref, send_ref, acc_ref):
    me = me_ref[0]
    groups, per, cols = acc_ref.shape
    k = groups * per
    wide = FINE * k
    dom, n, _ = got_ref.shape
    part = got_ref[:, :, :cols].astype(f32).reshape(dom * n, cols)
    stack = jnp.concatenate([turn(part, -STEP * FINE * i).astype(bf16) for i in range(COARSE)], axis=0)
    w = jnp.concatenate(
        [
            got_ref[:, :, cols + i * wide : cols + (i + 1) * wide].astype(f32).reshape(dom * n, wide).astype(bf16)
            for i in range(COARSE)
        ],
        axis=0,
    )
    total = None
    for j in range(FINE):
        t = lax.dot_general(
            w[:, j * k : (j + 1) * k], stack, (((0,), (0,)), ((), ())), preferred_element_type=f32
        )
        t = turn(t, -STEP * j)
        total = t if total is None else total + t
    acc_ref[...] = total.reshape(groups, per, cols)
    for m in range(groups // 2):
        keep_ref[m] = acc_ref[(2 * m) ^ me]
        send_ref[m] = acc_ref[(2 * m + 1) ^ me]


def scores_kernel(me_ref, part_ref, pose_ref, mask_ref, *refs):
    *blocks, out_ref = refs
    me = me_ref[0]
    n, length = part_ref.shape
    per = blocks[0].shape[0]
    k = per * len(blocks)
    chunk = 4 * ANG
    corr = None
    for c in range(length // chunk):
        at = slice(c * chunk, (c + 1) * chunk)
        part = part_ref[:, at].astype(f32)
        left = jnp.concatenate([turn(part, -STEP * FINE * i) for i in range(COARSE)], axis=0).astype(bf16)
        cls = jnp.concatenate([b[:, at].astype(f32) for b in blocks], axis=0)
        right = jnp.concatenate([turn(cls, STEP * j).astype(bf16) for j in range(FINE)], axis=0)
        more = lax.dot_general(left, right, (((1,), (1,)), ((), ())), preferred_element_type=f32)
        corr = more if corr is None else corr + more
    mask = mask_ref[...]
    total = jnp.zeros((n, FINE * k), f32)
    for i in range(COARSE):
        w = jnp.concatenate([pose_ref[:, FINE * i + j, :] * mask for j in range(FINE)], axis=1).astype(f32)
        total += swap_blocks(w, me, per, len(blocks)) * corr[i * n : (i + 1) * n]
    total = swap_blocks(total, me, per, len(blocks))
    out = total[:, :k]
    for j in range(1, FINE):
        out += total[:, j * k : (j + 1) * k]
    out_ref[...] = out / ROT


def on_device(particles, references, pose_weights, class_mask):
    n, length = particles.shape
    per = references.shape[0]
    k = class_mask.shape[1]
    dom, groups = lax.axis_size("dom"), lax.axis_size("cls")
    cols = length // dom
    me = lax.axis_index("cls").astype(jnp.int32).reshape(1)
    params = pltpu.CompilerParams(vmem_limit_bytes=VMEM_BYTES)
    smem = pl.BlockSpec(memory_space=pltpu.SMEM)
    vmem = pl.BlockSpec(memory_space=pltpu.VMEM)

    def across(x, bit):
        return lax.ppermute(x, "cls", [(c, c ^ bit) for c in range(groups)])

    packed = pl.pallas_call(
        pack_kernel,
        out_shape=jax.ShapeDtypeStruct((dom, n, cols + ROT * k), bf16),
        in_specs=[vmem] * 3,
        out_specs=vmem,
        compiler_params=params,
        name="pack",
    )(particles, pose_weights, class_mask)
    got = lax.all_to_all(packed, "dom", split_axis=0, concat_axis=0, tiled=True)

    blocks = {0: references}
    bit = groups // 2
    while bit:
        blocks.update({s | bit: across(b, bit) for s, b in list(blocks.items())})
        bit //= 2

    keep, send = pl.pallas_call(
        sums_kernel,
        out_shape=[jax.ShapeDtypeStruct((groups // 2, per, cols), f32)] * 2,
        in_specs=[smem, vmem],
        out_specs=[vmem] * 2,
        scratch_shapes=[pltpu.VMEM((groups, per, cols), f32)],
        compiler_params=params,
        name="sums",
    )(me, got)
    bit = 1
    while True:
        keep = keep + across(send, bit)
        bit *= 2
        if bit == groups:
            break
        pairs = keep.reshape(keep.shape[0] // 2, 2, per, cols)
        keep, send = pairs[:, 0], pairs[:, 1]
    particle_total = n * dom * groups
    class_sums = keep[0] / math.sqrt(particle_total * ROT)

    scored = pl.pallas_call(
        scores_kernel,
        out_shape=jax.ShapeDtypeStruct((n, k), f32),
        in_specs=[smem] + [vmem] * (3 + groups),
        out_specs=vmem,
        compiler_params=params,
        name="scores",
    )(me, particles, pose_weights, class_mask, *[blocks[s] for s in range(groups)])
    return (scored, class_sums)


def solution(mesh):
    return jax.shard_map(
        on_device,
        mesh=mesh,
        in_specs=(
            P(("dom", "cls"), None),
            P("cls", None),
            P(("dom", "cls"), None, None),
            P(("dom", "cls"), None),
        ),
        out_specs=(P(("dom", "cls"), None), P("cls", "dom")),
        check_vma=False,
    )
```

time: 306 us -> 34.8 us (0.11); the launches traced: 301 us -> 34.5 us
  local copies, waits for them, and re-layouts: 125 us -> 2.55 us
  waiting for transfers between devices: 133 us -> 12.4 us
  other arithmetic: 17.7 us -> 0.72 us
  between operations: 14.2 us -> 0.7 us
  matrix products: 11.4 us -> 0 us
  starting transfers between devices: 0.12 us -> 11.2 us
  Pallas kernels: 0 us -> 6.87 us
    reduce_scatter x2 -> x0, waiting for transfers between devices: 108 us -> none  [the longest x1 61.4 us: on_device(): lax.psum_scatter(local_sums, 'dom', scatter_dimension=1, tiled=True)]
    another operation x25 -> x0, local copies, waits for them, and re-layouts: 67.3 us -> none  [on_device(): jnp.stack([turned(particles, -r * angle_step) for r in range(ROT)], axis=0)]
    slice x35 -> x0, local copies, waits for them, and re-layouts: 33.7 us -> none  [turned(): return jnp.roll(polar, shift_by, axis=-1).reshape(shape_in)]
    all_gather x1 -> x0, waiting for transfers between devices: 24.2 us -> none  [on_device(): ref_piece = lax.all_gather(references, 'cls', axis=0, tiled=True)]
    unnamed x52 -> x14, local copies, waits for them, and re-layouts: 23.6 us -> 2.54 us
    concatenate x23 -> x0, other arithmetic: 15.5 us -> none  [turned(): return jnp.roll(polar, shift_by, axis=-1).reshape(shape_in)]
    all_to_all x0 -> x1, waiting for transfers between devices: none -> 11.5 us  [on_device(): got = lax.all_to_all(packed, 'dom', split_axis=0, concat_axis=0, tiled=True)]
    dot_general x2 -> x0, matrix products: 11.4 us -> none  [the longest x1 6.15 us: on_device(): jnp.einsum('nrk,rnl->kl', weight_cols, rotated, preferred_element_type=jn...]
  transfers between devices with their start and end apart: 3 -> 6, of which waited for: 3 -> 2; matrix products, arithmetic and copies ran while one was open for 2% -> 0% of each run, Pallas kernels for 0% -> 17%
where the time goes in v1:
time: 34.8 us; the launch traced here: 34.5 us
  waiting for transfers between devices  12.4 us (36%)
  starting transfers between devices  11.2 us (32%)
  Pallas kernels  6.87 us (20%)
  local copies, waits for them, and re-layouts  2.55 us (7%)
  other arithmetic  0.72 us (2%)
  between operations  0.7 us (2%)
    all_to_all x1, waiting for transfers between devices, on_device(): got = lax.all_to_all(packed, 'dom', split_axis=0, concat_axis=0, tiled=True)  11.5 us
    all_to_all x1, starting transfers between devices, on_device(): got = lax.all_to_all(packed, 'dom', split_axis=0, concat_axis=0, tiled=True)  7.38 us
    pallas_call x1, Pallas kernels, on_device(): pl.pallas_call(scores_kernel, out_shape=jax.ShapeDtypeStruct((n, k), f32)...  4.23 us
    ppermute x5, starting transfers between devices, across(): return lax.ppermute(x, 'cls', [(c, c ^ bit) for c in range(groups)])  3.82 us
    unnamed x14, local copies, waits for them, and re-layouts  2.54 us
    pallas_call x1, Pallas kernels, on_device(): pl.pallas_call(sums_kernel, out_shape=[jax.ShapeDtypeStruct((groups // 2,...  1.77 us
    ppermute x5, waiting for transfers between devices, across(): return lax.ppermute(x, 'cls', [(c, c ^ bit) for c in range(groups)])  0.95 us
    pallas_call x1, Pallas kernels, on_device(): pl.pallas_call(pack_kernel, out_shape=jax.ShapeDtypeStruct((dom, n, cols...  0.87 us
  transfers between devices with their start and end apart: 6, of which 2 were waited for; matrix products, arithmetic and copies ran while one was open for 0% of the time, Pallas kernels for 17%

profile of v1, /device:TPU:0, one launch (start us, length us, event | category | flops | bytes accessed | tf_op | source)
XLA Modules:
  0.0 34.5 jit_solution(18095741980127811105)
XLA Ops:
  0.6 0.0 copy-start
  0.6 0.9 %copy-done = bf16[8,16384]{1,0:T(8,128)(2,1)S(1)} copy-done((bf16[8,16384]{1,0:T(8,128)(2,1)S(1)}, bf16[8,16384]{1,0:T(8,128)(2,1)}, u32[]{:S(2)}) %copy-start) | copy-done | bytes 262168
  1.6 0.0 copy-start.3
  1.6 0.9 %copy-done.3 = s32[8,24,64]{2,1,0:T(8,128)S(1)} copy-done((s32[8,24,64]{2,1,0:T(8,128)S(1)}, s32[8,24,64]{2,1,0:T(8,128)}, u32[]{:S(2)}) %copy-start.3) | copy-done | bytes 49176
  2.5 0.0 copy-start.5
  2.5 0.7 %copy-done.5 = s32[8,64]{1,0:T(8,128)S(1)} copy-done((s32[8,64]{1,0:T(8,128)S(1)}, s32[8,64]{1,0:T(8,128)}, u32[]{:S(2)}) %copy-start.5) | copy-done | bytes 2072
  3.2 0.9 %pack.1 = bf16[8,8,3584]{2,1,0:T(8,128)(2,1)} custom-call(bf16[8,16384]{1,0:T(8,128)(2,1)S(1)} %copy-done, s32[8,24,64]{2,1,0:T(8,128)S(1)} %copy-done.3, s32[8,64]{1,0:T(8,128)S(1)} %copy-done.5), custom_call_target="tpu_custom_call" | custom-call | tf_op jit(solution)/shard_map/pack/pallas_call | solution.py:138
  4.0 0.0 copy-start.2
  4.0 7.4 %all-to-all-start = ((bf16[8,8,3584]{2,1,0:T(8,128)(2,1)}), bf16[8,8,3584]{2,1,0:T(8,128)(2,1)S(1)}, u32[]{:S(2)}, u32[]{:S(2)}) async-start(bf16[8,8,3584]{2,1,0:T(8,128)(2,1)} %pack.1), calls=%async_computation | async-start | bytes 917504 | tf_op jit(solution)/shard_map/all_to_all | solution.py:146
  11.4 0.0 copy-done.2
  11.4 1.6 %collective-permute-start.1 = (bf16[16,16384]{1,0:T(8,128)(2,1)S(1)}, bf16[16,16384]{1,0:T(8,128)(2,1)S(1)}, u32[]{:S(2)}, u32[]{:S(2)}) collective-permute-start(bf16[16,16384]{1,0:T(8,128)(2,1)S(1)} %copy-done.2), channel_id=1, source_target_pairs={{0,2},{1,3},{2,0},{3,1},{4,6},{5,7},{6,4},{7,5},{8,10},{9,11},{10,... | collective-permute-start | bytes 1572872 | tf_op jit(solution)/shard_map/ppermute | solution.py:136
  13.0 11.5 %all-to-all-done.got_ref = bf16[8,8,3584]{2,1,0:T(8,128)(2,1)S(1)} async-done(((bf16[8,8,3584]{2,1,0:T(8,128)(2,1)}), bf16[8,8,3584]{2,1,0:T(8,128)(2,1)S(1)}, u32[]{:S(2)}, u32[]{:S(2)}) %all-to-all-start) | async-done | bytes 458784 | tf_op jit(solution)/shard_map/all_to_all | solution.py:146
  24.5 1.8 %sums.1 = (f32[2,16,2048]{2,1,0:T(8,128)S(1)}, f32[2,16,2048]{2,1,0:T(8,128)S(1)}) custom-call(s32[1]{0:T(128)} %bitcast.me_ref, bf16[8,8,3584]{2,1,0:T(8,128)(2,1)S(1)} %all-to-all-done.got_ref), custom_call_target="tpu_custom_call" | custom-call | tf_op jit(solution)/shard_map/sums/pallas_call | solution.py:154
  26.3 0.1 collective-permute-start.3
  26.4 0.5 %collective-permute-start = (bf16[16,16384]{1,0:T(8,128)(2,1)S(1)}, bf16[16,16384]{1,0:T(8,128)(2,1)S(1)}, u32[]{:S(2)}, u32[]{:S(2)}) collective-permute-start(bf16[16,16384]{1,0:T(8,128)(2,1)S(1)} %copy-done.2), channel_id=1, source_target_pairs={{0,1},{1,0},{2,3},{3,2},{4,5},{5,4},{6,7},{7,6},{8,9},{9,8},{10,11... | collective-permute-start | bytes 1572872 | tf_op jit(solution)/shard_map/ppermute | solution.py:136
  26.9 0.0 collective-permute-done.1.refs_2_
  26.9 0.1 collective-permute-start.2
  26.9 0.9 %collective-permute-done.3 = f32[2,16,2048]{2,1,0:T(8,128)S(1)} collective-permute-done((f32[2,16,2048]{2,1,0:T(8,128)S(1)}, f32[2,16,2048]{2,1,0:T(8,128)S(1)}, u32[]{:S(2)}, u32[]{:S(2)}) %collective-permute-start.3) | collective-permute-done | bytes 262176 | tf_op jit(solution)/shard_map/ppermute | solution.py:136
  27.9 0.0 copy-start.4
  27.9 0.0 copy-start.6
  27.9 0.0 copy-start.1
  28.0 1.6 %collective-permute-start.4 = (f32[1,16,2048]{2,1,0:T(8,128)S(1)}, f32[1,16,2048]{2,1,0:T(8,128)S(1)}, u32[]{:S(2)}, u32[]{:S(2)}) collective-permute-start(f32[1,16,2048]{2,1,0:T(8,128)S(1)} %slice_bitcast_fusion), channel_id=1, source_target_pairs={{0,2},{1,3},{2,0},{3,1},{4,6},{5,7},{6,4},{7,5},{8,10},{9,11},{10,... | collective-permute-start | bytes 393224 | tf_op jit(solution)/shard_map/ppermute | solution.py:136
  29.5 0.0 collective-permute-done.refs_1_
  29.6 0.0 collective-permute-done.2.refs_3_
  29.6 0.0 copy-done.4
  29.6 0.0 copy-done.6
  29.6 0.0 copy-done.1
  29.6 4.2 %scores.1 = f32[8,64]{1,0:T(8,128)} custom-call(s32[1]{0:T(128)} %bitcast.me_ref, bf16[8,16384]{1,0:T(8,128)(2,1)S(1)} %copy-done.1, s32[8,24,64]{2,1,0:T(8,128)S(1)} %copy-done.4, s32[8,64]{1,0:T(8,128)S(1)} %copy-done.6, bf16[16,16384]{1,0:T(8,128)(2,1)S(1)} %copy-done.2, bf16[16,16384]{1,0:T(8,128)(2,1)S(1)} %collective-permute-done.refs_1_, ...), custom_call_target="tpu_custom_call" | custom-call | tf_op jit(solution)/shard_map/scores/pallas_call | solution.py:174
  33.8 0.0 collective-permute-done.4
  33.8 0.7 %fusion.2 = f32[16,2048]{1,0:T(8,128)} fusion(f32[1,16,2048]{2,1,0:T(8,128)S(1)} %collective-permute-done.4, f32[1,2,16,2048]{3,2,1,0:T(8,128)S(1)} %add_bitcast_fusion), kind=kLoop, calls=%fused_computation.5 | loop fusion | flops 65536 | bytes 393216 | tf_op jit(solution)/shard_map/div | solution.py:172
  (2 shorter events, 0.1 us)
Async XLA Ops:
  0.6 1.0 %copy-start = (bf16[8,16384]{1,0:T(8,128)(2,1)S(1)}, bf16[8,16384]{1,0:T(8,128)(2,1)}, u32[]{:S(2)}) copy-start(bf16[8,16384]{1,0:T(8,128)(2,1)} %part_ref.3) | copy-start | bytes 786436
  1.6 0.9 %copy-start.3 = (s32[8,24,64]{2,1,0:T(8,128)S(1)}, s32[8,24,64]{2,1,0:T(8,128)}, u32[]{:S(2)}) copy-start(s32[8,24,64]{2,1,0:T(8,128)} %pose_ref.3) | copy-start | bytes 147460
  2.5 0.7 %copy-start.5 = (s32[8,64]{1,0:T(8,128)S(1)}, s32[8,64]{1,0:T(8,128)}, u32[]{:S(2)}) copy-start(s32[8,64]{1,0:T(8,128)} %mask_ref.3) | copy-start | bytes 6148
  4.0 7.4 %copy-start.2 = (bf16[16,16384]{1,0:T(8,128)(2,1)S(1)}, bf16[16,16384]{1,0:T(8,128)(2,1)}, u32[]{:S(2)}) copy-start(bf16[16,16384]{1,0:T(8,128)(2,1)} %refs_0_.1) | copy-start | bytes 1572868
  4.0 20.5 %all-to-all-start = ((bf16[8,8,3584]{2,1,0:T(8,128)(2,1)}), bf16[8,8,3584]{2,1,0:T(8,128)(2,1)S(1)}, u32[]{:S(2)}, u32[]{:S(2)}) async-start(bf16[8,8,3584]{2,1,0:T(8,128)(2,1)} %pack.1), calls=%async_computation | async-start | bytes 917504 | tf_op jit(solution)/shard_map/all_to_all | solution.py:146
  11.4 15.4 %collective-permute-start.1 = (bf16[16,16384]{1,0:T(8,128)(2,1)S(1)}, bf16[16,16384]{1,0:T(8,128)(2,1)S(1)}, u32[]{:S(2)}, u32[]{:S(2)}) collective-permute-start(bf16[16,16384]{1,0:T(8,128)(2,1)S(1)} %copy-done.2), channel_id=1, source_target_pairs={{0,2},{1,3},{2,0},{3,1},{4,6},{5,7},{6,4},{7,5},{8,10},{9,11},{10,... | collective-permute-start | bytes 1572872 | tf_op jit(solution)/shard_map/ppermute | solution.py:136
  26.3 1.6 %collective-permute-start.3 = (f32[2,16,2048]{2,1,0:T(8,128)S(1)}, f32[2,16,2048]{2,1,0:T(8,128)S(1)}, u32[]{:S(2)}, u32[]{:S(2)}) collective-permute-start(f32[2,16,2048]{2,1,0:T(8,128)S(1)} %get-tuple-element.5), channel_id=1, source_target_pairs={{0,1},{1,0},{2,3},{3,2},{4,5},{5,4},{6,7},{7,6},{8,9},{9,8},{10,11... | collective-permute-start | bytes 786440 | tf_op jit(solution)/shard_map/ppermute | solution.py:136
  26.4 3.2 %collective-permute-start = (bf16[16,16384]{1,0:T(8,128)(2,1)S(1)}, bf16[16,16384]{1,0:T(8,128)(2,1)S(1)}, u32[]{:S(2)}, u32[]{:S(2)}) collective-permute-start(bf16[16,16384]{1,0:T(8,128)(2,1)S(1)} %copy-done.2), channel_id=1, source_target_pairs={{0,1},{1,0},{2,3},{3,2},{4,5},{5,4},{6,7},{7,6},{8,9},{9,8},{10,11... | collective-permute-start | bytes 1572872 | tf_op jit(solution)/shard_map/ppermute | solution.py:136
  26.9 2.7 %collective-permute-start.2 = (bf16[16,16384]{1,0:T(8,128)(2,1)S(1)}, bf16[16,16384]{1,0:T(8,128)(2,1)S(1)}, u32[]{:S(2)}, u32[]{:S(2)}) collective-permute-start(bf16[16,16384]{1,0:T(8,128)(2,1)S(1)} %collective-permute-done.1.refs_2_), channel_id=1, source_target_pairs={{0,1},{1,0},{2,3},{3,2},{4,5},{5,4},{6,7},{7,6},{8,9},{9,8},{10,11... | collective-permute-start | bytes 1572872 | tf_op jit(solution)/shard_map/ppermute | solution.py:136
  27.9 1.7 %copy-start.4 = (s32[8,24,64]{2,1,0:T(8,128)S(1)}, s32[8,24,64]{2,1,0:T(8,128)}, u32[]{:S(2)}) copy-start(s32[8,24,64]{2,1,0:T(8,128)} %pose_ref.3) | copy-start | bytes 147460
  27.9 1.7 %copy-start.6 = (s32[8,64]{1,0:T(8,128)S(1)}, s32[8,64]{1,0:T(8,128)}, u32[]{:S(2)}) copy-start(s32[8,64]{1,0:T(8,128)} %mask_ref.3) | copy-start | bytes 6148
  27.9 1.6 %copy-start.1 = (bf16[8,16384]{1,0:T(8,128)(2,1)S(1)}, bf16[8,16384]{1,0:T(8,128)(2,1)}, u32[]{:S(2)}) copy-start(bf16[8,16384]{1,0:T(8,128)(2,1)} %part_ref.3) | copy-start | bytes 786436
  28.0 5.8 %collective-permute-start.4 = (f32[1,16,2048]{2,1,0:T(8,128)S(1)}, f32[1,16,2048]{2,1,0:T(8,128)S(1)}, u32[]{:S(2)}, u32[]{:S(2)}) collective-permute-start(f32[1,16,2048]{2,1,0:T(8,128)S(1)} %slice_bitcast_fusion), channel_id=1, source_target_pairs={{0,2},{1,3},{2,0},{3,1},{4,6},{5,7},{6,4},{7,5},{8,10},{9,11},{10,... | collective-permute-start | bytes 393224 | tf_op jit(solution)/shard_map/ppermute | solution.py:136

commit v2 on v1

v2 whole, which is shorter than its diff:
```python
import math

import jax
import jax.numpy as jnp
from jax import lax
from jax.experimental import pallas as pl
from jax.experimental.pallas import tpu as pltpu
from jax.sharding import PartitionSpec as P

CYCLES = 64
ANG = 256
ROT = 24
STEP = ANG // ROT
FINE = 4
COARSE = ROT // FINE
PAIR = 2
CHUNK = 4
LANES = 128
VMEM_BYTES = 48 * 1024 * 1024
VMEM_MOST = 66584576
f32 = jnp.float32
bf16 = jnp.bfloat16


def turn(x, shift):
    shift %= ANG
    if shift == 0:
        return x
    halves, rest = shift // LANES, shift % LANES
    lane = lax.broadcasted_iota(jnp.int32, (x.shape[0], LANES), 1)
    pieces = []
    for c in range(x.shape[1] // ANG):
        lo = x[:, c * ANG : c * ANG + LANES]
        hi = x[:, c * ANG + LANES : (c + 1) * ANG]
        if halves:
            lo, hi = hi, lo
        if rest:
            lo, hi = pltpu.roll(lo, rest, 1), pltpu.roll(hi, rest, 1)
            lo, hi = jnp.where(lane < rest, hi, lo), jnp.where(lane < rest, lo, hi)
        pieces += [lo, hi]
    return jnp.concatenate(pieces, axis=1)


def swap_blocks(x, me, block, blocks):
    lane = lax.broadcasted_iota(jnp.int32, x.shape, 1)
    width = x.shape[1]
    bit = 1
    while bit < blocks:
        g = block * bit
        upper = (lane // g) % 2 == 1
        swapped = jnp.where(upper, pltpu.roll(x, g, 1), pltpu.roll(x, width - g, 1))
        x = jnp.where((me // bit) % 2 == 1, swapped, x)
        bit *= 2
    return x


def pack_kernel(part_hbm, pose_hbm, mask_hbm, out_ref, weights_ref, pose_ref, mask_ref, sems):
    dom, _, _ = out_ref.shape
    cols = part_hbm.shape[1] // dom
    me, groups = lax.axis_index("cls"), lax.axis_size("cls")
    k = pose_ref.shape[2]
    half = k // 2
    wide = FINE * k
    small = [
        pltpu.make_async_copy(pose_hbm, pose_ref, sems.at[dom]),
        pltpu.make_async_copy(mask_hbm, mask_ref, sems.at[dom + 1]),
    ]
    large = [
        pltpu.make_async_copy(
            part_hbm.at[:, pl.ds(d * cols, cols)], out_ref.at[d, :, pl.ds(0, cols)], sems.at[d]
        )
        for d in range(dom)
    ]
    for copy in small + large:
        copy.start()
    for copy in small:
        copy.wait()
    mask = mask_ref[...]
    for i in range(COARSE):
        fine = [pose_ref[:, FINE * i + j, :] * mask for j in range(FINE)]
        w = swap_blocks(jnp.concatenate(fine, axis=1).astype(f32), me, k // groups, groups)
        pieces = [w[:, j * k + h * half : j * k + (h + 1) * half] for h in range(2) for j in range(FINE)]
        w = jnp.concatenate(pieces, axis=1).astype(bf16)
        weights_ref[:, i * wide : (i + 1) * wide] = w
        for d in range(dom):
            out_ref[d, :, cols + i * wide : cols + (i + 1) * wide] = w
    for copy in large:
        copy.wait()


def half_sums(got_ref, stack, half):
    dom, n, width = got_ref.shape
    cols = stack.shape[1]
    wide = (width - cols) // COARSE // 2
    k = wide // FINE
    rows = []
    for i in range(COARSE):
        first = cols + (2 * i + half) * wide
        rows.append(got_ref[:, :, first : first + wide].astype(f32).reshape(dom * n, wide))
    w = jnp.concatenate(rows, axis=0).astype(bf16)
    t = lax.dot_general(w, stack, (((0,), (0,)), ((), ())), preferred_element_type=f32)
    total = t[:k]
    for j in range(1, FINE):
        total = total + turn(t[j * k : (j + 1) * k], -STEP * j)
    return total


def put_pairs(total, keep_ref, send_ref):
    half, per, _ = keep_ref.shape
    for m in range(half):
        keep_ref[m] = total[2 * m * per : (2 * m + 1) * per]
        if total.shape[0] > per:
            send_ref[m] = total[(2 * m + 1) * per : (2 * m + 2) * per]


def far_sums_kernel(got_ref, stack_ref, keep_ref, send_ref):
    dom, n, _ = got_ref.shape
    cols = stack_ref.shape[1]
    part = got_ref[:, :, :cols].astype(f32).reshape(dom * n, cols)
    stack = jnp.concatenate([turn(part, -STEP * FINE * i).astype(bf16) for i in range(COARSE)], axis=0)
    stack_ref[...] = stack
    put_pairs(half_sums(got_ref, stack, 1), keep_ref, send_ref)


def near_sums_kernel(got_ref, stack_ref, keep_ref, send_ref):
    put_pairs(half_sums(got_ref, stack_ref[...], 0), keep_ref, send_ref)


def half_scores(part_ref, weights_ref, blocks, half):
    n, length = part_ref.shape
    k = blocks[0].shape[0] * len(blocks)
    chunk = CHUNK * ANG
    corr = None
    for c in range(length // chunk):
        at = slice(c * chunk, (c + 1) * chunk)
        part = part_ref[:, at].astype(f32)
        left = jnp.concatenate([turn(part, -STEP * PAIR * m) for m in range(ROT // PAIR)], axis=0).astype(bf16)
        cls = jnp.concatenate([b[:, at].astype(f32) for b in blocks], axis=0)
        right = jnp.concatenate([turn(cls, STEP * j).astype(bf16) for j in range(PAIR)], axis=0)
        more = lax.dot_general(left, right, (((1,), (1,)), ((), ())), preferred_element_type=f32)
        corr = more if corr is None else corr + more
    wide = PAIR * k
    total = None
    for m in range(ROT // PAIR):
        i, b = m // 2, m % 2
        first = ((2 * i + half) * 2 + b) * wide
        w = weights_ref[:, first : first + wide].astype(f32)
        more = w * corr[m * n : (m + 1) * n]
        total = more if total is None else total + more
    out = total[:, :k]
    for j in range(1, PAIR):
        out = out + total[:, j * k : (j + 1) * k]
    return out


def near_scores_kernel(part_ref, weights_ref, *refs):
    *blocks, out_ref = refs
    out_ref[...] = half_scores(part_ref, weights_ref, blocks, 0)


def far_scores_kernel(near_ref, part_ref, weights_ref, *refs):
    *blocks, out_ref = refs
    groups = lax.axis_size("cls")
    far = half_scores(part_ref, weights_ref, blocks, 1)
    out = jnp.concatenate([near_ref[...], far], axis=1)
    out_ref[...] = swap_blocks(out, lax.axis_index("cls"), out.shape[1] // groups, groups) / ROT


def on_device(particles, references, pose_weights, class_mask):
    n, length = particles.shape
    per = references.shape[0]
    k = class_mask.shape[1]
    dom, groups = lax.axis_size("dom"), lax.axis_size("cls")
    cols = length // dom
    last = groups // 2
    hbm = pl.BlockSpec(memory_space=pl.ANY)
    vmem = pl.BlockSpec(memory_space=pltpu.VMEM)

    def call(kernel, name, outs, ins, scratch=(), limit=VMEM_BYTES):
        return pl.pallas_call(
            kernel,
            out_shape=[jax.ShapeDtypeStruct(*o) for o in outs],
            in_specs=ins,
            out_specs=[vmem] * len(outs),
            scratch_shapes=list(scratch),
            compiler_params=pltpu.CompilerParams(vmem_limit_bytes=limit),
            name=name,
        )

    def after(x, other):
        return lax.optimization_barrier((x, other))[0]

    def across(x, bit):
        return lax.ppermute(x, "cls", [(c, c ^ bit) for c in range(groups)])

    def reduced(keep, send):
        bit = 1
        while bit < last:
            keep = keep + across(send, bit)
            bit *= 2
            if bit < last:
                pairs = keep.reshape(keep.shape[0] // 2, 2, per, cols)
                keep, send = pairs[:, 0], pairs[:, 1]
        return keep[0]

    packed, weights = call(
        pack_kernel,
        "pack",
        [((dom, n, cols + ROT * k), bf16), ((n, ROT * k), bf16)],
        [hbm] * 3,
        [
            pltpu.VMEM(pose_weights.shape, jnp.int32),
            pltpu.VMEM(class_mask.shape, jnp.int32),
            pltpu.SemaphoreType.DMA((dom + 2,)),
        ],
        VMEM_MOST,
    )(particles, pose_weights, class_mask)
    got = lax.all_to_all(packed, "dom", split_axis=0, concat_axis=0, tiled=True)
    blocks = {0: references}
    bit = last
    while bit:
        for s, b in list(blocks.items()):
            blocks[s | bit] = across(after(b, packed) if s == 0 else b, bit)
        bit //= 2
    near, far = [blocks[s] for s in range(last)], [blocks[s] for s in range(last, groups)]
    (near_scores,) = call(
        near_scores_kernel, "near_scores", [((n, k // 2), f32)], [vmem] * (2 + last)
    )(particles, weights, *near)
    got = after(got, near_scores)

    send_shape = (max(last // 2, 1), per, cols)
    stack, keep, send = call(
        far_sums_kernel,
        "far_sums",
        [((n * dom * COARSE, cols), bf16), (send_shape, f32), (send_shape, f32)],
        [vmem],
    )(got)
    leaving = reduced(keep, send)
    arriving = across(leaving, last)
    stack = after(stack, leaving)

    keep, send = call(near_sums_kernel, "near_sums", [(send_shape, f32)] * 2, [vmem] * 2)(got, stack)
    near_sums = reduced(keep, send)

    (scored,) = call(far_scores_kernel, "far_scores", [((n, k), f32)], [vmem] * (3 + last))(
        near_scores, particles, weights, *far
    )
    arriving = after(arriving, scored)
    class_sums = (near_sums + arriving) / math.sqrt(n * dom * groups * ROT)
    return (scored, class_sums)


def solution(mesh):
    return jax.shard_map(
        on_device,
        mesh=mesh,
        in_specs=(
            P(("dom", "cls"), None),
            P("cls", None),
            P(("dom", "cls"), None, None),
            P(("dom", "cls"), None),
        ),
        out_specs=(P(("dom", "cls"), None), P("cls", "dom")),
        check_vma=False,
    )
```

time: 34.8 us -> 32.1 us (0.922)
  waiting for transfers between devices: 12.4 us -> 8.96 us
  Pallas kernels: 6.87 us -> 8.03 us
  starting transfers between devices: 11.2 us -> 10.6 us
    all_to_all x1, waiting for transfers between devices: 11.5 us -> 6.48 us  [on_device(): got = lax.all_to_all(packed, 'dom', split_axis=0, concat_axis=0, tiled=True)]
    ppermute x5 -> x6, waiting for transfers between devices: 0.95 us -> 2.48 us  [across(): return lax.ppermute(x, 'cls', [(c, c ^ bit) for c in range(groups)])]
    pallas_call x3 -> x5, Pallas kernels: 6.87 us -> 8.03 us  [the longest x1 2.7 us: on_device(): call(far_scores_kernel, 'far_scores', [((n, k), f32)], [vmem] * (3 + last))]
    ppermute x5 -> x6, starting transfers between devices: 3.82 us -> 3.36 us  [across(): return lax.ppermute(x, 'cls', [(c, c ^ bit) for c in range(groups)])]
    unnamed x14 -> x10, local copies, waits for them, and re-layouts: 2.54 us -> 2.74 us
  transfers between devices with their start and end apart: 6 -> 7, of which waited for: 2 -> 5; matrix products, arithmetic and copies ran while one was open for 0% -> 0% of each run, Pallas kernels for 17% -> 19%
where the time goes in v2:
time: 32.1 us; the launch traced here: 31.8 us
  starting transfers between devices  10.6 us (33%)
  waiting for transfers between devices  8.96 us (28%)
  Pallas kernels  8.03 us (25%)
  local copies, waits for them, and re-layouts  2.74 us (9%)
  between operations  0.71 us (2%)
  other arithmetic  0.69 us (2%)
    all_to_all x1, starting transfers between devices, on_device(): got = lax.all_to_all(packed, 'dom', split_axis=0, concat_axis=0, tiled=True)  7.26 us
    all_to_all x1, waiting for transfers between devices, on_device(): got = lax.all_to_all(packed, 'dom', split_axis=0, concat_axis=0, tiled=True)  6.48 us
    ppermute x6, starting transfers between devices, across(): return lax.ppermute(x, 'cls', [(c, c ^ bit) for c in range(groups)])  3.36 us
    unnamed x10, local copies, waits for them, and re-layouts  2.74 us
    pallas_call x1, Pallas kernels, on_device(): call(far_scores_kernel, 'far_scores', [((n, k), f32)], [vmem] * (3 + last))  2.7 us
    ppermute x6, waiting for transfers between devices, across(): return lax.ppermute(x, 'cls', [(c, c ^ bit) for c in range(groups)])  2.48 us
    pallas_call x1, Pallas kernels, on_device(): call(pack_kernel, 'pack', [((dom, n, cols + ROT * k), bf16), ((n, ROT * k...  2.09 us
    pallas_call x1, Pallas kernels, on_device(): call(near_scores_kernel, 'near_scores', [((n, k // 2), f32)], [vmem] * (2...  1.75 us
  transfers between devices with their start and end apart: 7, of which 5 were waited for; matrix products, arithmetic and copies ran while one was open for 0% of the time, Pallas kernels for 19%

profile of v2, /device:TPU:0, one launch (start us, length us, event | category | flops | bytes accessed | tf_op | source)
XLA Modules:
  0.0 31.8 jit_solution(13383603593015492679)
XLA Ops:
  0.6 2.1 %pack.1 = (bf16[8,8,3584]{2,1,0:T(8,128)(2,1)}, bf16[8,1536]{1,0:T(8,128)(2,1)}) custom-call(bf16[8,16384]{1,0:T(8,128)(2,1)} %part_ref.3, s32[8,24,64]{2,1,0:T(8,128)} %pose_hbm.1, s32[8,64]{1,0:T(8,128)} %mask_hbm.1), custom_call_target="tpu_custom_call" | custom-call | tf_op jit(solution)/shard_map/pack/pallas_call | solution.py:206
  2.7 7.3 %all-to-all-start = ((bf16[8,8,3584]{2,1,0:T(8,128)(2,1)}), bf16[8,8,3584]{2,1,0:T(8,128)(2,1)S(1)}, u32[]{:S(2)}, u32[]{:S(2)}) async-start(bf16[8,8,3584]{2,1,0:T(8,128)(2,1)} %get-tuple-element.14), calls=%async_computation | async-start | bytes 917504 | tf_op jit(solution)/shard_map/all_to_all | solution.py:218
  10.0 0.0 collective-permute-start
  10.0 1.6 %collective-permute-start.1 = (bf16[16,16384]{1,0:T(8,128)(2,1)}, bf16[16,16384]{1,0:T(8,128)(2,1)S(1)}, u32[]{:S(2)}, u32[]{:S(2)}) collective-permute-start(bf16[16,16384]{1,0:T(8,128)(2,1)} %refs_0_.1), channel_id=1, source_target_pairs={{0,2},{1,3},{2,0},{3,1},{4,6},{5,7},{6,4},{7,5},{8,10},{9,11},{10,... | collective-permute-start | bytes 1572872 | tf_op jit(solution)/shard_map/ppermute | solution.py:194
  11.6 0.5 %collective-permute-done.refs_1_ = bf16[16,16384]{1,0:T(8,128)(2,1)S(1)} collective-permute-done((bf16[16,16384]{1,0:T(8,128)(2,1)}, bf16[16,16384]{1,0:T(8,128)(2,1)S(1)}, u32[]{:S(2)}, u32[]{:S(2)}) %collective-permute-start) | collective-permute-done | bytes 524320 | tf_op jit(solution)/shard_map/ppermute | solution.py:194
  12.1 0.0 copy-start
  12.1 0.9 %copy-done = bf16[8,16384]{1,0:T(8,128)(2,1)S(1)} copy-done((bf16[8,16384]{1,0:T(8,128)(2,1)S(1)}, bf16[8,16384]{1,0:T(8,128)(2,1)}, u32[]{:S(2)}) %copy-start) | copy-done | bytes 262168
  13.1 0.0 copy-start.2
  13.1 1.0 %copy-done.2 = bf16[16,16384]{1,0:T(8,128)(2,1)S(1)} copy-done((bf16[16,16384]{1,0:T(8,128)(2,1)S(1)}, bf16[16,16384]{1,0:T(8,128)(2,1)}, u32[]{:S(2)}) %copy-start.2) | copy-done | bytes 524312
  14.1 0.0 copy-start.3
  14.1 0.7 %copy-done.3 = bf16[8,1536]{1,0:T(8,128)(2,1)S(1)} copy-done((bf16[8,1536]{1,0:T(8,128)(2,1)S(1)}, bf16[8,1536]{1,0:T(8,128)(2,1)}, u32[]{:S(2)}) %copy-start.3) | copy-done | bytes 24600
  14.8 1.7 %near_scores.1.near_ref = f32[8,32]{1,0:T(8,128)S(1)} custom-call(bf16[8,16384]{1,0:T(8,128)(2,1)S(1)} %copy-done, bf16[8,1536]{1,0:T(8,128)(2,1)S(1)} %copy-done.3, bf16[16,16384]{1,0:T(8,128)(2,1)S(1)} %copy-done.2, bf16[16,16384]{1,0:T(8,128)(2,1)S(1)} %collective-permute-done.refs_1_), custom_call_target="tpu_custom_call" | custom-call | tf_op jit(solution)/shard_map/near_scores/pallas_call | solution.py:226
  16.6 0.0 copy-start.1
  16.6 0.0 copy-start.4
  16.6 6.5 %all-to-all-done.got_ref = bf16[8,8,3584]{2,1,0:T(8,128)(2,1)S(1)} async-done(((bf16[8,8,3584]{2,1,0:T(8,128)(2,1)}), bf16[8,8,3584]{2,1,0:T(8,128)(2,1)S(1)}, u32[]{:S(2)}, u32[]{:S(2)}) %all-to-all-start) | async-done | bytes 458784 | tf_op jit(solution)/shard_map/all_to_all | solution.py:218
  23.1 0.9 %far_sums.1 = (bf16[384,2048]{1,0:T(8,128)(2,1)S(1)}, f32[1,16,2048]{2,1,0:T(8,128)S(1)}, f32[1,16,2048]{2,1,0:T(8,128)S(1)}) custom-call(bf16[8,8,3584]{2,1,0:T(8,128)(2,1)S(1)} %all-to-all-done.got_ref), custom_call_target="tpu_custom_call" | custom-call | tf_op jit(solution)/shard_map/far_sums/pallas_call | solution.py:232
  24.0 0.1 collective-permute-start.3
  24.1 0.5 %collective-permute-done.1.refs_0_ = bf16[16,16384]{1,0:T(8,128)(2,1)S(1)} collective-permute-done((bf16[16,16384]{1,0:T(8,128)(2,1)}, bf16[16,16384]{1,0:T(8,128)(2,1)S(1)}, u32[]{:S(2)}, u32[]{:S(2)}) %collective-permute-start.1) | collective-permute-done | bytes 524320 | tf_op jit(solution)/shard_map/ppermute | solution.py:194
  24.6 0.0 collective-permute-start.2
  24.6 0.8 %collective-permute-done.3 = f32[1,16,2048]{2,1,0:T(8,128)S(1)} collective-permute-done((f32[1,16,2048]{2,1,0:T(8,128)S(1)}, f32[1,16,2048]{2,1,0:T(8,128)S(1)}, u32[]{:S(2)}, u32[]{:S(2)}) %collective-permute-start.3) | collective-permute-done | bytes 131104 | tf_op jit(solution)/shard_map/ppermute | solution.py:194
  25.5 1.6 %collective-permute-start.5 = (f32[16,2048]{1,0:T(8,128)S(1)}, f32[16,2048]{1,0:T(8,128)S(1)}, u32[]{:S(2)}, u32[]{:S(2)}) collective-permute-start(f32[16,2048]{1,0:T(8,128)S(1)} %add_bitcast_fusion), channel_id=1, source_target_pairs={{0,2},{1,3},{2,0},{3,1},{4,6},{5,7},{6,4},{7,5},{8,10},{9,11},{10,... | collective-permute-start | bytes 393224 | tf_op jit(solution)/shard_map/ppermute | solution.py:194
  27.0 0.6 %near_sums.1 = (f32[1,16,2048]{2,1,0:T(8,128)S(1)}, f32[1,16,2048]{2,1,0:T(8,128)S(1)}) custom-call(bf16[8,8,3584]{2,1,0:T(8,128)(2,1)S(1)} %all-to-all-done.got_ref, bf16[384,2048]{1,0:T(8,128)(2,1)S(1)} %get-tuple-element.20.stack_ref), custom_call_target="tpu_custom_call" | custom-call | tf_op jit(solution)/shard_map/near_sums/pallas_call | solution.py:242
  27.6 0.1 collective-permute-start.4
  27.7 0.0 collective-permute-done.2.refs_1_
  27.7 0.0 copy-done.1
  27.7 0.0 copy-done.4
  27.7 2.7 %far_scores.1 = f32[8,64]{1,0:T(8,128)} custom-call(f32[8,32]{1,0:T(8,128)S(1)} %near_scores.1.near_ref, bf16[8,16384]{1,0:T(8,128)(2,1)S(1)} %copy-done.1, bf16[8,1536]{1,0:T(8,128)(2,1)S(1)} %copy-done.4, bf16[16,16384]{1,0:T(8,128)(2,1)S(1)} %collective-permute-done.1.refs_0_, bf16[16,16384]{1,0:T(8,128)(2,1)S(1)} %collective-permute-done.2.refs_1_), custom_call_target="tpu_custom_call" | custom-call | tf_op jit(solution)/shard_map/far_scores/pallas_call | solution.py:245
  30.4 0.7 %collective-permute-done.5 = f32[16,2048]{1,0:T(8,128)S(1)} collective-permute-done((f32[16,2048]{1,0:T(8,128)S(1)}, f32[16,2048]{1,0:T(8,128)S(1)}, u32[]{:S(2)}, u32[]{:S(2)}) %collective-permute-start.5) | collective-permute-done | bytes 131104 | tf_op jit(solution)/shard_map/ppermute | solution.py:194
  31.1 0.0 collective-permute-done.4
  31.1 0.7 %fusion = f32[16,2048]{1,0:T(8,128)} fusion(f32[16,2048]{1,0:T(8,128)S(1)} %collective-permute-done.5, f32[1,16,2048]{2,1,0:T(8,128)S(1)} %get-tuple-element.21, f32[1,16,2048]{2,1,0:T(8,128)S(1)} %collective-permute-done.4), kind=kLoop, calls=%fused_computation.1 | loop fusion | flops 98304 | bytes 524288 | tf_op jit(solution)/shard_map/div | solution.py:249
  (1 shorter events, 0.0 us)
Async XLA Ops:
  2.7 20.3 %all-to-all-start = ((bf16[8,8,3584]{2,1,0:T(8,128)(2,1)}), bf16[8,8,3584]{2,1,0:T(8,128)(2,1)S(1)}, u32[]{:S(2)}, u32[]{:S(2)}) async-start(bf16[8,8,3584]{2,1,0:T(8,128)(2,1)} %get-tuple-element.14), calls=%async_computation | async-start | bytes 917504 | tf_op jit(solution)/shard_map/all_to_all | solution.py:218
  10.0 2.1 %collective-permute-start = (bf16[16,16384]{1,0:T(8,128)(2,1)}, bf16[16,16384]{1,0:T(8,128)(2,1)S(1)}, u32[]{:S(2)}, u32[]{:S(2)}) collective-permute-start(bf16[16,16384]{1,0:T(8,128)(2,1)} %refs_0_.1), channel_id=1, source_target_pairs={{0,1},{1,0},{2,3},{3,2},{4,5},{5,4},{6,7},{7,6},{8,9},{9,8},{10,11... | collective-permute-start | bytes 1572872 | tf_op jit(solution)/shard_map/ppermute | solution.py:194
  10.0 14.6 %collective-permute-start.1 = (bf16[16,16384]{1,0:T(8,128)(2,1)}, bf16[16,16384]{1,0:T(8,128)(2,1)S(1)}, u32[]{:S(2)}, u32[]{:S(2)}) collective-permute-start(bf16[16,16384]{1,0:T(8,128)(2,1)} %refs_0_.1), channel_id=1, source_target_pairs={{0,2},{1,3},{2,0},{3,1},{4,6},{5,7},{6,4},{7,5},{8,10},{9,11},{10,... | collective-permute-start | bytes 1572872 | tf_op jit(solution)/shard_map/ppermute | solution.py:194
  12.1 1.0 %copy-start = (bf16[8,16384]{1,0:T(8,128)(2,1)S(1)}, bf16[8,16384]{1,0:T(8,128)(2,1)}, u32[]{:S(2)}) copy-start(bf16[8,16384]{1,0:T(8,128)(2,1)} %part_ref.3) | copy-start | bytes 786436
  13.1 1.0 %copy-start.2 = (bf16[16,16384]{1,0:T(8,128)(2,1)S(1)}, bf16[16,16384]{1,0:T(8,128)(2,1)}, u32[]{:S(2)}) copy-start(bf16[16,16384]{1,0:T(8,128)(2,1)} %refs_0_.1) | copy-start | bytes 1572868
  14.1 0.7 %copy-start.3 = (bf16[8,1536]{1,0:T(8,128)(2,1)S(1)}, bf16[8,1536]{1,0:T(8,128)(2,1)}, u32[]{:S(2)}) copy-start(bf16[8,1536]{1,0:T(8,128)(2,1)} %get-tuple-element.13.weights_ref) | copy-start | bytes 73732
  16.6 11.1 %copy-start.1 = (bf16[8,16384]{1,0:T(8,128)(2,1)S(1)}, bf16[8,16384]{1,0:T(8,128)(2,1)}, u32[]{:S(2)}) copy-start(bf16[8,16384]{1,0:T(8,128)(2,1)} %part_ref.3) | copy-start | bytes 786436
  16.6 11.1 %copy-start.4 = (bf16[8,1536]{1,0:T(8,128)(2,1)S(1)}, bf16[8,1536]{1,0:T(8,128)(2,1)}, u32[]{:S(2)}) copy-start(bf16[8,1536]{1,0:T(8,128)(2,1)} %get-tuple-element.13.weights_ref) | copy-start | bytes 73732
  24.0 1.4 %collective-permute-start.3 = (f32[1,16,2048]{2,1,0:T(8,128)S(1)}, f32[1,16,2048]{2,1,0:T(8,128)S(1)}, u32[]{:S(2)}, u32[]{:S(2)}) collective-permute-start(f32[1,16,2048]{2,1,0:T(8,128)S(1)} %get-tuple-element.19), channel_id=1, source_target_pairs={{0,1},{1,0},{2,3},{3,2},{4,5},{5,4},{6,7},{7,6},{8,9},{9,8},{10,11... | collective-permute-start | bytes 393224 | tf_op jit(solution)/shard_map/ppermute | solution.py:194
  24.6 3.1 %collective-permute-start.2 = (bf16[16,16384]{1,0:T(8,128)(2,1)S(1)}, bf16[16,16384]{1,0:T(8,128)(2,1)S(1)}, u32[]{:S(2)}, u32[]{:S(2)}) collective-permute-start(bf16[16,16384]{1,0:T(8,128)(2,1)S(1)} %collective-permute-done.1.refs_0_), channel_id=1, source_target_pairs={{0,1},{1,0},{2,3},{3,2},{4,5},{5,4},{6,7},{7,6},{8,9},{9,8},{10,11... | collective-permute-start | bytes 1572872 | tf_op jit(solution)/shard_map/ppermute | solution.py:194
  25.5 5.6 %collective-permute-start.5 = (f32[16,2048]{1,0:T(8,128)S(1)}, f32[16,2048]{1,0:T(8,128)S(1)}, u32[]{:S(2)}, u32[]{:S(2)}) collective-permute-start(f32[16,2048]{1,0:T(8,128)S(1)} %add_bitcast_fusion), channel_id=1, source_target_pairs={{0,2},{1,3},{2,0},{3,1},{4,6},{5,7},{6,4},{7,5},{8,10},{9,11},{10,... | collective-permute-start | bytes 393224 | tf_op jit(solution)/shard_map/ppermute | solution.py:194
  27.6 3.5 %collective-permute-start.4 = (f32[1,16,2048]{2,1,0:T(8,128)S(1)}, f32[1,16,2048]{2,1,0:T(8,128)S(1)}, u32[]{:S(2)}, u32[]{:S(2)}) collective-permute-start(f32[1,16,2048]{2,1,0:T(8,128)S(1)} %get-tuple-element.22), channel_id=1, source_target_pairs={{0,1},{1,0},{2,3},{3,2},{4,5},{5,4},{6,7},{7,6},{8,9},{9,8},{10,11... | collective-permute-start | bytes 393224 | tf_op jit(solution)/shard_map/ppermute | solution.py:194

commit v3 on v2

--- a/solution.py
+++ b/solution.py
@@ -1,3 +1,4 @@
+import functools
 import math
 
 import jax
@@ -17,7 +18,7 @@
 CHUNK = 4
 LANES = 128
 VMEM_BYTES = 48 * 1024 * 1024
-VMEM_MOST = 66584576
+VMEM_MOST = 65900000
 f32 = jnp.float32
 bf16 = jnp.bfloat16
 
@@ -54,22 +55,24 @@
     return x
 
 
-def pack_kernel(part_hbm, pose_hbm, mask_hbm, out_ref, weights_ref, pose_ref, mask_ref, sems):
-    dom, _, _ = out_ref.shape
+def pack_kernel(part_hbm, pose_hbm, mask_hbm, *refs):
+    slots, (pose_ref, mask_ref, sems) = refs[:-3], refs[-3:]
+    dom = len(slots)
     cols = part_hbm.shape[1] // dom
-    me, groups = lax.axis_index("cls"), lax.axis_size("cls")
+    d, me, groups = lax.axis_index("dom"), lax.axis_index("cls"), lax.axis_size("cls")
     k = pose_ref.shape[2]
     half = k // 2
-    wide = FINE * k
     small = [
         pltpu.make_async_copy(pose_hbm, pose_ref, sems.at[dom]),
         pltpu.make_async_copy(mask_hbm, mask_ref, sems.at[dom + 1]),
     ]
     large = [
         pltpu.make_async_copy(
-            part_hbm.at[:, pl.ds(d * cols, cols)], out_ref.at[d, :, pl.ds(0, cols)], sems.at[d]
+            part_hbm.at[:, pl.ds(pl.multiple_of((d ^ s) * cols, cols), cols)],
+            slots[s].at[:, pl.ds(0, cols)],
+            sems.at[s],
         )
-        for d in range(dom)
+        for s in range(dom)
     ]
     for copy in small + large:
         copy.start()
@@ -81,23 +84,23 @@
         w = swap_blocks(jnp.concatenate(fine, axis=1).astype(f32), me, k // groups, groups)
         pieces = [w[:, j * k + h * half : j * k + (h + 1) * half] for h in range(2) for j in range(FINE)]
         w = jnp.concatenate(pieces, axis=1).astype(bf16)
-        weights_ref[:, i * wide : (i + 1) * wide] = w
-        for d in range(dom):
-            out_ref[d, :, cols + i * wide : cols + (i + 1) * wide] = w
+        wide = w.shape[1]
+        for slot in slots:
+            slot[:, cols + i * wide : cols + (i + 1) * wide] = w
     for copy in large:
         copy.wait()
 
 
-def half_sums(got_ref, stack, half):
-    dom, n, width = got_ref.shape
+def rows_of(got, at):
+    return jnp.concatenate([g[:, at].astype(f32) for g in got], axis=0)
+
+
+def half_sums(got, stack, half):
     cols = stack.shape[1]
-    wide = (width - cols) // COARSE // 2
+    wide = (got[0].shape[1] - cols) // COARSE // 2
     k = wide // FINE
-    rows = []
-    for i in range(COARSE):
-        first = cols + (2 * i + half) * wide
-        rows.append(got_ref[:, :, first : first + wide].astype(f32).reshape(dom * n, wide))
-    w = jnp.concatenate(rows, axis=0).astype(bf16)
+    at = [slice(cols + (2 * i + half) * wide, cols + (2 * i + half + 1) * wide) for i in range(COARSE)]
+    w = jnp.concatenate([rows_of(got, a).astype(bf16) for a in at], axis=0)
     t = lax.dot_general(w, stack, (((0,), (0,)), ((), ())), preferred_element_type=f32)
     total = t[:k]
     for j in range(1, FINE):
@@ -113,22 +116,22 @@
             send_ref[m] = total[(2 * m + 1) * per : (2 * m + 2) * per]
 
 
-def far_sums_kernel(got_ref, stack_ref, keep_ref, send_ref):
-    dom, n, _ = got_ref.shape
+def far_sums_kernel(count, *refs):
+    got, (stack_ref, *outs) = refs[:count], refs[-3:]
     cols = stack_ref.shape[1]
-    part = got_ref[:, :, :cols].astype(f32).reshape(dom * n, cols)
+    part = rows_of(got, slice(0, cols))
     stack = jnp.concatenate([turn(part, -STEP * FINE * i).astype(bf16) for i in range(COARSE)], axis=0)
     stack_ref[...] = stack
-    put_pairs(half_sums(got_ref, stack, 1), keep_ref, send_ref)
-
-
-def near_sums_kernel(got_ref, stack_ref, keep_ref, send_ref):
-    put_pairs(half_sums(got_ref, stack_ref[...], 0), keep_ref, send_ref)
-
-
-def half_scores(part_ref, weights_ref, blocks, half):
-    n, length = part_ref.shape
-    k = blocks[0].shape[0] * len(blocks)
+    put_pairs(half_sums(got, stack, 1), *outs)
+
+
+def near_sums_kernel(count, stack_ref, *refs):
+    got, (keep_ref, send_ref) = refs[:count], refs[-2:]
+    put_pairs(half_sums(got, stack_ref[...], 0), keep_ref, send_ref)
+
+
+def correlate(part_ref, blocks):
+    length = part_ref.shape[1]
     chunk = CHUNK * ANG
     corr = None
     for c in range(length // chunk):
@@ -139,11 +142,18 @@
         right = jnp.concatenate([turn(cls, STEP * j).astype(bf16) for j in range(PAIR)], axis=0)
         more = lax.dot_general(left, right, (((1,), (1,)), ((), ())), preferred_element_type=f32)
         corr = more if corr is None else corr + more
-    wide = PAIR * k
+    return corr
+
+
+def weighted(corr, weights_ref, half):
+    n = weights_ref.shape[0]
+    wide = corr.shape[1]
+    k = wide // PAIR
+    cols = weights_ref.shape[1] - ROT * 2 * k
     total = None
     for m in range(ROT // PAIR):
         i, b = m // 2, m % 2
-        first = ((2 * i + half) * 2 + b) * wide
+        first = cols + ((2 * i + half) * 2 + b) * wide
         w = weights_ref[:, first : first + wide].astype(f32)
         more = w * corr[m * n : (m + 1) * n]
         total = more if total is None else total + more
@@ -153,15 +163,20 @@
     return out
 
 
+def guest_kernel(part_ref, packed_ref, *refs):
+    *blocks, out_ref, own_ref = refs
+    out_ref[...] = correlate(part_ref, blocks)
+    own_ref[...] = packed_ref[...]
+
+
 def near_scores_kernel(part_ref, weights_ref, *refs):
     *blocks, out_ref = refs
-    out_ref[...] = half_scores(part_ref, weights_ref, blocks, 0)
-
-
-def far_scores_kernel(near_ref, part_ref, weights_ref, *refs):
-    *blocks, out_ref = refs
+    out_ref[...] = weighted(correlate(part_ref, blocks), weights_ref, 0)
+
+
+def scores_kernel(near_ref, back_ref, weights_ref, out_ref):
     groups = lax.axis_size("cls")
-    far = half_scores(part_ref, weights_ref, blocks, 1)
+    far = weighted(back_ref[...], weights_ref, 1)
     out = jnp.concatenate([near_ref[...], far], axis=1)
     out_ref[...] = swap_blocks(out, lax.axis_index("cls"), out.shape[1] // groups, groups) / ROT
 
@@ -176,7 +191,7 @@
     hbm = pl.BlockSpec(memory_space=pl.ANY)
     vmem = pl.BlockSpec(memory_space=pltpu.VMEM)
 
-    def call(kernel, name, outs, ins, scratch=(), limit=VMEM_BYTES):
+    def call(kernel, name, outs, ins, scratch=(), limit=VMEM_BYTES, cost=None):
         return pl.pallas_call(
             kernel,
             out_shape=[jax.ShapeDtypeStruct(*o) for o in outs],
@@ -185,6 +200,7 @@
             scratch_shapes=list(scratch),
             compiler_params=pltpu.CompilerParams(vmem_limit_bytes=limit),
             name=name,
+            cost_estimate=cost,
         )
 
     def after(x, other):
@@ -203,10 +219,16 @@
                 keep, send = pairs[:, 0], pairs[:, 1]
         return keep[0]
 
-    packed, weights = call(
+    blocks = {0: references}
+    bit = last // 2
+    while bit:
+        blocks.update({s | bit: across(b, bit) for s, b in list(blocks.items())})
+        bit //= 2
+    near = [blocks[s] for s in range(last)]
+    packed = call(
         pack_kernel,
         "pack",
-        [((dom, n, cols + ROT * k), bf16), ((n, ROT * k), bf16)],
+        [((n, cols + ROT * k), bf16)] * dom,
         [hbm] * 3,
         [
             pltpu.VMEM(pose_weights.shape, jnp.int32),
@@ -215,36 +237,41 @@
         ],
         VMEM_MOST,
     )(particles, pose_weights, class_mask)
-    got = lax.all_to_all(packed, "dom", split_axis=0, concat_axis=0, tiled=True)
-    blocks = {0: references}
-    bit = last
-    while bit:
-        for s, b in list(blocks.items()):
-            blocks[s | bit] = across(after(b, packed) if s == 0 else b, bit)
-        bit //= 2
-    near, far = [blocks[s] for s in range(last)], [blocks[s] for s in range(last, groups)]
-    (near_scores,) = call(
-        near_scores_kernel, "near_scores", [((n, k // 2), f32)], [vmem] * (2 + last)
-    )(particles, weights, *near)
-    got = after(got, near_scores)
-
+    guests = across(after(particles, packed), last)
+    packed = after(packed, near)
+    got = [packed[0]]
+    for s in range(dom - 1, 0, -1):
+        x = packed[s]
+        got.append(lax.ppermute(x, "dom", [(d, d ^ s) for d in range(dom)]))
+
+    back, got[0] = call(
+        guest_kernel,
+        "guest_scores",
+        [((n * ROT // PAIR, PAIR * k // 2), f32), (packed[0].shape, bf16)],
+        [vmem] * (2 + last),
+    )(guests, packed[0], *near)
+    got = after(got, back)
     send_shape = (max(last // 2, 1), per, cols)
     stack, keep, send = call(
-        far_sums_kernel,
+        functools.partial(far_sums_kernel, dom),
         "far_sums",
         [((n * dom * COARSE, cols), bf16), (send_shape, f32), (send_shape, f32)],
-        [vmem],
-    )(got)
+        [vmem] * dom,
+    )(*got)
+    back = across(after(back, send), last)
     leaving = reduced(keep, send)
     arriving = across(leaving, last)
-    stack = after(stack, leaving)
-
-    keep, send = call(near_sums_kernel, "near_sums", [(send_shape, f32)] * 2, [vmem] * 2)(got, stack)
+    (near_scores,) = call(near_scores_kernel, "near_scores", [((n, k // 2), f32)], [vmem] * (2 + last))(
+        after(particles, leaving), got[0], *near
+    )
+    stack = after(stack, (near_scores, back))
+
+    keep, send = call(
+        functools.partial(near_sums_kernel, dom), "near_sums", [(send_shape, f32)] * 2, [vmem] * (1 + dom)
+    )(stack, *got)
     near_sums = reduced(keep, send)
 
-    (scored,) = call(far_scores_kernel, "far_scores", [((n, k), f32)], [vmem] * (3 + last))(
-        near_scores, particles, weights, *far
-    )
+    (scored,) = call(scores_kernel, "scores", [((n, k), f32)], [vmem] * 3)(near_scores, back, got[0])
     arriving = after(arriving, scored)
     class_sums = (near_sums + arriving) / math.sqrt(n * dom * groups * ROT)
     return (scored, class_sums)

time: 32.1 us -> 30.8 us (0.960)
  waiting for transfers between devices: 8.96 us -> 2.88 us
  starting transfers between devices: 10.6 us -> 16.2 us
  local copies, waits for them, and re-layouts: 2.74 us -> 1.87 us
    ppermute x0 -> x7, starting transfers between devices: none -> 11.1 us  [on_device(): got.append(lax.ppermute(x, 'dom', [(d, d ^ s) for d in range(dom)]))]
    all_to_all x1 -> x0, starting transfers between devices: 7.26 us -> none  [on_device(): got = lax.all_to_all(packed, 'dom', split_axis=0, concat_axis=0, tiled=True)]
    all_to_all x1 -> x0, waiting for transfers between devices: 6.48 us -> none  [on_device(): got = lax.all_to_all(packed, 'dom', split_axis=0, concat_axis=0, tiled=True)]
    ppermute x6, starting transfers between devices: 3.36 us -> 5.06 us  [across(): return lax.ppermute(x, 'cls', [(c, c ^ bit) for c in range(groups)])]
    ppermute x0 -> x7, waiting for transfers between devices: none -> 1.41 us  [on_device(): got.append(lax.ppermute(x, 'dom', [(d, d ^ s) for d in range(dom)]))]
    ppermute x6, waiting for transfers between devices: 2.48 us -> 1.47 us  [across(): return lax.ppermute(x, 'cls', [(c, c ^ bit) for c in range(groups)])]
    unnamed x10 -> x8, local copies, waits for them, and re-layouts: 2.74 us -> 1.87 us
    pallas_call x4 -> x5, Pallas kernels: 6.28 us -> 6.42 us  [the longest x1 2.08 us: on_device(): call(pack_kernel, 'pack', [((n, cols + ROT * k), bf16)] * dom, [hbm] * 3,...]
  transfers between devices with their start and end apart: 7 -> 13, of which waited for: 5 -> 5; matrix products, arithmetic and copies ran while one was open for 0% -> 0% of each run, Pallas kernels for 19% -> 24%
where the time goes in v3:
time: 30.8 us; the launch traced here: 30.5 us
  starting transfers between devices  16.2 us (53%)
  Pallas kernels  8.17 us (27%)
  waiting for transfers between devices  2.88 us (9%)
  local copies, waits for them, and re-layouts  1.87 us (6%)
  between operations  0.72 us (2%)
  other arithmetic  0.71 us (2%)
    ppermute x7, starting transfers between devices, on_device(): got.append(lax.ppermute(x, 'dom', [(d, d ^ s) for d in range(dom)]))  11.1 us
    ppermute x6, starting transfers between devices, across(): return lax.ppermute(x, 'cls', [(c, c ^ bit) for c in range(groups)])  5.06 us
    pallas_call x1, Pallas kernels, on_device(): call(pack_kernel, 'pack', [((n, cols + ROT * k), bf16)] * dom, [hbm] * 3,...  2.08 us
    unnamed x8, local copies, waits for them, and re-layouts  1.87 us
    pallas_call x1, Pallas kernels, on_device(): call(near_scores_kernel, 'near_scores', [((n, k // 2), f32)], [vmem] * (2...  1.75 us
    pallas_call x1, Pallas kernels, on_device(): call(guest_kernel, 'guest_scores', [((n * ROT // PAIR, PAIR * k // 2), f3...  1.55 us
    ppermute x6, waiting for transfers between devices, across(): return lax.ppermute(x, 'cls', [(c, c ^ bit) for c in range(groups)])  1.47 us
    ppermute x7, waiting for transfers between devices, on_device(): got.append(lax.ppermute(x, 'dom', [(d, d ^ s) for d in range(dom)]))  1.41 us
  transfers between devices with their start and end apart: 13, of which 5 were waited for; matrix products, arithmetic and copies ran while one was open for 0% of the time, Pallas kernels for 24%

profile of v3, /device:TPU:0, one launch (start us, length us, event | category | flops | bytes accessed | tf_op | source)
XLA Modules:
  0.0 30.5 jit_solution(9913963097812865140)
XLA Ops:
  0.6 0.0 copy-start.2
  0.6 0.5 %collective-permute-start.1 = (bf16[16,16384]{1,0:T(8,128)(2,1)}, bf16[16,16384]{1,0:T(8,128)(2,1)S(1)}, u32[]{:S(2)}, u32[]{:S(2)}) collective-permute-start(bf16[16,16384]{1,0:T(8,128)(2,1)} %refs_0_.3), channel_id=1, source_target_pairs={{0,1},{1,0},{2,3},{3,2},{4,5},{5,4},{6,7},{7,6},{8,9},{9,8},{10,11... | collective-permute-start | bytes 1572872 | tf_op jit(solution)/shard_map/ppermute | solution.py:210
  1.2 2.1 %pack.1 = (bf16[8,3584]{1,0:T(8,128)(2,1)}, bf16[8,3584]{1,0:T(8,128)(2,1)}, bf16[8,3584]{1,0:T(8,128)(2,1)}, bf16[8,3584]{1,0:T(8,128)(2,1)}, bf16[8,3584]{1,0:...) custom-call(bf16[8,16384]{1,0:T(8,128)(2,1)} %part_ref, ...), custom_call_target="tpu_custom_call" | custom-call | tf_op jit(solution)/shard_map/pack/pallas_call | solution.py:228
  3.2 2.6 %collective-permute-start = (bf16[8,16384]{1,0:T(8,128)(2,1)}, bf16[8,16384]{1,0:T(8,128)(2,1)S(1)}, u32[]{:S(2)}, u32[]{:S(2)}) collective-permute-start(bf16[8,16384]{1,0:T(8,128)(2,1)} %part_ref), channel_id=1, source_target_pairs={{0,2},{1,3},{2,0},{3,1},{4,6},{5,7},{6,4},{7,5},{8,10},{9,11},{10,... | collective-permute-start | bytes 786440 | tf_op jit(solution)/shard_map/ppermute | solution.py:210
  5.8 0.0 collective-permute-done.1.refs_1_
  5.8 4.5 %collective-permute-start.2 = (bf16[8,3584]{1,0:T(8,128)(2,1)}, bf16[8,3584]{1,0:T(8,128)(2,1)S(1)}, u32[]{:S(2)}, u32[]{:S(2)}) collective-permute-start(bf16[8,3584]{1,0:T(8,128)(2,1)} %get-tuple-element.49), channel_id=1, source_target_pairs={{0,28},{4,24},{8,20},{12,16},{16,12},{20,8},{24,4},{28,0},{1,29},{... | collective-permute-start | bytes 172040 | tf_op jit(solution)/shard_map/ppermute | solution.py:245
  10.4 0.2 collective-permute-start.3
  10.6 0.8 %collective-permute-start.4 = (bf16[8,3584]{1,0:T(8,128)(2,1)}, bf16[8,3584]{1,0:T(8,128)(2,1)S(1)}, u32[]{:S(2)}, u32[]{:S(2)}) collective-permute-start(bf16[8,3584]{1,0:T(8,128)(2,1)} %get-tuple-element.51), channel_id=1, source_target_pairs={{0,20},{4,16},{8,28},{12,24},{16,4},{20,0},{24,12},{28,8},{1,21},{... | collective-permute-start | bytes 172040 | tf_op jit(solution)/shard_map/ppermute | solution.py:245
  11.4 2.1 %collective-permute-start.5 = (bf16[8,3584]{1,0:T(8,128)(2,1)}, bf16[8,3584]{1,0:T(8,128)(2,1)S(1)}, u32[]{:S(2)}, u32[]{:S(2)}) collective-permute-start(bf16[8,3584]{1,0:T(8,128)(2,1)} %get-tuple-element.52), channel_id=1, source_target_pairs={{0,16},{4,20},{8,24},{12,28},{16,0},{20,4},{24,8},{28,12},{1,17},{... | collective-permute-start | bytes 172040 | tf_op jit(solution)/shard_map/ppermute | solution.py:245
  13.5 0.0 collective-permute-done.part_ref
  13.5 2.2 %collective-permute-start.6 = (bf16[8,3584]{1,0:T(8,128)(2,1)}, bf16[8,3584]{1,0:T(8,128)(2,1)S(1)}, u32[]{:S(2)}, u32[]{:S(2)}) collective-permute-start(bf16[8,3584]{1,0:T(8,128)(2,1)} %get-tuple-element.53), channel_id=1, source_target_pairs={{0,12},{4,8},{8,4},{12,0},{16,28},{20,24},{24,20},{28,16},{1,13},{... | collective-permute-start | bytes 172040 | tf_op jit(solution)/shard_map/ppermute | solution.py:245
  15.7 0.0 collective-permute-done.2.refs_1_
  15.7 0.7 %collective-permute-start.7 = (bf16[8,3584]{1,0:T(8,128)(2,1)}, bf16[8,3584]{1,0:T(8,128)(2,1)S(1)}, u32[]{:S(2)}, u32[]{:S(2)}) collective-permute-start(bf16[8,3584]{1,0:T(8,128)(2,1)} %get-tuple-element.54), channel_id=1, source_target_pairs={{0,8},{4,12},{8,0},{12,4},{16,24},{20,28},{24,16},{28,20},{1,9},{5... | collective-permute-start | bytes 172040 | tf_op jit(solution)/shard_map/ppermute | solution.py:245
  16.5 0.4 %collective-permute-done.3.refs_2_ = bf16[8,3584]{1,0:T(8,128)(2,1)S(1)} collective-permute-done((bf16[8,3584]{1,0:T(8,128)(2,1)}, bf16[8,3584]{1,0:T(8,128)(2,1)S(1)}, u32[]{:S(2)}, u32[]{:S(2)}) %collective-permute-start.3) | collective-permute-done | bytes 57376 | tf_op jit(solution)/shard_map/ppermute | solution.py:245
  16.9 0.5 %collective-permute-start.8 = (bf16[8,3584]{1,0:T(8,128)(2,1)}, bf16[8,3584]{1,0:T(8,128)(2,1)S(1)}, u32[]{:S(2)}, u32[]{:S(2)}) collective-permute-start(bf16[8,3584]{1,0:T(8,128)(2,1)} %get-tuple-element.55), channel_id=1, source_target_pairs={{0,4},{4,0},{8,12},{12,8},{16,20},{20,16},{24,28},{28,24},{1,5},{5... | collective-permute-start | bytes 172040 | tf_op jit(solution)/shard_map/ppermute | solution.py:245
  17.4 0.0 copy-start
  17.4 1.0 %copy-done = bf16[16,16384]{1,0:T(8,128)(2,1)S(1)} copy-done((bf16[16,16384]{1,0:T(8,128)(2,1)S(1)}, bf16[16,16384]{1,0:T(8,128)(2,1)}, u32[]{:S(2)}) %copy-start) | copy-done | bytes 524312
  18.4 0.0 copy-start.3
  18.5 0.8 %copy-done.3 = bf16[8,3584]{1,0:T(8,128)(2,1)S(1)} copy-done((bf16[8,3584]{1,0:T(8,128)(2,1)S(1)}, bf16[8,3584]{1,0:T(8,128)(2,1)}, u32[]{:S(2)}) %copy-start.3) | copy-done | bytes 57368
  19.3 0.0 copy-start.1
  19.3 1.6 %guest_scores.1 = (f32[96,64]{1,0:T(8,128)S(1)}, bf16[8,3584]{1,0:T(8,128)(2,1)S(1)}) custom-call(bf16[8,16384]{1,0:T(8,128)(2,1)S(1)} %collective-permute-done.part_ref, bf16[8,3584]{1,0:T(8,128)(2,1)S(1)} %copy-done.3, bf16[16,16384]{1,0:T(8,128)(2,1)S(1)} %copy-done, bf16[16,16384]{1,0:T(8,128)(2,1)S(1)} %collective-permute-done.1.refs_1_), custom_call_target="tpu_custom_call" | custom-call | tf_op jit(solution)/shard_map/guest_scores/pallas_call | solution.py:247
  20.8 0.0 collective-permute-done.4.refs_3_
  20.8 0.0 collective-permute-done.5.refs_4_
  20.9 0.0 collective-permute-done.6.refs_5_
  20.9 1.0 %collective-permute-done.7.refs_6_ = bf16[8,3584]{1,0:T(8,128)(2,1)S(1)} collective-permute-done((bf16[8,3584]{1,0:T(8,128)(2,1)}, bf16[8,3584]{1,0:T(8,128)(2,1)S(1)}, u32[]{:S(2)}, u32[]{:S(2)}) %collective-permute-start.7) | collective-permute-done | bytes 57376 | tf_op jit(solution)/shard_map/ppermute | solution.py:245
  21.8 0.0 collective-permute-done.8.refs_7_
  21.9 0.9 %far_sums.1 = (bf16[384,2048]{1,0:T(8,128)(2,1)S(1)}, f32[1,16,2048]{2,1,0:T(8,128)S(1)}, f32[1,16,2048]{2,1,0:T(8,128)S(1)}) custom-call(bf16[8,3584]{1,0:T(8,128)(2,1)S(1)} %get-tuple-element.57.refs_0_.weights_ref, bf16[8,3584]{1,0:T(8,128)(2,1)S(1)} %collective-permute-done.2.refs_1_, bf16[8,3584]{1,0:T(8,128)(2,1)S(1)} %collective-permute-done.3.refs_2_, ...), custom_call_target="tpu_custom_call" | custom-call | tf_op jit(solution)/shard_map/far_sums/pallas_call | solution.py:255
  22.8 0.1 collective-permute-start.9
  22.9 0.9 %collective-permute-start.10 = (f32[96,64]{1,0:T(8,128)S(1)}, f32[96,64]{1,0:T(8,128)S(1)}, u32[]{:S(2)}, u32[]{:S(2)}) collective-permute-start(f32[96,64]{1,0:T(8,128)S(1)} %get-tuple-element.68), channel_id=1, source_target_pairs={{0,2},{1,3},{2,0},{3,1},{4,6},{5,7},{6,4},{7,5},{8,10},{9,11},{10,... | collective-permute-start | bytes 73736 | tf_op jit(solution)/shard_map/ppermute | solution.py:210
  23.8 0.4 %collective-permute-done.9 = f32[1,16,2048]{2,1,0:T(8,128)S(1)} collective-permute-done((f32[1,16,2048]{2,1,0:T(8,128)S(1)}, f32[1,16,2048]{2,1,0:T(8,128)S(1)}, u32[]{:S(2)}, u32[]{:S(2)}) %collective-permute-start.9) | collective-permute-done | bytes 131104 | tf_op jit(solution)/shard_map/ppermute | solution.py:210
  24.2 0.9 %collective-permute-start.12 = (f32[16,2048]{1,0:T(8,128)S(1)}, f32[16,2048]{1,0:T(8,128)S(1)}, u32[]{:S(2)}, u32[]{:S(2)}) collective-permute-start(f32[16,2048]{1,0:T(8,128)S(1)} %add_bitcast_fusion), channel_id=1, source_target_pairs={{0,2},{1,3},{2,0},{3,1},{4,6},{5,7},{6,4},{7,5},{8,10},{9,11},{10,... | collective-permute-start | bytes 393224 | tf_op jit(solution)/shard_map/ppermute | solution.py:210
  25.1 0.0 copy-done.2
  25.1 0.0 copy-done.1
  25.1 1.7 %near_scores.1.near_ref = f32[8,32]{1,0:T(8,128)S(1)} custom-call(bf16[8,16384]{1,0:T(8,128)(2,1)S(1)} %copy-done.2, bf16[8,3584]{1,0:T(8,128)(2,1)S(1)} %get-tuple-element.57.refs_0_.weights_ref, bf16[16,16384]{1,0:T(8,128)(2,1)S(1)} %copy-done.1, bf16[16,16384]{1,0:T(8,128)(2,1)S(1)} %collective-permute-done.1.refs_1_), custom_call_target="tpu_custom_call" | custom-call | tf_op jit(solution)/shard_map/near_scores/pallas_call | solution.py:264
  26.9 0.2 collective-permute-done.10.back_ref
  27.0 0.6 %near_sums.1 = (f32[1,16,2048]{2,1,0:T(8,128)S(1)}, f32[1,16,2048]{2,1,0:T(8,128)S(1)}) custom-call(bf16[384,2048]{1,0:T(8,128)(2,1)S(1)} %get-tuple-element.70.stack_ref, bf16[8,3584]{1,0:T(8,128)(2,1)S(1)} %get-tuple-element.57.refs_0_.weights_ref, bf16[8,3584]{1,0:T(8,128)(2,1)S(1)} %collective-permute-done.2.refs_1_, ...), custom_call_target="tpu_custom_call" | custom-call | tf_op jit(solution)/shard_map/near_sums/pallas_call | solution.py:269
  27.6 0.1 collective-permute-start.11
  27.7 1.3 %scores.1 = f32[8,64]{1,0:T(8,128)} custom-call(f32[8,32]{1,0:T(8,128)S(1)} %near_scores.1.near_ref, f32[96,64]{1,0:T(8,128)S(1)} %collective-permute-done.10.back_ref, bf16[8,3584]{1,0:T(8,128)(2,1)S(1)} %get-tuple-element.57.refs_0_.weights_ref), custom_call_target="tpu_custom_call" | custom-call | tf_op jit(solution)/shard_map/scores/pallas_call | solution.py:274
  29.0 0.9 %collective-permute-done.12 = f32[16,2048]{1,0:T(8,128)S(1)} collective-permute-done((f32[16,2048]{1,0:T(8,128)S(1)}, f32[16,2048]{1,0:T(8,128)S(1)}, u32[]{:S(2)}, u32[]{:S(2)}) %collective-permute-start.12) | collective-permute-done | bytes 131104 | tf_op jit(solution)/shard_map/ppermute | solution.py:210
  29.9 0.0 collective-permute-done.11
  29.9 0.7 %fusion = f32[16,2048]{1,0:T(8,128)} fusion(f32[16,2048]{1,0:T(8,128)S(1)} %collective-permute-done.12, f32[1,16,2048]{2,1,0:T(8,128)S(1)} %get-tuple-element.71, f32[1,16,2048]{2,1,0:T(8,128)S(1)} %collective-permute-done.11), kind=kLoop, calls=%fused_computation.1 | loop fusion | flops 98304 | bytes 524288 | tf_op jit(solution)/shard_map/div | solution.py:276
  (1 shorter events, 0.0 us)
Async XLA Ops:
  0.6 24.5 %copy-start.2 = (bf16[8,16384]{1,0:T(8,128)(2,1)S(1)}, bf16[8,16384]{1,0:T(8,128)(2,1)}, u32[]{:S(2)}) copy-start(bf16[8,16384]{1,0:T(8,128)(2,1)} %part_ref) | copy-start | bytes 786436
  0.6 5.2 %collective-permute-start.1 = (bf16[16,16384]{1,0:T(8,128)(2,1)}, bf16[16,16384]{1,0:T(8,128)(2,1)S(1)}, u32[]{:S(2)}, u32[]{:S(2)}) collective-permute-start(bf16[16,16384]{1,0:T(8,128)(2,1)} %refs_0_.3), channel_id=1, source_target_pairs={{0,1},{1,0},{2,3},{3,2},{4,5},{5,4},{6,7},{7,6},{8,9},{9,8},{10,11... | collective-permute-start | bytes 1572872 | tf_op jit(solution)/shard_map/ppermute | solution.py:210
  3.2 10.3 %collective-permute-start = (bf16[8,16384]{1,0:T(8,128)(2,1)}, bf16[8,16384]{1,0:T(8,128)(2,1)S(1)}, u32[]{:S(2)}, u32[]{:S(2)}) collective-permute-start(bf16[8,16384]{1,0:T(8,128)(2,1)} %part_ref), channel_id=1, source_target_pairs={{0,2},{1,3},{2,0},{3,1},{4,6},{5,7},{6,4},{7,5},{8,10},{9,11},{10,... | collective-permute-start | bytes 786440 | tf_op jit(solution)/shard_map/ppermute | solution.py:210
  5.8 9.9 %collective-permute-start.2 = (bf16[8,3584]{1,0:T(8,128)(2,1)}, bf16[8,3584]{1,0:T(8,128)(2,1)S(1)}, u32[]{:S(2)}, u32[]{:S(2)}) collective-permute-start(bf16[8,3584]{1,0:T(8,128)(2,1)} %get-tuple-element.49), channel_id=1, source_target_pairs={{0,28},{4,24},{8,20},{12,16},{16,12},{20,8},{24,4},{28,0},{1,29},{... | collective-permute-start | bytes 172040 | tf_op jit(solution)/shard_map/ppermute | solution.py:245
  10.4 6.5 %collective-permute-start.3 = (bf16[8,3584]{1,0:T(8,128)(2,1)}, bf16[8,3584]{1,0:T(8,128)(2,1)S(1)}, u32[]{:S(2)}, u32[]{:S(2)}) collective-permute-start(bf16[8,3584]{1,0:T(8,128)(2,1)} %get-tuple-element.50), channel_id=1, source_target_pairs={{0,24},{4,28},{8,16},{12,20},{16,8},{20,12},{24,0},{28,4},{1,25},{... | collective-permute-start | bytes 172040 | tf_op jit(solution)/shard_map/ppermute | solution.py:245
  10.6 10.2 %collective-permute-start.4 = (bf16[8,3584]{1,0:T(8,128)(2,1)}, bf16[8,3584]{1,0:T(8,128)(2,1)S(1)}, u32[]{:S(2)}, u32[]{:S(2)}) collective-permute-start(bf16[8,3584]{1,0:T(8,128)(2,1)} %get-tuple-element.51), channel_id=1, source_target_pairs={{0,20},{4,16},{8,28},{12,24},{16,4},{20,0},{24,12},{28,8},{1,21},{... | collective-permute-start | bytes 172040 | tf_op jit(solution)/shard_map/ppermute | solution.py:245
  11.4 9.5 %collective-permute-start.5 = (bf16[8,3584]{1,0:T(8,128)(2,1)}, bf16[8,3584]{1,0:T(8,128)(2,1)S(1)}, u32[]{:S(2)}, u32[]{:S(2)}) collective-permute-start(bf16[8,3584]{1,0:T(8,128)(2,1)} %get-tuple-element.52), channel_id=1, source_target_pairs={{0,16},{4,20},{8,24},{12,28},{16,0},{20,4},{24,8},{28,12},{1,17},{... | collective-permute-start | bytes 172040 | tf_op jit(solution)/shard_map/ppermute | solution.py:245
  13.5 7.4 %collective-permute-start.6 = (bf16[8,3584]{1,0:T(8,128)(2,1)}, bf16[8,3584]{1,0:T(8,128)(2,1)S(1)}, u32[]{:S(2)}, u32[]{:S(2)}) collective-permute-start(bf16[8,3584]{1,0:T(8,128)(2,1)} %get-tuple-element.53), channel_id=1, source_target_pairs={{0,12},{4,8},{8,4},{12,0},{16,28},{20,24},{24,20},{28,16},{1,13},{... | collective-permute-start | bytes 172040 | tf_op jit(solution)/shard_map/ppermute | solution.py:245
  15.7 6.1 %collective-permute-start.7 = (bf16[8,3584]{1,0:T(8,128)(2,1)}, bf16[8,3584]{1,0:T(8,128)(2,1)S(1)}, u32[]{:S(2)}, u32[]{:S(2)}) collective-permute-start(bf16[8,3584]{1,0:T(8,128)(2,1)} %get-tuple-element.54), channel_id=1, source_target_pairs={{0,8},{4,12},{8,0},{12,4},{16,24},{20,28},{24,16},{28,20},{1,9},{5... | collective-permute-start | bytes 172040 | tf_op jit(solution)/shard_map/ppermute | solution.py:245
  16.9 5.0 %collective-permute-start.8 = (bf16[8,3584]{1,0:T(8,128)(2,1)}, bf16[8,3584]{1,0:T(8,128)(2,1)S(1)}, u32[]{:S(2)}, u32[]{:S(2)}) collective-permute-start(bf16[8,3584]{1,0:T(8,128)(2,1)} %get-tuple-element.55), channel_id=1, source_target_pairs={{0,4},{4,0},{8,12},{12,8},{16,20},{20,16},{24,28},{28,24},{1,5},{5... | collective-permute-start | bytes 172040 | tf_op jit(solution)/shard_map/ppermute | solution.py:245
  17.4 1.0 %copy-start = (bf16[16,16384]{1,0:T(8,128)(2,1)S(1)}, bf16[16,16384]{1,0:T(8,128)(2,1)}, u32[]{:S(2)}) copy-start(bf16[16,16384]{1,0:T(8,128)(2,1)} %refs_0_.3) | copy-start | bytes 1572868
  18.4 0.8 %copy-start.3 = (bf16[8,3584]{1,0:T(8,128)(2,1)S(1)}, bf16[8,3584]{1,0:T(8,128)(2,1)}, u32[]{:S(2)}) copy-start(bf16[8,3584]{1,0:T(8,128)(2,1)} %get-tuple-element.47.packed_ref) | copy-start | bytes 172036
  19.3 5.9 %copy-start.1 = (bf16[16,16384]{1,0:T(8,128)(2,1)S(1)}, bf16[16,16384]{1,0:T(8,128)(2,1)}, u32[]{:S(2)}) copy-start(bf16[16,16384]{1,0:T(8,128)(2,1)} %refs_0_.3) | copy-start | bytes 1572868
  22.8 1.4 %collective-permute-start.9 = (f32[1,16,2048]{2,1,0:T(8,128)S(1)}, f32[1,16,2048]{2,1,0:T(8,128)S(1)}, u32[]{:S(2)}, u32[]{:S(2)}) collective-permute-start(f32[1,16,2048]{2,1,0:T(8,128)S(1)} %get-tuple-element.66), channel_id=1, source_target_pairs={{0,1},{1,0},{2,3},{3,2},{4,5},{5,4},{6,7},{7,6},{8,9},{9,8},{10,11... | collective-permute-start | bytes 393224 | tf_op jit(solution)/shard_map/ppermute | solution.py:210
  22.9 4.2 %collective-permute-start.10 = (f32[96,64]{1,0:T(8,128)S(1)}, f32[96,64]{1,0:T(8,128)S(1)}, u32[]{:S(2)}, u32[]{:S(2)}) collective-permute-start(f32[96,64]{1,0:T(8,128)S(1)} %get-tuple-element.68), channel_id=1, source_target_pairs={{0,2},{1,3},{2,0},{3,1},{4,6},{5,7},{6,4},{7,5},{8,10},{9,11},{10,... | collective-permute-start | bytes 73736 | tf_op jit(solution)/shard_map/ppermute | solution.py:210
  24.2 5.6 %collective-permute-start.12 = (f32[16,2048]{1,0:T(8,128)S(1)}, f32[16,2048]{1,0:T(8,128)S(1)}, u32[]{:S(2)}, u32[]{:S(2)}) collective-permute-start(f32[16,2048]{1,0:T(8,128)S(1)} %add_bitcast_fusion), channel_id=1, source_target_pairs={{0,2},{1,3},{2,0},{3,1},{4,6},{5,7},{6,4},{7,5},{8,10},{9,11},{10,... | collective-permute-start | bytes 393224 | tf_op jit(solution)/shard_map/ppermute | solution.py:210
  27.6 2.2 %collective-permute-start.11 = (f32[1,16,2048]{2,1,0:T(8,128)S(1)}, f32[1,16,2048]{2,1,0:T(8,128)S(1)}, u32[]{:S(2)}, u32[]{:S(2)}) collective-permute-start(f32[1,16,2048]{2,1,0:T(8,128)S(1)} %get-tuple-element.72), channel_id=1, source_target_pairs={{0,1},{1,0},{2,3},{3,2},{4,5},{5,4},{6,7},{7,6},{8,9},{9,8},{10,11... | collective-permute-start | bytes 393224 | tf_op jit(solution)/shard_map/ppermute | solution.py:210

commit v4 on v3

--- a/solution.py
+++ b/solution.py
@@ -237,13 +237,13 @@
         ],
         VMEM_MOST,
     )(particles, pose_weights, class_mask)
-    guests = across(after(particles, packed), last)
     packed = after(packed, near)
     got = [packed[0]]
     for s in range(dom - 1, 0, -1):
         x = packed[s]
         got.append(lax.ppermute(x, "dom", [(d, d ^ s) for d in range(dom)]))
 
+    guests = across(particles, last)
     back, got[0] = call(
         guest_kernel,
         "guest_scores",

time: 30.8 us -> 30.4 us (0.987)
  starting transfers between devices: 16.2 us -> 15.8 us
    ppermute x6, waiting for transfers between devices: 1.47 us -> 1.89 us  [across(): return lax.ppermute(x, 'cls', [(c, c ^ bit) for c in range(groups)])]
    ppermute x6, starting transfers between devices: 5.06 us -> 4.65 us  [across(): return lax.ppermute(x, 'cls', [(c, c ^ bit) for c in range(groups)])]
    ppermute x7, waiting for transfers between devices: 1.41 us -> 1.04 us  [on_device(): got.append(lax.ppermute(x, 'dom', [(d, d ^ s) for d in range(dom)]))]
where the time goes in v4:
time: 30.4 us; the launch traced here: 30.2 us
  starting transfers between devices  15.8 us (52%)
  Pallas kernels  8.16 us (27%)
  waiting for transfers between devices  2.92 us (10%)
  local copies, waits for them, and re-layouts  1.87 us (6%)
  between operations  0.72 us (2%)
  other arithmetic  0.7 us (2%)
    ppermute x7, starting transfers between devices, on_device(): got.append(lax.ppermute(x, 'dom', [(d, d ^ s) for d in range(dom)]))  11.1 us
    ppermute x6, starting transfers between devices, across(): return lax.ppermute(x, 'cls', [(c, c ^ bit) for c in range(groups)])  4.65 us
    pallas_call x1, Pallas kernels, on_device(): call(pack_kernel, 'pack', [((n, cols + ROT * k), bf16)] * dom, [hbm] * 3,...  2.08 us
    ppermute x6, waiting for transfers between devices, across(): return lax.ppermute(x, 'cls', [(c, c ^ bit) for c in range(groups)])  1.89 us
    unnamed x8, local copies, waits for them, and re-layouts  1.87 us
    pallas_call x1, Pallas kernels, on_device(): call(near_scores_kernel, 'near_scores', [((n, k // 2), f32)], [vmem] * (2...  1.75 us
    pallas_call x1, Pallas kernels, on_device(): call(guest_kernel, 'guest_scores', [((n * ROT // PAIR, PAIR * k // 2), f3...  1.56 us
    pallas_call x1, Pallas kernels, on_device(): call(scores_kernel, 'scores', [((n, k), f32)], [vmem] * 3)  1.29 us
  transfers between devices with their start and end apart: 13, of which 5 were waited for; matrix products, arithmetic and copies ran while one was open for 0% of the time, Pallas kernels for 24%

profile of v4, /device:TPU:0, one launch (start us, length us, event | category | flops | bytes accessed | tf_op | source)
XLA Modules:
  0.0 30.2 jit_solution(2672275201701145018)
XLA Ops:
  0.6 0.0 copy-start.2
  0.6 0.5 %collective-permute-start.1 = (bf16[16,16384]{1,0:T(8,128)(2,1)}, bf16[16,16384]{1,0:T(8,128)(2,1)S(1)}, u32[]{:S(2)}, u32[]{:S(2)}) collective-permute-start(bf16[16,16384]{1,0:T(8,128)(2,1)} %refs_0_.3), channel_id=1, source_target_pairs={{0,1},{1,0},{2,3},{3,2},{4,5},{5,4},{6,7},{7,6},{8,9},{9,8},{10,11... | collective-permute-start | bytes 1572872 | tf_op jit(solution)/shard_map/ppermute | solution.py:210
  1.2 2.6 %collective-permute-start = (bf16[8,16384]{1,0:T(8,128)(2,1)}, bf16[8,16384]{1,0:T(8,128)(2,1)S(1)}, u32[]{:S(2)}, u32[]{:S(2)}) collective-permute-start(bf16[8,16384]{1,0:T(8,128)(2,1)} %part_ref), channel_id=1, source_target_pairs={{0,2},{1,3},{2,0},{3,1},{4,6},{5,7},{6,4},{7,5},{8,10},{9,11},{10,... | collective-permute-start | bytes 786440 | tf_op jit(solution)/shard_map/ppermute | solution.py:210
  3.8 2.1 %pack.1 = (bf16[8,3584]{1,0:T(8,128)(2,1)}, bf16[8,3584]{1,0:T(8,128)(2,1)}, bf16[8,3584]{1,0:T(8,128)(2,1)}, bf16[8,3584]{1,0:T(8,128)(2,1)}, bf16[8,3584]{1,0:...) custom-call(bf16[8,16384]{1,0:T(8,128)(2,1)} %part_ref, ...), custom_call_target="tpu_custom_call" | custom-call | tf_op jit(solution)/shard_map/pack/pallas_call | solution.py:228
  5.8 0.0 collective-permute-done.1.refs_1_
  5.9 4.6 %collective-permute-start.2 = (bf16[8,3584]{1,0:T(8,128)(2,1)}, bf16[8,3584]{1,0:T(8,128)(2,1)S(1)}, u32[]{:S(2)}, u32[]{:S(2)}) collective-permute-start(bf16[8,3584]{1,0:T(8,128)(2,1)} %get-tuple-element.47), channel_id=1, source_target_pairs={{0,28},{4,24},{8,20},{12,16},{16,12},{20,8},{24,4},{28,0},{1,29},{... | collective-permute-start | bytes 172040 | tf_op jit(solution)/shard_map/ppermute | solution.py:244
  10.4 0.2 collective-permute-start.3
  10.7 0.8 %collective-permute-start.4 = (bf16[8,3584]{1,0:T(8,128)(2,1)}, bf16[8,3584]{1,0:T(8,128)(2,1)S(1)}, u32[]{:S(2)}, u32[]{:S(2)}) collective-permute-start(bf16[8,3584]{1,0:T(8,128)(2,1)} %get-tuple-element.49), channel_id=1, source_target_pairs={{0,20},{4,16},{8,28},{12,24},{16,4},{20,0},{24,12},{28,8},{1,21},{... | collective-permute-start | bytes 172040 | tf_op jit(solution)/shard_map/ppermute | solution.py:244
  11.4 2.1 %collective-permute-start.5 = (bf16[8,3584]{1,0:T(8,128)(2,1)}, bf16[8,3584]{1,0:T(8,128)(2,1)S(1)}, u32[]{:S(2)}, u32[]{:S(2)}) collective-permute-start(bf16[8,3584]{1,0:T(8,128)(2,1)} %get-tuple-element.50), channel_id=1, source_target_pairs={{0,16},{4,20},{8,24},{12,28},{16,0},{20,4},{24,8},{28,12},{1,17},{... | collective-permute-start | bytes 172040 | tf_op jit(solution)/shard_map/ppermute | solution.py:244
  13.6 0.0 collective-permute-done.part_ref
  13.6 2.2 %collective-permute-start.6 = (bf16[8,3584]{1,0:T(8,128)(2,1)}, bf16[8,3584]{1,0:T(8,128)(2,1)S(1)}, u32[]{:S(2)}, u32[]{:S(2)}) collective-permute-start(bf16[8,3584]{1,0:T(8,128)(2,1)} %get-tuple-element.51), channel_id=1, source_target_pairs={{0,12},{4,8},{8,4},{12,0},{16,28},{20,24},{24,20},{28,16},{1,13},{... | collective-permute-start | bytes 172040 | tf_op jit(solution)/shard_map/ppermute | solution.py:244
  15.7 0.0 collective-permute-done.2.refs_1_
  15.7 0.8 %collective-permute-start.7 = (bf16[8,3584]{1,0:T(8,128)(2,1)}, bf16[8,3584]{1,0:T(8,128)(2,1)S(1)}, u32[]{:S(2)}, u32[]{:S(2)}) collective-permute-start(bf16[8,3584]{1,0:T(8,128)(2,1)} %get-tuple-element.52), channel_id=1, source_target_pairs={{0,8},{4,12},{8,0},{12,4},{16,24},{20,28},{24,16},{28,20},{1,9},{5... | collective-permute-start | bytes 172040 | tf_op jit(solution)/shard_map/ppermute | solution.py:244
  16.5 0.4 %collective-permute-done.3.refs_2_ = bf16[8,3584]{1,0:T(8,128)(2,1)S(1)} collective-permute-done((bf16[8,3584]{1,0:T(8,128)(2,1)}, bf16[8,3584]{1,0:T(8,128)(2,1)S(1)}, u32[]{:S(2)}, u32[]{:S(2)}) %collective-permute-start.3) | collective-permute-done | bytes 57376 | tf_op jit(solution)/shard_map/ppermute | solution.py:244
  17.0 0.5 %collective-permute-start.8 = (bf16[8,3584]{1,0:T(8,128)(2,1)}, bf16[8,3584]{1,0:T(8,128)(2,1)S(1)}, u32[]{:S(2)}, u32[]{:S(2)}) collective-permute-start(bf16[8,3584]{1,0:T(8,128)(2,1)} %get-tuple-element.53), channel_id=1, source_target_pairs={{0,4},{4,0},{8,12},{12,8},{16,20},{20,16},{24,28},{28,24},{1,5},{5... | collective-permute-start | bytes 172040 | tf_op jit(solution)/shard_map/ppermute | solution.py:244
  17.4 0.0 copy-start
  17.4 1.0 %copy-done = bf16[16,16384]{1,0:T(8,128)(2,1)S(1)} copy-done((bf16[16,16384]{1,0:T(8,128)(2,1)S(1)}, bf16[16,16384]{1,0:T(8,128)(2,1)}, u32[]{:S(2)}) %copy-start) | copy-done | bytes 524312
  18.5 0.0 copy-start.3
  18.5 0.8 %copy-done.3 = bf16[8,3584]{1,0:T(8,128)(2,1)S(1)} copy-done((bf16[8,3584]{1,0:T(8,128)(2,1)S(1)}, bf16[8,3584]{1,0:T(8,128)(2,1)}, u32[]{:S(2)}) %copy-start.3) | copy-done | bytes 57368
  19.3 0.0 copy-start.1
  19.3 1.6 %guest_scores.1 = (f32[96,64]{1,0:T(8,128)S(1)}, bf16[8,3584]{1,0:T(8,128)(2,1)S(1)}) custom-call(bf16[8,16384]{1,0:T(8,128)(2,1)S(1)} %collective-permute-done.part_ref, bf16[8,3584]{1,0:T(8,128)(2,1)S(1)} %copy-done.3, bf16[16,16384]{1,0:T(8,128)(2,1)S(1)} %copy-done, bf16[16,16384]{1,0:T(8,128)(2,1)S(1)} %collective-permute-done.1.refs_1_), custom_call_target="tpu_custom_call" | custom-call | tf_op jit(solution)/shard_map/guest_scores/pallas_call | solution.py:247
  20.9 0.0 collective-permute-done.4.refs_3_
  20.9 0.0 collective-permute-done.5.refs_4_
  20.9 0.0 collective-permute-done.6.refs_5_
  21.0 0.5 %collective-permute-done.7.refs_6_ = bf16[8,3584]{1,0:T(8,128)(2,1)S(1)} collective-permute-done((bf16[8,3584]{1,0:T(8,128)(2,1)}, bf16[8,3584]{1,0:T(8,128)(2,1)S(1)}, u32[]{:S(2)}, u32[]{:S(2)}) %collective-permute-start.7) | collective-permute-done | bytes 57376 | tf_op jit(solution)/shard_map/ppermute | solution.py:244
  21.5 0.0 collective-permute-done.8.refs_7_
  21.5 0.9 %far_sums.1 = (bf16[384,2048]{1,0:T(8,128)(2,1)S(1)}, f32[1,16,2048]{2,1,0:T(8,128)S(1)}, f32[1,16,2048]{2,1,0:T(8,128)S(1)}) custom-call(bf16[8,3584]{1,0:T(8,128)(2,1)S(1)} %get-tuple-element.55.refs_0_.weights_ref, bf16[8,3584]{1,0:T(8,128)(2,1)S(1)} %collective-permute-done.2.refs_1_, bf16[8,3584]{1,0:T(8,128)(2,1)S(1)} %collective-permute-done.3.refs_2_, ...), custom_call_target="tpu_custom_call" | custom-call | tf_op jit(solution)/shard_map/far_sums/pallas_call | solution.py:255
  22.4 0.1 collective-permute-start.9
  22.5 0.6 %collective-permute-start.10 = (f32[96,64]{1,0:T(8,128)S(1)}, f32[96,64]{1,0:T(8,128)S(1)}, u32[]{:S(2)}, u32[]{:S(2)}) collective-permute-start(f32[96,64]{1,0:T(8,128)S(1)} %get-tuple-element.66), channel_id=1, source_target_pairs={{0,2},{1,3},{2,0},{3,1},{4,6},{5,7},{6,4},{7,5},{8,10},{9,11},{10,... | collective-permute-start | bytes 73736 | tf_op jit(solution)/shard_map/ppermute | solution.py:210
  23.1 0.8 %collective-permute-done.9 = f32[1,16,2048]{2,1,0:T(8,128)S(1)} collective-permute-done((f32[1,16,2048]{2,1,0:T(8,128)S(1)}, f32[1,16,2048]{2,1,0:T(8,128)S(1)}, u32[]{:S(2)}, u32[]{:S(2)}) %collective-permute-start.9) | collective-permute-done | bytes 131104 | tf_op jit(solution)/shard_map/ppermute | solution.py:210
  23.9 0.8 %collective-permute-start.12 = (f32[16,2048]{1,0:T(8,128)S(1)}, f32[16,2048]{1,0:T(8,128)S(1)}, u32[]{:S(2)}, u32[]{:S(2)}) collective-permute-start(f32[16,2048]{1,0:T(8,128)S(1)} %add_bitcast_fusion), channel_id=1, source_target_pairs={{0,2},{1,3},{2,0},{3,1},{4,6},{5,7},{6,4},{7,5},{8,10},{9,11},{10,... | collective-permute-start | bytes 393224 | tf_op jit(solution)/shard_map/ppermute | solution.py:210
  24.7 0.0 copy-done.2
  24.7 0.0 copy-done.1
  24.7 1.7 %near_scores.1.near_ref = f32[8,32]{1,0:T(8,128)S(1)} custom-call(bf16[8,16384]{1,0:T(8,128)(2,1)S(1)} %copy-done.2, bf16[8,3584]{1,0:T(8,128)(2,1)S(1)} %get-tuple-element.55.refs_0_.weights_ref, bf16[16,16384]{1,0:T(8,128)(2,1)S(1)} %copy-done.1, bf16[16,16384]{1,0:T(8,128)(2,1)S(1)} %collective-permute-done.1.refs_1_), custom_call_target="tpu_custom_call" | custom-call | tf_op jit(solution)/shard_map/near_scores/pallas_call | solution.py:264
  26.4 0.2 collective-permute-done.10.back_ref
  26.7 0.6 %near_sums.1 = (f32[1,16,2048]{2,1,0:T(8,128)S(1)}, f32[1,16,2048]{2,1,0:T(8,128)S(1)}) custom-call(bf16[384,2048]{1,0:T(8,128)(2,1)S(1)} %get-tuple-element.68.stack_ref, bf16[8,3584]{1,0:T(8,128)(2,1)S(1)} %get-tuple-element.55.refs_0_.weights_ref, bf16[8,3584]{1,0:T(8,128)(2,1)S(1)} %collective-permute-done.2.refs_1_, ...), custom_call_target="tpu_custom_call" | custom-call | tf_op jit(solution)/shard_map/near_sums/pallas_call | solution.py:269
  27.2 0.1 collective-permute-start.11
  27.3 1.3 %scores.1 = f32[8,64]{1,0:T(8,128)} custom-call(f32[8,32]{1,0:T(8,128)S(1)} %near_scores.1.near_ref, f32[96,64]{1,0:T(8,128)S(1)} %collective-permute-done.10.back_ref, bf16[8,3584]{1,0:T(8,128)(2,1)S(1)} %get-tuple-element.55.refs_0_.weights_ref), custom_call_target="tpu_custom_call" | custom-call | tf_op jit(solution)/shard_map/scores/pallas_call | solution.py:274
  28.6 0.9 %collective-permute-done.12 = f32[16,2048]{1,0:T(8,128)S(1)} collective-permute-done((f32[16,2048]{1,0:T(8,128)S(1)}, f32[16,2048]{1,0:T(8,128)S(1)}, u32[]{:S(2)}, u32[]{:S(2)}) %collective-permute-start.12) | collective-permute-done | bytes 131104 | tf_op jit(solution)/shard_map/ppermute | solution.py:210
  29.5 0.0 collective-permute-done.11
  29.5 0.7 %fusion = f32[16,2048]{1,0:T(8,128)} fusion(f32[16,2048]{1,0:T(8,128)S(1)} %collective-permute-done.12, f32[1,16,2048]{2,1,0:T(8,128)S(1)} %get-tuple-element.69, f32[1,16,2048]{2,1,0:T(8,128)S(1)} %collective-permute-done.11), kind=kLoop, calls=%fused_computation.1 | loop fusion | flops 98304 | bytes 524288 | tf_op jit(solution)/shard_map/div | solution.py:276
  (1 shorter events, 0.0 us)
Async XLA Ops:
  0.6 24.1 %copy-start.2 = (bf16[8,16384]{1,0:T(8,128)(2,1)S(1)}, bf16[8,16384]{1,0:T(8,128)(2,1)}, u32[]{:S(2)}) copy-start(bf16[8,16384]{1,0:T(8,128)(2,1)} %part_ref) | copy-start | bytes 786436
  0.6 5.2 %collective-permute-start.1 = (bf16[16,16384]{1,0:T(8,128)(2,1)}, bf16[16,16384]{1,0:T(8,128)(2,1)S(1)}, u32[]{:S(2)}, u32[]{:S(2)}) collective-permute-start(bf16[16,16384]{1,0:T(8,128)(2,1)} %refs_0_.3), channel_id=1, source_target_pairs={{0,1},{1,0},{2,3},{3,2},{4,5},{5,4},{6,7},{7,6},{8,9},{9,8},{10,11... | collective-permute-start | bytes 1572872 | tf_op jit(solution)/shard_map/ppermute | solution.py:210
  1.2 12.4 %collective-permute-start = (bf16[8,16384]{1,0:T(8,128)(2,1)}, bf16[8,16384]{1,0:T(8,128)(2,1)S(1)}, u32[]{:S(2)}, u32[]{:S(2)}) collective-permute-start(bf16[8,16384]{1,0:T(8,128)(2,1)} %part_ref), channel_id=1, source_target_pairs={{0,2},{1,3},{2,0},{3,1},{4,6},{5,7},{6,4},{7,5},{8,10},{9,11},{10,... | collective-permute-start | bytes 786440 | tf_op jit(solution)/shard_map/ppermute | solution.py:210
  5.9 9.9 %collective-permute-start.2 = (bf16[8,3584]{1,0:T(8,128)(2,1)}, bf16[8,3584]{1,0:T(8,128)(2,1)S(1)}, u32[]{:S(2)}, u32[]{:S(2)}) collective-permute-start(bf16[8,3584]{1,0:T(8,128)(2,1)} %get-tuple-element.47), channel_id=1, source_target_pairs={{0,28},{4,24},{8,20},{12,16},{16,12},{20,8},{24,4},{28,0},{1,29},{... | collective-permute-start | bytes 172040 | tf_op jit(solution)/shard_map/ppermute | solution.py:244
  10.4 6.5 %collective-permute-start.3 = (bf16[8,3584]{1,0:T(8,128)(2,1)}, bf16[8,3584]{1,0:T(8,128)(2,1)S(1)}, u32[]{:S(2)}, u32[]{:S(2)}) collective-permute-start(bf16[8,3584]{1,0:T(8,128)(2,1)} %get-tuple-element.48), channel_id=1, source_target_pairs={{0,24},{4,28},{8,16},{12,20},{16,8},{20,12},{24,0},{28,4},{1,25},{... | collective-permute-start | bytes 172040 | tf_op jit(solution)/shard_map/ppermute | solution.py:244
  10.7 10.2 %collective-permute-start.4 = (bf16[8,3584]{1,0:T(8,128)(2,1)}, bf16[8,3584]{1,0:T(8,128)(2,1)S(1)}, u32[]{:S(2)}, u32[]{:S(2)}) collective-permute-start(bf16[8,3584]{1,0:T(8,128)(2,1)} %get-tuple-element.49), channel_id=1, source_target_pairs={{0,20},{4,16},{8,28},{12,24},{16,4},{20,0},{24,12},{28,8},{1,21},{... | collective-permute-start | bytes 172040 | tf_op jit(solution)/shard_map/ppermute | solution.py:244
  11.4 9.5 %collective-permute-start.5 = (bf16[8,3584]{1,0:T(8,128)(2,1)}, bf16[8,3584]{1,0:T(8,128)(2,1)S(1)}, u32[]{:S(2)}, u32[]{:S(2)}) collective-permute-start(bf16[8,3584]{1,0:T(8,128)(2,1)} %get-tuple-element.50), channel_id=1, source_target_pairs={{0,16},{4,20},{8,24},{12,28},{16,0},{20,4},{24,8},{28,12},{1,17},{... | collective-permute-start | bytes 172040 | tf_op jit(solution)/shard_map/ppermute | solution.py:244
  13.6 7.4 %collective-permute-start.6 = (bf16[8,3584]{1,0:T(8,128)(2,1)}, bf16[8,3584]{1,0:T(8,128)(2,1)S(1)}, u32[]{:S(2)}, u32[]{:S(2)}) collective-permute-start(bf16[8,3584]{1,0:T(8,128)(2,1)} %get-tuple-element.51), channel_id=1, source_target_pairs={{0,12},{4,8},{8,4},{12,0},{16,28},{20,24},{24,20},{28,16},{1,13},{... | collective-permute-start | bytes 172040 | tf_op jit(solution)/shard_map/ppermute | solution.py:244
  15.7 5.7 %collective-permute-start.7 = (bf16[8,3584]{1,0:T(8,128)(2,1)}, bf16[8,3584]{1,0:T(8,128)(2,1)S(1)}, u32[]{:S(2)}, u32[]{:S(2)}) collective-permute-start(bf16[8,3584]{1,0:T(8,128)(2,1)} %get-tuple-element.52), channel_id=1, source_target_pairs={{0,8},{4,12},{8,0},{12,4},{16,24},{20,28},{24,16},{28,20},{1,9},{5... | collective-permute-start | bytes 172040 | tf_op jit(solution)/shard_map/ppermute | solution.py:244
  17.0 4.5 %collective-permute-start.8 = (bf16[8,3584]{1,0:T(8,128)(2,1)}, bf16[8,3584]{1,0:T(8,128)(2,1)S(1)}, u32[]{:S(2)}, u32[]{:S(2)}) collective-permute-start(bf16[8,3584]{1,0:T(8,128)(2,1)} %get-tuple-element.53), channel_id=1, source_target_pairs={{0,4},{4,0},{8,12},{12,8},{16,20},{20,16},{24,28},{28,24},{1,5},{5... | collective-permute-start | bytes 172040 | tf_op jit(solution)/shard_map/ppermute | solution.py:244
  17.4 1.0 %copy-start = (bf16[16,16384]{1,0:T(8,128)(2,1)S(1)}, bf16[16,16384]{1,0:T(8,128)(2,1)}, u32[]{:S(2)}) copy-start(bf16[16,16384]{1,0:T(8,128)(2,1)} %refs_0_.3) | copy-start | bytes 1572868
  18.5 0.8 %copy-start.3 = (bf16[8,3584]{1,0:T(8,128)(2,1)S(1)}, bf16[8,3584]{1,0:T(8,128)(2,1)}, u32[]{:S(2)}) copy-start(bf16[8,3584]{1,0:T(8,128)(2,1)} %get-tuple-element.45.packed_ref) | copy-start | bytes 172036
  19.3 5.4 %copy-start.1 = (bf16[16,16384]{1,0:T(8,128)(2,1)S(1)}, bf16[16,16384]{1,0:T(8,128)(2,1)}, u32[]{:S(2)}) copy-start(bf16[16,16384]{1,0:T(8,128)(2,1)} %refs_0_.3) | copy-start | bytes 1572868
  22.4 1.4 %collective-permute-start.9 = (f32[1,16,2048]{2,1,0:T(8,128)S(1)}, f32[1,16,2048]{2,1,0:T(8,128)S(1)}, u32[]{:S(2)}, u32[]{:S(2)}) collective-permute-start(f32[1,16,2048]{2,1,0:T(8,128)S(1)} %get-tuple-element.64), channel_id=1, source_target_pairs={{0,1},{1,0},{2,3},{3,2},{4,5},{5,4},{6,7},{7,6},{8,9},{9,8},{10,11... | collective-permute-start | bytes 393224 | tf_op jit(solution)/shard_map/ppermute | solution.py:210
  22.5 4.2 %collective-permute-start.10 = (f32[96,64]{1,0:T(8,128)S(1)}, f32[96,64]{1,0:T(8,128)S(1)}, u32[]{:S(2)}, u32[]{:S(2)}) collective-permute-start(f32[96,64]{1,0:T(8,128)S(1)} %get-tuple-element.66), channel_id=1, source_target_pairs={{0,2},{1,3},{2,0},{3,1},{4,6},{5,7},{6,4},{7,5},{8,10},{9,11},{10,... | collective-permute-start | bytes 73736 | tf_op jit(solution)/shard_map/ppermute | solution.py:210
  23.9 5.6 %collective-permute-start.12 = (f32[16,2048]{1,0:T(8,128)S(1)}, f32[16,2048]{1,0:T(8,128)S(1)}, u32[]{:S(2)}, u32[]{:S(2)}) collective-permute-start(f32[16,2048]{1,0:T(8,128)S(1)} %add_bitcast_fusion), channel_id=1, source_target_pairs={{0,2},{1,3},{2,0},{3,1},{4,6},{5,7},{6,4},{7,5},{8,10},{9,11},{10,... | collective-permute-start | bytes 393224 | tf_op jit(solution)/shard_map/ppermute | solution.py:210
  27.2 2.3 %collective-permute-start.11 = (f32[1,16,2048]{2,1,0:T(8,128)S(1)}, f32[1,16,2048]{2,1,0:T(8,128)S(1)}, u32[]{:S(2)}, u32[]{:S(2)}) collective-permute-start(f32[1,16,2048]{2,1,0:T(8,128)S(1)} %get-tuple-element.70), channel_id=1, source_target_pairs={{0,1},{1,0},{2,3},{3,2},{4,5},{5,4},{6,7},{7,6},{8,9},{9,8},{10,11... | collective-permute-start | bytes 393224 | tf_op jit(solution)/shard_map/ppermute | solution.py:210

commit v5 on v4

--- a/solution.py
+++ b/solution.py
@@ -55,29 +55,13 @@
     return x
 
 
-def pack_kernel(part_hbm, pose_hbm, mask_hbm, *refs):
-    slots, (pose_ref, mask_ref, sems) = refs[:-3], refs[-3:]
-    dom = len(slots)
-    cols = part_hbm.shape[1] // dom
+def pack_kernel(part_ref, pose_ref, mask_ref, *slots):
+    cols = part_ref.shape[1] // len(slots)
     d, me, groups = lax.axis_index("dom"), lax.axis_index("cls"), lax.axis_size("cls")
     k = pose_ref.shape[2]
     half = k // 2
-    small = [
-        pltpu.make_async_copy(pose_hbm, pose_ref, sems.at[dom]),
-        pltpu.make_async_copy(mask_hbm, mask_ref, sems.at[dom + 1]),
-    ]
-    large = [
-        pltpu.make_async_copy(
-            part_hbm.at[:, pl.ds(pl.multiple_of((d ^ s) * cols, cols), cols)],
-            slots[s].at[:, pl.ds(0, cols)],
-            sems.at[s],
-        )
-        for s in range(dom)
-    ]
-    for copy in small + large:
-        copy.start()
-    for copy in small:
-        copy.wait()
+    for s, slot in enumerate(slots):
+        slot[:, :cols] = part_ref[:, pl.ds(pl.multiple_of((d ^ s) * cols, cols), cols)]
     mask = mask_ref[...]
     for i in range(COARSE):
         fine = [pose_ref[:, FINE * i + j, :] * mask for j in range(FINE)]
@@ -87,8 +71,6 @@
         wide = w.shape[1]
         for slot in slots:
             slot[:, cols + i * wide : cols + (i + 1) * wide] = w
-    for copy in large:
-        copy.wait()
 
 
 def rows_of(got, at):
@@ -188,19 +170,16 @@
     dom, groups = lax.axis_size("dom"), lax.axis_size("cls")
     cols = length // dom
     last = groups // 2
-    hbm = pl.BlockSpec(memory_space=pl.ANY)
     vmem = pl.BlockSpec(memory_space=pltpu.VMEM)
 
-    def call(kernel, name, outs, ins, scratch=(), limit=VMEM_BYTES, cost=None):
+    def call(kernel, name, outs, ins, limit=VMEM_BYTES):
         return pl.pallas_call(
             kernel,
             out_shape=[jax.ShapeDtypeStruct(*o) for o in outs],
             in_specs=ins,
             out_specs=[vmem] * len(outs),
-            scratch_shapes=list(scratch),
             compiler_params=pltpu.CompilerParams(vmem_limit_bytes=limit),
             name=name,
-            cost_estimate=cost,
         )
 
     def after(x, other):
@@ -229,13 +208,8 @@
         pack_kernel,
         "pack",
         [((n, cols + ROT * k), bf16)] * dom,
-        [hbm] * 3,
-        [
-            pltpu.VMEM(pose_weights.shape, jnp.int32),
-            pltpu.VMEM(class_mask.shape, jnp.int32),
-            pltpu.SemaphoreType.DMA((dom + 2,)),
-        ],
-        VMEM_MOST,
+        [vmem] * 3,
+        limit=VMEM_MOST,
     )(particles, pose_weights, class_mask)
     packed = after(packed, near)
     got = [packed[0]]

time: 30.4 us -> 30.4 us (level)
  no operation moved by 1% of the time
where the time goes in v5:
time: 30.4 us; the launch traced here: 30.2 us
  starting transfers between devices  15.8 us (52%)
  Pallas kernels  8.19 us (27%)
  waiting for transfers between devices  2.92 us (10%)
  local copies, waits for them, and re-layouts  1.87 us (6%)
  other arithmetic  0.7 us (2%)
  between operations  0.7 us (2%)
    ppermute x7, starting transfers between devices, on_device(): got.append(lax.ppermute(x, 'dom', [(d, d ^ s) for d in range(dom)]))  11.1 us
    ppermute x6, starting transfers between devices, across(): return lax.ppermute(x, 'cls', [(c, c ^ bit) for c in range(groups)])  4.65 us
    pallas_call x1, Pallas kernels, on_device(): call(pack_kernel, 'pack', [((n, cols + ROT * k), bf16)] * dom, [vmem] * 3...  2.11 us
    ppermute x6, waiting for transfers between devices, across(): return lax.ppermute(x, 'cls', [(c, c ^ bit) for c in range(groups)])  1.88 us
    unnamed x8, local copies, waits for them, and re-layouts  1.87 us
    pallas_call x1, Pallas kernels, on_device(): call(near_scores_kernel, 'near_scores', [((n, k // 2), f32)], [vmem] * (2...  1.75 us
    pallas_call x1, Pallas kernels, on_device(): call(guest_kernel, 'guest_scores', [((n * ROT // PAIR, PAIR * k // 2), f3...  1.55 us
    pallas_call x1, Pallas kernels, on_device(): call(scores_kernel, 'scores', [((n, k), f32)], [vmem] * 3)  1.29 us
  transfers between devices with their start and end apart: 13, of which 5 were waited for; matrix products, arithmetic and copies ran while one was open for 0% of the time, Pallas kernels for 24%

profile of v5, /device:TPU:0, one launch (start us, length us, event | category | flops | bytes accessed | tf_op | source)
XLA Modules:
  0.0 30.2 jit_solution(9743006875719370454)
XLA Ops:
  0.6 0.0 copy-start.2
  0.6 0.5 %collective-permute-start.1 = (bf16[16,16384]{1,0:T(8,128)(2,1)}, bf16[16,16384]{1,0:T(8,128)(2,1)S(1)}, u32[]{:S(2)}, u32[]{:S(2)}) collective-permute-start(bf16[16,16384]{1,0:T(8,128)(2,1)} %refs_0_.3), channel_id=1, source_target_pairs={{0,1},{1,0},{2,3},{3,2},{4,5},{5,4},{6,7},{7,6},{8,9},{9,8},{10,11... | collective-permute-start | bytes 1572872 | tf_op jit(solution)/shard_map/ppermute | solution.py:189
  1.2 2.6 %collective-permute-start = (bf16[8,16384]{1,0:T(8,128)(2,1)}, bf16[8,16384]{1,0:T(8,128)(2,1)S(1)}, u32[]{:S(2)}, u32[]{:S(2)}) collective-permute-start(bf16[8,16384]{1,0:T(8,128)(2,1)} %part_ref.2), channel_id=1, source_target_pairs={{0,2},{1,3},{2,0},{3,1},{4,6},{5,7},{6,4},{7,5},{8,10},{9,11},{10,... | collective-permute-start | bytes 786440 | tf_op jit(solution)/shard_map/ppermute | solution.py:189
  3.8 2.1 %pack.1 = (bf16[8,3584]{1,0:T(8,128)(2,1)}, bf16[8,3584]{1,0:T(8,128)(2,1)}, bf16[8,3584]{1,0:T(8,128)(2,1)}, bf16[8,3584]{1,0:T(8,128)(2,1)}, bf16[8,3584]{1,0:...) custom-call(bf16[8,16384]{1,0:T(8,128)(2,1)} %part_ref.2, ...), custom_call_target="tpu_custom_call" | custom-call | tf_op jit(solution)/shard_map/pack/pallas_call | solution.py:207
  5.9 0.0 collective-permute-done.1.refs_1_
  5.9 4.6 %collective-permute-start.2 = (bf16[8,3584]{1,0:T(8,128)(2,1)}, bf16[8,3584]{1,0:T(8,128)(2,1)S(1)}, u32[]{:S(2)}, u32[]{:S(2)}) collective-permute-start(bf16[8,3584]{1,0:T(8,128)(2,1)} %get-tuple-element.47), channel_id=1, source_target_pairs={{0,28},{4,24},{8,20},{12,16},{16,12},{20,8},{24,4},{28,0},{1,29},{... | collective-permute-start | bytes 172040 | tf_op jit(solution)/shard_map/ppermute | solution.py:218
  10.4 0.2 collective-permute-start.3
  10.7 0.8 %collective-permute-start.4 = (bf16[8,3584]{1,0:T(8,128)(2,1)}, bf16[8,3584]{1,0:T(8,128)(2,1)S(1)}, u32[]{:S(2)}, u32[]{:S(2)}) collective-permute-start(bf16[8,3584]{1,0:T(8,128)(2,1)} %get-tuple-element.49), channel_id=1, source_target_pairs={{0,20},{4,16},{8,28},{12,24},{16,4},{20,0},{24,12},{28,8},{1,21},{... | collective-permute-start | bytes 172040 | tf_op jit(solution)/shard_map/ppermute | solution.py:218
  11.4 2.1 %collective-permute-start.5 = (bf16[8,3584]{1,0:T(8,128)(2,1)}, bf16[8,3584]{1,0:T(8,128)(2,1)S(1)}, u32[]{:S(2)}, u32[]{:S(2)}) collective-permute-start(bf16[8,3584]{1,0:T(8,128)(2,1)} %get-tuple-element.50), channel_id=1, source_target_pairs={{0,16},{4,20},{8,24},{12,28},{16,0},{20,4},{24,8},{28,12},{1,17},{... | collective-permute-start | bytes 172040 | tf_op jit(solution)/shard_map/ppermute | solution.py:218
  13.6 0.0 collective-permute-done.part_ref
  13.6 2.2 %collective-permute-start.6 = (bf16[8,3584]{1,0:T(8,128)(2,1)}, bf16[8,3584]{1,0:T(8,128)(2,1)S(1)}, u32[]{:S(2)}, u32[]{:S(2)}) collective-permute-start(bf16[8,3584]{1,0:T(8,128)(2,1)} %get-tuple-element.51), channel_id=1, source_target_pairs={{0,12},{4,8},{8,4},{12,0},{16,28},{20,24},{24,20},{28,16},{1,13},{... | collective-permute-start | bytes 172040 | tf_op jit(solution)/shard_map/ppermute | solution.py:218
  15.7 0.0 collective-permute-done.2.refs_1_
  15.7 0.8 %collective-permute-start.7 = (bf16[8,3584]{1,0:T(8,128)(2,1)}, bf16[8,3584]{1,0:T(8,128)(2,1)S(1)}, u32[]{:S(2)}, u32[]{:S(2)}) collective-permute-start(bf16[8,3584]{1,0:T(8,128)(2,1)} %get-tuple-element.52), channel_id=1, source_target_pairs={{0,8},{4,12},{8,0},{12,4},{16,24},{20,28},{24,16},{28,20},{1,9},{5... | collective-permute-start | bytes 172040 | tf_op jit(solution)/shard_map/ppermute | solution.py:218
  16.5 0.4 %collective-permute-done.3.refs_2_ = bf16[8,3584]{1,0:T(8,128)(2,1)S(1)} collective-permute-done((bf16[8,3584]{1,0:T(8,128)(2,1)}, bf16[8,3584]{1,0:T(8,128)(2,1)S(1)}, u32[]{:S(2)}, u32[]{:S(2)}) %collective-permute-start.3) | collective-permute-done | bytes 57376 | tf_op jit(solution)/shard_map/ppermute | solution.py:218
  17.0 0.5 %collective-permute-start.8 = (bf16[8,3584]{1,0:T(8,128)(2,1)}, bf16[8,3584]{1,0:T(8,128)(2,1)S(1)}, u32[]{:S(2)}, u32[]{:S(2)}) collective-permute-start(bf16[8,3584]{1,0:T(8,128)(2,1)} %get-tuple-element.53), channel_id=1, source_target_pairs={{0,4},{4,0},{8,12},{12,8},{16,20},{20,16},{24,28},{28,24},{1,5},{5... | collective-permute-start | bytes 172040 | tf_op jit(solution)/shard_map/ppermute | solution.py:218
  17.4 0.0 copy-start
  17.5 1.0 %copy-done = bf16[16,16384]{1,0:T(8,128)(2,1)S(1)} copy-done((bf16[16,16384]{1,0:T(8,128)(2,1)S(1)}, bf16[16,16384]{1,0:T(8,128)(2,1)}, u32[]{:S(2)}) %copy-start) | copy-done | bytes 524312
  18.5 0.0 copy-start.3
  18.5 0.8 %copy-done.3 = bf16[8,3584]{1,0:T(8,128)(2,1)S(1)} copy-done((bf16[8,3584]{1,0:T(8,128)(2,1)S(1)}, bf16[8,3584]{1,0:T(8,128)(2,1)}, u32[]{:S(2)}) %copy-start.3) | copy-done | bytes 57368
  19.3 0.0 copy-start.1
  19.3 1.6 %guest_scores.1 = (f32[96,64]{1,0:T(8,128)S(1)}, bf16[8,3584]{1,0:T(8,128)(2,1)S(1)}) custom-call(bf16[8,16384]{1,0:T(8,128)(2,1)S(1)} %collective-permute-done.part_ref, bf16[8,3584]{1,0:T(8,128)(2,1)S(1)} %copy-done.3, bf16[16,16384]{1,0:T(8,128)(2,1)S(1)} %copy-done, bf16[16,16384]{1,0:T(8,128)(2,1)S(1)} %collective-permute-done.1.refs_1_), custom_call_target="tpu_custom_call" | custom-call | tf_op jit(solution)/shard_map/guest_scores/pallas_call | solution.py:221
  20.9 0.0 collective-permute-done.4.refs_3_
  20.9 0.0 collective-permute-done.5.refs_4_
  20.9 0.0 collective-permute-done.6.refs_5_
  21.0 0.5 %collective-permute-done.7.refs_6_ = bf16[8,3584]{1,0:T(8,128)(2,1)S(1)} collective-permute-done((bf16[8,3584]{1,0:T(8,128)(2,1)}, bf16[8,3584]{1,0:T(8,128)(2,1)S(1)}, u32[]{:S(2)}, u32[]{:S(2)}) %collective-permute-start.7) | collective-permute-done | bytes 57376 | tf_op jit(solution)/shard_map/ppermute | solution.py:218
  21.5 0.0 collective-permute-done.8.refs_7_
  21.5 0.9 %far_sums.1 = (bf16[384,2048]{1,0:T(8,128)(2,1)S(1)}, f32[1,16,2048]{2,1,0:T(8,128)S(1)}, f32[1,16,2048]{2,1,0:T(8,128)S(1)}) custom-call(bf16[8,3584]{1,0:T(8,128)(2,1)S(1)} %get-tuple-element.55.refs_0_.weights_ref, bf16[8,3584]{1,0:T(8,128)(2,1)S(1)} %collective-permute-done.2.refs_1_, bf16[8,3584]{1,0:T(8,128)(2,1)S(1)} %collective-permute-done.3.refs_2_, ...), custom_call_target="tpu_custom_call" | custom-call | tf_op jit(solution)/shard_map/far_sums/pallas_call | solution.py:229
  22.4 0.1 collective-permute-start.9
  22.5 0.6 %collective-permute-start.10 = (f32[96,64]{1,0:T(8,128)S(1)}, f32[96,64]{1,0:T(8,128)S(1)}, u32[]{:S(2)}, u32[]{:S(2)}) collective-permute-start(f32[96,64]{1,0:T(8,128)S(1)} %get-tuple-element.66), channel_id=1, source_target_pairs={{0,2},{1,3},{2,0},{3,1},{4,6},{5,7},{6,4},{7,5},{8,10},{9,11},{10,... | collective-permute-start | bytes 73736 | tf_op jit(solution)/shard_map/ppermute | solution.py:189
  23.1 0.8 %collective-permute-done.9 = f32[1,16,2048]{2,1,0:T(8,128)S(1)} collective-permute-done((f32[1,16,2048]{2,1,0:T(8,128)S(1)}, f32[1,16,2048]{2,1,0:T(8,128)S(1)}, u32[]{:S(2)}, u32[]{:S(2)}) %collective-permute-start.9) | collective-permute-done | bytes 131104 | tf_op jit(solution)/shard_map/ppermute | solution.py:189
  23.9 0.8 %collective-permute-start.12 = (f32[16,2048]{1,0:T(8,128)S(1)}, f32[16,2048]{1,0:T(8,128)S(1)}, u32[]{:S(2)}, u32[]{:S(2)}) collective-permute-start(f32[16,2048]{1,0:T(8,128)S(1)} %add_bitcast_fusion), channel_id=1, source_target_pairs={{0,2},{1,3},{2,0},{3,1},{4,6},{5,7},{6,4},{7,5},{8,10},{9,11},{10,... | collective-permute-start | bytes 393224 | tf_op jit(solution)/shard_map/ppermute | solution.py:189
  24.7 0.0 copy-done.2
  24.7 0.0 copy-done.1
  24.7 1.7 %near_scores.1.near_ref = f32[8,32]{1,0:T(8,128)S(1)} custom-call(bf16[8,16384]{1,0:T(8,128)(2,1)S(1)} %copy-done.2, bf16[8,3584]{1,0:T(8,128)(2,1)S(1)} %get-tuple-element.55.refs_0_.weights_ref, bf16[16,16384]{1,0:T(8,128)(2,1)S(1)} %copy-done.1, bf16[16,16384]{1,0:T(8,128)(2,1)S(1)} %collective-permute-done.1.refs_1_), custom_call_target="tpu_custom_call" | custom-call | tf_op jit(solution)/shard_map/near_scores/pallas_call | solution.py:238
  26.4 0.2 collective-permute-done.10.back_ref
  26.7 0.6 %near_sums.1 = (f32[1,16,2048]{2,1,0:T(8,128)S(1)}, f32[1,16,2048]{2,1,0:T(8,128)S(1)}) custom-call(bf16[384,2048]{1,0:T(8,128)(2,1)S(1)} %get-tuple-element.68.stack_ref, bf16[8,3584]{1,0:T(8,128)(2,1)S(1)} %get-tuple-element.55.refs_0_.weights_ref, bf16[8,3584]{1,0:T(8,128)(2,1)S(1)} %collective-permute-done.2.refs_1_, ...), custom_call_target="tpu_custom_call" | custom-call | tf_op jit(solution)/shard_map/near_sums/pallas_call | solution.py:243
  27.2 0.1 collective-permute-start.11
  27.3 1.3 %scores.1 = f32[8,64]{1,0:T(8,128)} custom-call(f32[8,32]{1,0:T(8,128)S(1)} %near_scores.1.near_ref, f32[96,64]{1,0:T(8,128)S(1)} %collective-permute-done.10.back_ref, bf16[8,3584]{1,0:T(8,128)(2,1)S(1)} %get-tuple-element.55.refs_0_.weights_ref), custom_call_target="tpu_custom_call" | custom-call | tf_op jit(solution)/shard_map/scores/pallas_call | solution.py:248
  28.6 0.9 %collective-permute-done.12 = f32[16,2048]{1,0:T(8,128)S(1)} collective-permute-done((f32[16,2048]{1,0:T(8,128)S(1)}, f32[16,2048]{1,0:T(8,128)S(1)}, u32[]{:S(2)}, u32[]{:S(2)}) %collective-permute-start.12) | collective-permute-done | bytes 131104 | tf_op jit(solution)/shard_map/ppermute | solution.py:189
  29.5 0.0 collective-permute-done.11
  29.5 0.7 %fusion = f32[16,2048]{1,0:T(8,128)} fusion(f32[16,2048]{1,0:T(8,128)S(1)} %collective-permute-done.12, f32[1,16,2048]{2,1,0:T(8,128)S(1)} %get-tuple-element.69, f32[1,16,2048]{2,1,0:T(8,128)S(1)} %collective-permute-done.11), kind=kLoop, calls=%fused_computation.1 | loop fusion | flops 98304 | bytes 524288 | tf_op jit(solution)/shard_map/div | solution.py:250
  (1 shorter events, 0.0 us)
Async XLA Ops:
  0.6 24.1 %copy-start.2 = (bf16[8,16384]{1,0:T(8,128)(2,1)S(1)}, bf16[8,16384]{1,0:T(8,128)(2,1)}, u32[]{:S(2)}) copy-start(bf16[8,16384]{1,0:T(8,128)(2,1)} %part_ref.2) | copy-start | bytes 786436
  0.6 5.2 %collective-permute-start.1 = (bf16[16,16384]{1,0:T(8,128)(2,1)}, bf16[16,16384]{1,0:T(8,128)(2,1)S(1)}, u32[]{:S(2)}, u32[]{:S(2)}) collective-permute-start(bf16[16,16384]{1,0:T(8,128)(2,1)} %refs_0_.3), channel_id=1, source_target_pairs={{0,1},{1,0},{2,3},{3,2},{4,5},{5,4},{6,7},{7,6},{8,9},{9,8},{10,11... | collective-permute-start | bytes 1572872 | tf_op jit(solution)/shard_map/ppermute | solution.py:189
  1.2 12.4 %collective-permute-start = (bf16[8,16384]{1,0:T(8,128)(2,1)}, bf16[8,16384]{1,0:T(8,128)(2,1)S(1)}, u32[]{:S(2)}, u32[]{:S(2)}) collective-permute-start(bf16[8,16384]{1,0:T(8,128)(2,1)} %part_ref.2), channel_id=1, source_target_pairs={{0,2},{1,3},{2,0},{3,1},{4,6},{5,7},{6,4},{7,5},{8,10},{9,11},{10,... | collective-permute-start | bytes 786440 | tf_op jit(solution)/shard_map/ppermute | solution.py:189
  5.9 9.9 %collective-permute-start.2 = (bf16[8,3584]{1,0:T(8,128)(2,1)}, bf16[8,3584]{1,0:T(8,128)(2,1)S(1)}, u32[]{:S(2)}, u32[]{:S(2)}) collective-permute-start(bf16[8,3584]{1,0:T(8,128)(2,1)} %get-tuple-element.47), channel_id=1, source_target_pairs={{0,28},{4,24},{8,20},{12,16},{16,12},{20,8},{24,4},{28,0},{1,29},{... | collective-permute-start | bytes 172040 | tf_op jit(solution)/shard_map/ppermute | solution.py:218
  10.4 6.5 %collective-permute-start.3 = (bf16[8,3584]{1,0:T(8,128)(2,1)}, bf16[8,3584]{1,0:T(8,128)(2,1)S(1)}, u32[]{:S(2)}, u32[]{:S(2)}) collective-permute-start(bf16[8,3584]{1,0:T(8,128)(2,1)} %get-tuple-element.48), channel_id=1, source_target_pairs={{0,24},{4,28},{8,16},{12,20},{16,8},{20,12},{24,0},{28,4},{1,25},{... | collective-permute-start | bytes 172040 | tf_op jit(solution)/shard_map/ppermute | solution.py:218
  10.7 10.2 %collective-permute-start.4 = (bf16[8,3584]{1,0:T(8,128)(2,1)}, bf16[8,3584]{1,0:T(8,128)(2,1)S(1)}, u32[]{:S(2)}, u32[]{:S(2)}) collective-permute-start(bf16[8,3584]{1,0:T(8,128)(2,1)} %get-tuple-element.49), channel_id=1, source_target_pairs={{0,20},{4,16},{8,28},{12,24},{16,4},{20,0},{24,12},{28,8},{1,21},{... | collective-permute-start | bytes 172040 | tf_op jit(solution)/shard_map/ppermute | solution.py:218
  11.4 9.5 %collective-permute-start.5 = (bf16[8,3584]{1,0:T(8,128)(2,1)}, bf16[8,3584]{1,0:T(8,128)(2,1)S(1)}, u32[]{:S(2)}, u32[]{:S(2)}) collective-permute-start(bf16[8,3584]{1,0:T(8,128)(2,1)} %get-tuple-element.50), channel_id=1, source_target_pairs={{0,16},{4,20},{8,24},{12,28},{16,0},{20,4},{24,8},{28,12},{1,17},{... | collective-permute-start | bytes 172040 | tf_op jit(solution)/shard_map/ppermute | solution.py:218
  13.6 7.4 %collective-permute-start.6 = (bf16[8,3584]{1,0:T(8,128)(2,1)}, bf16[8,3584]{1,0:T(8,128)(2,1)S(1)}, u32[]{:S(2)}, u32[]{:S(2)}) collective-permute-start(bf16[8,3584]{1,0:T(8,128)(2,1)} %get-tuple-element.51), channel_id=1, source_target_pairs={{0,12},{4,8},{8,4},{12,0},{16,28},{20,24},{24,20},{28,16},{1,13},{... | collective-permute-start | bytes 172040 | tf_op jit(solution)/shard_map/ppermute | solution.py:218
  15.7 5.7 %collective-permute-start.7 = (bf16[8,3584]{1,0:T(8,128)(2,1)}, bf16[8,3584]{1,0:T(8,128)(2,1)S(1)}, u32[]{:S(2)}, u32[]{:S(2)}) collective-permute-start(bf16[8,3584]{1,0:T(8,128)(2,1)} %get-tuple-element.52), channel_id=1, source_target_pairs={{0,8},{4,12},{8,0},{12,4},{16,24},{20,28},{24,16},{28,20},{1,9},{5... | collective-permute-start | bytes 172040 | tf_op jit(solution)/shard_map/ppermute | solution.py:218
  17.0 4.5 %collective-permute-start.8 = (bf16[8,3584]{1,0:T(8,128)(2,1)}, bf16[8,3584]{1,0:T(8,128)(2,1)S(1)}, u32[]{:S(2)}, u32[]{:S(2)}) collective-permute-start(bf16[8,3584]{1,0:T(8,128)(2,1)} %get-tuple-element.53), channel_id=1, source_target_pairs={{0,4},{4,0},{8,12},{12,8},{16,20},{20,16},{24,28},{28,24},{1,5},{5... | collective-permute-start | bytes 172040 | tf_op jit(solution)/shard_map/ppermute | solution.py:218
  17.4 1.0 %copy-start = (bf16[16,16384]{1,0:T(8,128)(2,1)S(1)}, bf16[16,16384]{1,0:T(8,128)(2,1)}, u32[]{:S(2)}) copy-start(bf16[16,16384]{1,0:T(8,128)(2,1)} %refs_0_.3) | copy-start | bytes 1572868
  18.5 0.8 %copy-start.3 = (bf16[8,3584]{1,0:T(8,128)(2,1)S(1)}, bf16[8,3584]{1,0:T(8,128)(2,1)}, u32[]{:S(2)}) copy-start(bf16[8,3584]{1,0:T(8,128)(2,1)} %get-tuple-element.45.packed_ref) | copy-start | bytes 172036
  19.3 5.4 %copy-start.1 = (bf16[16,16384]{1,0:T(8,128)(2,1)S(1)}, bf16[16,16384]{1,0:T(8,128)(2,1)}, u32[]{:S(2)}) copy-start(bf16[16,16384]{1,0:T(8,128)(2,1)} %refs_0_.3) | copy-start | bytes 1572868
  22.4 1.4 %collective-permute-start.9 = (f32[1,16,2048]{2,1,0:T(8,128)S(1)}, f32[1,16,2048]{2,1,0:T(8,128)S(1)}, u32[]{:S(2)}, u32[]{:S(2)}) collective-permute-start(f32[1,16,2048]{2,1,0:T(8,128)S(1)} %get-tuple-element.64), channel_id=1, source_target_pairs={{0,1},{1,0},{2,3},{3,2},{4,5},{5,4},{6,7},{7,6},{8,9},{9,8},{10,11... | collective-permute-start | bytes 393224 | tf_op jit(solution)/shard_map/ppermute | solution.py:189
  22.5 4.2 %collective-permute-start.10 = (f32[96,64]{1,0:T(8,128)S(1)}, f32[96,64]{1,0:T(8,128)S(1)}, u32[]{:S(2)}, u32[]{:S(2)}) collective-permute-start(f32[96,64]{1,0:T(8,128)S(1)} %get-tuple-element.66), channel_id=1, source_target_pairs={{0,2},{1,3},{2,0},{3,1},{4,6},{5,7},{6,4},{7,5},{8,10},{9,11},{10,... | collective-permute-start | bytes 73736 | tf_op jit(solution)/shard_map/ppermute | solution.py:189
  23.9 5.6 %collective-permute-start.12 = (f32[16,2048]{1,0:T(8,128)S(1)}, f32[16,2048]{1,0:T(8,128)S(1)}, u32[]{:S(2)}, u32[]{:S(2)}) collective-permute-start(f32[16,2048]{1,0:T(8,128)S(1)} %add_bitcast_fusion), channel_id=1, source_target_pairs={{0,2},{1,3},{2,0},{3,1},{4,6},{5,7},{6,4},{7,5},{8,10},{9,11},{10,... | collective-permute-start | bytes 393224 | tf_op jit(solution)/shard_map/ppermute | solution.py:189
  27.2 2.3 %collective-permute-start.11 = (f32[1,16,2048]{2,1,0:T(8,128)S(1)}, f32[1,16,2048]{2,1,0:T(8,128)S(1)}, u32[]{:S(2)}, u32[]{:S(2)}) collective-permute-start(f32[1,16,2048]{2,1,0:T(8,128)S(1)} %get-tuple-element.70), channel_id=1, source_target_pairs={{0,1},{1,0},{2,3},{3,2},{4,5},{5,4},{6,7},{7,6},{8,9},{9,8},{10,11... | collective-permute-start | bytes 393224 | tf_op jit(solution)/shard_map/ppermute | solution.py:189

commit v6 on v5

--- a/solution.py
+++ b/solution.py
@@ -77,17 +77,25 @@
     return jnp.concatenate([g[:, at].astype(f32) for g in got], axis=0)
 
 
-def half_sums(got, stack, half):
+def products(got, stack, half):
     cols = stack.shape[1]
     wide = (got[0].shape[1] - cols) // COARSE // 2
-    k = wide // FINE
     at = [slice(cols + (2 * i + half) * wide, cols + (2 * i + half + 1) * wide) for i in range(COARSE)]
     w = jnp.concatenate([rows_of(got, a).astype(bf16) for a in at], axis=0)
-    t = lax.dot_general(w, stack, (((0,), (0,)), ((), ())), preferred_element_type=f32)
+    return lax.dot_general(w, stack, (((0,), (0,)), ((), ())), preferred_element_type=f32)
+
+
+def turned_back(t):
+    k = t.shape[0] // FINE
     total = t[:k]
     for j in range(1, FINE):
         total = total + turn(t[j * k : (j + 1) * k], -STEP * j)
     return total
+
+
+def rotated(got, cols):
+    part = rows_of(got, slice(0, cols))
+    return jnp.concatenate([turn(part, -STEP * FINE * i).astype(bf16) for i in range(COARSE)], axis=0)
 
 
 def put_pairs(total, keep_ref, send_ref):
@@ -98,18 +106,24 @@
             send_ref[m] = total[(2 * m + 1) * per : (2 * m + 2) * per]
 
 
-def far_sums_kernel(count, *refs):
-    got, (stack_ref, *outs) = refs[:count], refs[-3:]
-    cols = stack_ref.shape[1]
-    part = rows_of(got, slice(0, cols))
-    stack = jnp.concatenate([turn(part, -STEP * FINE * i).astype(bf16) for i in range(COARSE)], axis=0)
+def early_sums_kernel(*refs):
+    *got, stack_ref, out_ref = refs
+    stack = rotated(got, stack_ref.shape[1])
     stack_ref[...] = stack
-    put_pairs(half_sums(got, stack, 1), *outs)
-
-
-def near_sums_kernel(count, stack_ref, *refs):
-    got, (keep_ref, send_ref) = refs[:count], refs[-2:]
-    put_pairs(half_sums(got, stack_ref[...], 0), keep_ref, send_ref)
+    out_ref[...] = products(got, stack, 1)
+
+
+def far_sums_kernel(early_ref, *refs):
+    *got, stack_ref, keep_ref, send_ref = refs
+    stack = rotated(got, stack_ref.shape[1])
+    stack_ref[...] = stack
+    put_pairs(turned_back(early_ref[...] + products(got, stack, 1)), keep_ref, send_ref)
+
+
+def near_sums_kernel(count, early_ref, late_ref, *refs):
+    *got, keep_ref, send_ref = refs
+    t = products(got[:count], early_ref[...], 0) + products(got[count:], late_ref[...], 0)
+    put_pairs(turned_back(t), keep_ref, send_ref)
 
 
 def correlate(part_ref, blocks):
@@ -224,25 +238,32 @@
         [((n * ROT // PAIR, PAIR * k // 2), f32), (packed[0].shape, bf16)],
         [vmem] * (2 + last),
     )(guests, packed[0], *near)
-    got = after(got, back)
     send_shape = (max(last // 2, 1), per, cols)
-    stack, keep, send = call(
-        functools.partial(far_sums_kernel, dom),
+    first = dom // 2
+    early_stack, early = call(
+        early_sums_kernel,
+        "early_sums",
+        [((n * first * COARSE, cols), bf16), ((FINE * k // 2, cols), f32)],
+        [vmem] * first,
+    )(*got[:first])
+    got = got[:first] + after(got[first:], early)
+    late_stack, keep, send = call(
+        far_sums_kernel,
         "far_sums",
-        [((n * dom * COARSE, cols), bf16), (send_shape, f32), (send_shape, f32)],
-        [vmem] * dom,
-    )(*got)
+        [((n * (dom - first) * COARSE, cols), bf16), (send_shape, f32), (send_shape, f32)],
+        [vmem] * (1 + dom - first),
+    )(early, *got[first:])
     back = across(after(back, send), last)
     leaving = reduced(keep, send)
     arriving = across(leaving, last)
     (near_scores,) = call(near_scores_kernel, "near_scores", [((n, k // 2), f32)], [vmem] * (2 + last))(
         after(particles, leaving), got[0], *near
     )
-    stack = after(stack, (near_scores, back))
+    late_stack = after(late_stack, (near_scores, back))
 
     keep, send = call(
-        functools.partial(near_sums_kernel, dom), "near_sums", [(send_shape, f32)] * 2, [vmem] * (1 + dom)
-    )(stack, *got)
+        functools.partial(near_sums_kernel, first), "near_sums", [(send_shape, f32)] * 2, [vmem] * (2 + dom)
+    )(early_stack, late_stack, *got)
     near_sums = reduced(keep, send)
 
     (scored,) = call(scores_kernel, "scores", [((n, k), f32)], [vmem] * 3)(near_scores, back, got[0])

time: 30.4 us -> 30.1 us (level)
  waiting for transfers between devices: 2.92 us -> 2.4 us
    ppermute x7, waiting for transfers between devices: 1.04 us -> 0.57 us  [on_device(): got.append(lax.ppermute(x, 'dom', [(d, d ^ s) for d in range(dom)]))]
    pallas_call x2 -> x3, Pallas kernels: 1.49 us -> 1.69 us  [the longest x1 0.64 us: on_device(): call(far_sums_kernel, 'far_sums', [((n * (dom - first) * COARSE, cols), b...]
  transfers between devices with their start and end apart: 13 -> 13, of which waited for: 5 -> 5; matrix products, arithmetic and copies ran while one was open for 0% -> 0% of each run, Pallas kernels for 24% -> 26%
where the time goes in v6:
time: 30.1 us; the launch traced here: 29.9 us
  starting transfers between devices  15.8 us (52%)
  Pallas kernels  8.37 us (28%)
  waiting for transfers between devices  2.4 us (8%)
  local copies, waits for them, and re-layouts  1.87 us (6%)
  between operations  0.73 us (2%)
  other arithmetic  0.7 us (2%)
    ppermute x7, starting transfers between devices, on_device(): got.append(lax.ppermute(x, 'dom', [(d, d ^ s) for d in range(dom)]))  11.1 us
    ppermute x6, starting transfers between devices, across(): return lax.ppermute(x, 'cls', [(c, c ^ bit) for c in range(groups)])  4.65 us
    pallas_call x1, Pallas kernels, on_device(): call(pack_kernel, 'pack', [((n, cols + ROT * k), bf16)] * dom, [vmem] * 3...  2.1 us
    unnamed x8, local copies, waits for them, and re-layouts  1.87 us
    ppermute x6, waiting for transfers between devices, across(): return lax.ppermute(x, 'cls', [(c, c ^ bit) for c in range(groups)])  1.83 us
    pallas_call x1, Pallas kernels, on_device(): call(near_scores_kernel, 'near_scores', [((n, k // 2), f32)], [vmem] * (2...  1.75 us
    pallas_call x1, Pallas kernels, on_device(): call(guest_kernel, 'guest_scores', [((n * ROT // PAIR, PAIR * k // 2), f3...  1.55 us
    pallas_call x1, Pallas kernels, on_device(): call(scores_kernel, 'scores', [((n, k), f32)], [vmem] * 3)  1.29 us
  transfers between devices with their start and end apart: 13, of which 5 were waited for; matrix products, arithmetic and copies ran while one was open for 0% of the time, Pallas kernels for 26%

profile of v6, /device:TPU:0, one launch (start us, length us, event | category | flops | bytes accessed | tf_op | source)
XLA Modules:
  0.0 29.9 jit_solution(13648786481153066367)
XLA Ops:
  0.6 0.5 %collective-permute-start.1 = (bf16[16,16384]{1,0:T(8,128)(2,1)}, bf16[16,16384]{1,0:T(8,128)(2,1)S(1)}, u32[]{:S(2)}, u32[]{:S(2)}) collective-permute-start(bf16[16,16384]{1,0:T(8,128)(2,1)} %refs_0_.3), channel_id=1, source_target_pairs={{0,1},{1,0},{2,3},{3,2},{4,5},{5,4},{6,7},{7,6},{8,9},{9,8},{10,11... | collective-permute-start | bytes 1572872 | tf_op jit(solution)/shard_map/ppermute | solution.py:203
  1.1 2.6 %collective-permute-start = (bf16[8,16384]{1,0:T(8,128)(2,1)}, bf16[8,16384]{1,0:T(8,128)(2,1)S(1)}, u32[]{:S(2)}, u32[]{:S(2)}) collective-permute-start(bf16[8,16384]{1,0:T(8,128)(2,1)} %part_ref.2), channel_id=1, source_target_pairs={{0,2},{1,3},{2,0},{3,1},{4,6},{5,7},{6,4},{7,5},{8,10},{9,11},{10,... | collective-permute-start | bytes 786440 | tf_op jit(solution)/shard_map/ppermute | solution.py:203
  3.7 2.1 %pack.1 = (bf16[8,3584]{1,0:T(8,128)(2,1)}, bf16[8,3584]{1,0:T(8,128)(2,1)}, bf16[8,3584]{1,0:T(8,128)(2,1)}, bf16[8,3584]{1,0:T(8,128)(2,1)}, bf16[8,3584]{1,0:...) custom-call(bf16[8,16384]{1,0:T(8,128)(2,1)} %part_ref.2, ...), custom_call_target="tpu_custom_call" | custom-call | tf_op jit(solution)/shard_map/pack/pallas_call | solution.py:221
  5.8 0.0 collective-permute-done.1.refs_1_
  5.8 4.6 %collective-permute-start.2 = (bf16[8,3584]{1,0:T(8,128)(2,1)}, bf16[8,3584]{1,0:T(8,128)(2,1)S(1)}, u32[]{:S(2)}, u32[]{:S(2)}) collective-permute-start(bf16[8,3584]{1,0:T(8,128)(2,1)} %get-tuple-element.45), channel_id=1, source_target_pairs={{0,28},{4,24},{8,20},{12,16},{16,12},{20,8},{24,4},{28,0},{1,29},{... | collective-permute-start | bytes 172040 | tf_op jit(solution)/shard_map/ppermute | solution.py:232
  10.4 0.2 collective-permute-start.3
  10.6 0.8 %collective-permute-start.4 = (bf16[8,3584]{1,0:T(8,128)(2,1)}, bf16[8,3584]{1,0:T(8,128)(2,1)S(1)}, u32[]{:S(2)}, u32[]{:S(2)}) collective-permute-start(bf16[8,3584]{1,0:T(8,128)(2,1)} %get-tuple-element.47), channel_id=1, source_target_pairs={{0,20},{4,16},{8,28},{12,24},{16,4},{20,0},{24,12},{28,8},{1,21},{... | collective-permute-start | bytes 172040 | tf_op jit(solution)/shard_map/ppermute | solution.py:232
  11.4 2.1 %collective-permute-start.5 = (bf16[8,3584]{1,0:T(8,128)(2,1)}, bf16[8,3584]{1,0:T(8,128)(2,1)S(1)}, u32[]{:S(2)}, u32[]{:S(2)}) collective-permute-start(bf16[8,3584]{1,0:T(8,128)(2,1)} %get-tuple-element.49), channel_id=1, source_target_pairs={{0,16},{4,20},{8,24},{12,28},{16,0},{20,4},{24,8},{28,12},{1,17},{... | collective-permute-start | bytes 172040 | tf_op jit(solution)/shard_map/ppermute | solution.py:232
  13.5 0.0 collective-permute-done.part_ref
  13.5 2.2 %collective-permute-start.6 = (bf16[8,3584]{1,0:T(8,128)(2,1)}, bf16[8,3584]{1,0:T(8,128)(2,1)S(1)}, u32[]{:S(2)}, u32[]{:S(2)}) collective-permute-start(bf16[8,3584]{1,0:T(8,128)(2,1)} %get-tuple-element.50), channel_id=1, source_target_pairs={{0,12},{4,8},{8,4},{12,0},{16,28},{20,24},{24,20},{28,16},{1,13},{... | collective-permute-start | bytes 172040 | tf_op jit(solution)/shard_map/ppermute | solution.py:232
  15.7 0.0 collective-permute-done.2.refs_1_
  15.7 0.8 %collective-permute-start.7 = (bf16[8,3584]{1,0:T(8,128)(2,1)}, bf16[8,3584]{1,0:T(8,128)(2,1)S(1)}, u32[]{:S(2)}, u32[]{:S(2)}) collective-permute-start(bf16[8,3584]{1,0:T(8,128)(2,1)} %get-tuple-element.51), channel_id=1, source_target_pairs={{0,8},{4,12},{8,0},{12,4},{16,24},{20,28},{24,16},{28,20},{1,9},{5... | collective-permute-start | bytes 172040 | tf_op jit(solution)/shard_map/ppermute | solution.py:232
  16.5 0.4 %collective-permute-done.3.refs_2_ = bf16[8,3584]{1,0:T(8,128)(2,1)S(1)} collective-permute-done((bf16[8,3584]{1,0:T(8,128)(2,1)}, bf16[8,3584]{1,0:T(8,128)(2,1)S(1)}, u32[]{:S(2)}, u32[]{:S(2)}) %collective-permute-start.3) | collective-permute-done | bytes 57376 | tf_op jit(solution)/shard_map/ppermute | solution.py:232
  17.0 0.5 %collective-permute-start.8 = (bf16[8,3584]{1,0:T(8,128)(2,1)}, bf16[8,3584]{1,0:T(8,128)(2,1)S(1)}, u32[]{:S(2)}, u32[]{:S(2)}) collective-permute-start(bf16[8,3584]{1,0:T(8,128)(2,1)} %get-tuple-element.52), channel_id=1, source_target_pairs={{0,4},{4,0},{8,12},{12,8},{16,20},{20,16},{24,28},{28,24},{1,5},{5... | collective-permute-start | bytes 172040 | tf_op jit(solution)/shard_map/ppermute | solution.py:232
  17.4 0.0 copy-start
  17.4 1.0 %copy-done = bf16[16,16384]{1,0:T(8,128)(2,1)S(1)} copy-done((bf16[16,16384]{1,0:T(8,128)(2,1)S(1)}, bf16[16,16384]{1,0:T(8,128)(2,1)}, u32[]{:S(2)}) %copy-start) | copy-done | bytes 524312
  18.5 0.0 copy-start.3
  18.5 0.8 %copy-done.3 = bf16[8,3584]{1,0:T(8,128)(2,1)S(1)} copy-done((bf16[8,3584]{1,0:T(8,128)(2,1)S(1)}, bf16[8,3584]{1,0:T(8,128)(2,1)}, u32[]{:S(2)}) %copy-start.3) | copy-done | bytes 57368
  19.3 1.6 %guest_scores.1 = (f32[96,64]{1,0:T(8,128)S(1)}, bf16[8,3584]{1,0:T(8,128)(2,1)S(1)}) custom-call(bf16[8,16384]{1,0:T(8,128)(2,1)S(1)} %collective-permute-done.part_ref, bf16[8,3584]{1,0:T(8,128)(2,1)S(1)} %copy-done.3, bf16[16,16384]{1,0:T(8,128)(2,1)S(1)} %copy-done, bf16[16,16384]{1,0:T(8,128)(2,1)S(1)} %collective-permute-done.1.refs_1_), custom_call_target="tpu_custom_call" | custom-call | tf_op jit(solution)/shard_map/guest_scores/pallas_call | solution.py:235
  20.9 0.0 collective-permute-done.4.refs_3_
  20.9 0.4 %early_sums.1 = (bf16[192,2048]{1,0:T(8,128)(2,1)S(1)}, f32[128,2048]{1,0:T(8,128)S(1)}) custom-call(bf16[8,3584]{1,0:T(8,128)(2,1)S(1)} %get-tuple-element.44.refs_0_.weights_ref, bf16[8,3584]{1,0:T(8,128)(2,1)S(1)} %collective-permute-done.2.refs_1_, bf16[8,3584]{1,0:T(8,128)(2,1)S(1)} %collective-permute-done.3.refs_2_, ...), custom_call_target="tpu_custom_call" | custom-call | tf_op jit(solution)/shard_map/early_sums/pallas_call | solution.py:243
  21.3 0.0 collective-permute-done.5.refs_0_.refs_4_
  21.3 0.0 collective-permute-done.6.refs_1_.refs_5_
  21.3 0.1 collective-permute-done.7.refs_2_.refs_6_
  21.4 0.0 collective-permute-done.8.refs_3_.refs_7_
  21.4 0.0 copy-start.1
  21.5 0.6 %far_sums.1 = (bf16[192,2048]{1,0:T(8,128)(2,1)S(1)}, f32[1,16,2048]{2,1,0:T(8,128)S(1)}, f32[1,16,2048]{2,1,0:T(8,128)S(1)}) custom-call(f32[128,2048]{1,0:T(8,128)S(1)} %get-tuple-element.48.early_ref, bf16[8,3584]{1,0:T(8,128)(2,1)S(1)} %collective-permute-done.5.refs_0_.refs_4_, bf16[8,3584]{1,0:T(8,128)(2,1)S(1)} %collective-permute-done.6.refs_1_.refs_5_, ...), custom_call_target="tpu_custom_call" | custom-call | tf_op jit(solution)/shard_map/far_sums/pallas_call | solution.py:250
  22.1 0.0 copy-start.2
  22.1 0.1 collective-permute-start.9
  22.2 0.6 %collective-permute-start.10 = (f32[96,64]{1,0:T(8,128)S(1)}, f32[96,64]{1,0:T(8,128)S(1)}, u32[]{:S(2)}, u32[]{:S(2)}) collective-permute-start(f32[96,64]{1,0:T(8,128)S(1)} %get-tuple-element.61), channel_id=1, source_target_pairs={{0,2},{1,3},{2,0},{3,1},{4,6},{5,7},{6,4},{7,5},{8,10},{9,11},{10,... | collective-permute-start | bytes 73736 | tf_op jit(solution)/shard_map/ppermute | solution.py:203
  22.8 0.8 %collective-permute-done.9 = f32[1,16,2048]{2,1,0:T(8,128)S(1)} collective-permute-done((f32[1,16,2048]{2,1,0:T(8,128)S(1)}, f32[1,16,2048]{2,1,0:T(8,128)S(1)}, u32[]{:S(2)}, u32[]{:S(2)}) %collective-permute-start.9) | collective-permute-done | bytes 131104 | tf_op jit(solution)/shard_map/ppermute | solution.py:203
  23.5 0.8 %collective-permute-start.12 = (f32[16,2048]{1,0:T(8,128)S(1)}, f32[16,2048]{1,0:T(8,128)S(1)}, u32[]{:S(2)}, u32[]{:S(2)}) collective-permute-start(f32[16,2048]{1,0:T(8,128)S(1)} %add_bitcast_fusion), channel_id=1, source_target_pairs={{0,2},{1,3},{2,0},{3,1},{4,6},{5,7},{6,4},{7,5},{8,10},{9,11},{10,... | collective-permute-start | bytes 393224 | tf_op jit(solution)/shard_map/ppermute | solution.py:203
  24.4 0.0 copy-done.1
  24.4 0.0 copy-done.2
  24.4 1.7 %near_scores.1.near_ref = f32[8,32]{1,0:T(8,128)S(1)} custom-call(bf16[8,16384]{1,0:T(8,128)(2,1)S(1)} %copy-done.2, bf16[8,3584]{1,0:T(8,128)(2,1)S(1)} %get-tuple-element.44.refs_0_.weights_ref, bf16[16,16384]{1,0:T(8,128)(2,1)S(1)} %copy-done.1, bf16[16,16384]{1,0:T(8,128)(2,1)S(1)} %collective-permute-done.1.refs_1_), custom_call_target="tpu_custom_call" | custom-call | tf_op jit(solution)/shard_map/near_scores/pallas_call | solution.py:259
  26.1 0.2 collective-permute-done.10.back_ref
  26.4 0.6 %near_sums.1 = (f32[1,16,2048]{2,1,0:T(8,128)S(1)}, f32[1,16,2048]{2,1,0:T(8,128)S(1)}) custom-call(bf16[192,2048]{1,0:T(8,128)(2,1)S(1)} %get-tuple-element.62.early_ref, bf16[192,2048]{1,0:T(8,128)(2,1)S(1)} %get-tuple-element.64.late_ref, bf16[8,3584]{1,0:T(8,128)(2,1)S(1)} %get-tuple-element.44.refs_0_.weights_ref, ...), custom_call_target="tpu_custom_call" | custom-call | tf_op jit(solution)/shard_map/near_sums/pallas_call | solution.py:264
  27.0 0.1 collective-permute-start.11
  27.0 1.3 %scores.1 = f32[8,64]{1,0:T(8,128)} custom-call(f32[8,32]{1,0:T(8,128)S(1)} %near_scores.1.near_ref, f32[96,64]{1,0:T(8,128)S(1)} %collective-permute-done.10.back_ref, bf16[8,3584]{1,0:T(8,128)(2,1)S(1)} %get-tuple-element.44.refs_0_.weights_ref), custom_call_target="tpu_custom_call" | custom-call | tf_op jit(solution)/shard_map/scores/pallas_call | solution.py:269
  28.3 0.8 %collective-permute-done.12 = f32[16,2048]{1,0:T(8,128)S(1)} collective-permute-done((f32[16,2048]{1,0:T(8,128)S(1)}, f32[16,2048]{1,0:T(8,128)S(1)}, u32[]{:S(2)}, u32[]{:S(2)}) %collective-permute-start.12) | collective-permute-done | bytes 131104 | tf_op jit(solution)/shard_map/ppermute | solution.py:203
  29.2 0.0 collective-permute-done.11
  29.2 0.7 %fusion = f32[16,2048]{1,0:T(8,128)} fusion(f32[16,2048]{1,0:T(8,128)S(1)} %collective-permute-done.12, f32[1,16,2048]{2,1,0:T(8,128)S(1)} %get-tuple-element.65, f32[1,16,2048]{2,1,0:T(8,128)S(1)} %collective-permute-done.11), kind=kLoop, calls=%fused_computation.1 | loop fusion | flops 98304 | bytes 524288 | tf_op jit(solution)/shard_map/div | solution.py:271
  (1 shorter events, 0.0 us)
Async XLA Ops:
  0.6 5.2 %collective-permute-start.1 = (bf16[16,16384]{1,0:T(8,128)(2,1)}, bf16[16,16384]{1,0:T(8,128)(2,1)S(1)}, u32[]{:S(2)}, u32[]{:S(2)}) collective-permute-start(bf16[16,16384]{1,0:T(8,128)(2,1)} %refs_0_.3), channel_id=1, source_target_pairs={{0,1},{1,0},{2,3},{3,2},{4,5},{5,4},{6,7},{7,6},{8,9},{9,8},{10,11... | collective-permute-start | bytes 1572872 | tf_op jit(solution)/shard_map/ppermute | solution.py:203
  1.1 12.4 %collective-permute-start = (bf16[8,16384]{1,0:T(8,128)(2,1)}, bf16[8,16384]{1,0:T(8,128)(2,1)S(1)}, u32[]{:S(2)}, u32[]{:S(2)}) collective-permute-start(bf16[8,16384]{1,0:T(8,128)(2,1)} %part_ref.2), channel_id=1, source_target_pairs={{0,2},{1,3},{2,0},{3,1},{4,6},{5,7},{6,4},{7,5},{8,10},{9,11},{10,... | collective-permute-start | bytes 786440 | tf_op jit(solution)/shard_map/ppermute | solution.py:203
  5.8 9.9 %collective-permute-start.2 = (bf16[8,3584]{1,0:T(8,128)(2,1)}, bf16[8,3584]{1,0:T(8,128)(2,1)S(1)}, u32[]{:S(2)}, u32[]{:S(2)}) collective-permute-start(bf16[8,3584]{1,0:T(8,128)(2,1)} %get-tuple-element.45), channel_id=1, source_target_pairs={{0,28},{4,24},{8,20},{12,16},{16,12},{20,8},{24,4},{28,0},{1,29},{... | collective-permute-start | bytes 172040 | tf_op jit(solution)/shard_map/ppermute | solution.py:232
  10.4 6.5 %collective-permute-start.3 = (bf16[8,3584]{1,0:T(8,128)(2,1)}, bf16[8,3584]{1,0:T(8,128)(2,1)S(1)}, u32[]{:S(2)}, u32[]{:S(2)}) collective-permute-start(bf16[8,3584]{1,0:T(8,128)(2,1)} %get-tuple-element.46), channel_id=1, source_target_pairs={{0,24},{4,28},{8,16},{12,20},{16,8},{20,12},{24,0},{28,4},{1,25},{... | collective-permute-start | bytes 172040 | tf_op jit(solution)/shard_map/ppermute | solution.py:232
  10.6 10.2 %collective-permute-start.4 = (bf16[8,3584]{1,0:T(8,128)(2,1)}, bf16[8,3584]{1,0:T(8,128)(2,1)S(1)}, u32[]{:S(2)}, u32[]{:S(2)}) collective-permute-start(bf16[8,3584]{1,0:T(8,128)(2,1)} %get-tuple-element.47), channel_id=1, source_target_pairs={{0,20},{4,16},{8,28},{12,24},{16,4},{20,0},{24,12},{28,8},{1,21},{... | collective-permute-start | bytes 172040 | tf_op jit(solution)/shard_map/ppermute | solution.py:232
  11.4 9.9 %collective-permute-start.5 = (bf16[8,3584]{1,0:T(8,128)(2,1)}, bf16[8,3584]{1,0:T(8,128)(2,1)S(1)}, u32[]{:S(2)}, u32[]{:S(2)}) collective-permute-start(bf16[8,3584]{1,0:T(8,128)(2,1)} %get-tuple-element.49), channel_id=1, source_target_pairs={{0,16},{4,20},{8,24},{12,28},{16,0},{20,4},{24,8},{28,12},{1,17},{... | collective-permute-start | bytes 172040 | tf_op jit(solution)/shard_map/ppermute | solution.py:232
  13.5 7.8 %collective-permute-start.6 = (bf16[8,3584]{1,0:T(8,128)(2,1)}, bf16[8,3584]{1,0:T(8,128)(2,1)S(1)}, u32[]{:S(2)}, u32[]{:S(2)}) collective-permute-start(bf16[8,3584]{1,0:T(8,128)(2,1)} %get-tuple-element.50), channel_id=1, source_target_pairs={{0,12},{4,8},{8,4},{12,0},{16,28},{20,24},{24,20},{28,16},{1,13},{... | collective-permute-start | bytes 172040 | tf_op jit(solution)/shard_map/ppermute | solution.py:232
  15.7 5.7 %collective-permute-start.7 = (bf16[8,3584]{1,0:T(8,128)(2,1)}, bf16[8,3584]{1,0:T(8,128)(2,1)S(1)}, u32[]{:S(2)}, u32[]{:S(2)}) collective-permute-start(bf16[8,3584]{1,0:T(8,128)(2,1)} %get-tuple-element.51), channel_id=1, source_target_pairs={{0,8},{4,12},{8,0},{12,4},{16,24},{20,28},{24,16},{28,20},{1,9},{5... | collective-permute-start | bytes 172040 | tf_op jit(solution)/shard_map/ppermute | solution.py:232
  17.0 4.5 %collective-permute-start.8 = (bf16[8,3584]{1,0:T(8,128)(2,1)}, bf16[8,3584]{1,0:T(8,128)(2,1)S(1)}, u32[]{:S(2)}, u32[]{:S(2)}) collective-permute-start(bf16[8,3584]{1,0:T(8,128)(2,1)} %get-tuple-element.52), channel_id=1, source_target_pairs={{0,4},{4,0},{8,12},{12,8},{16,20},{20,16},{24,28},{28,24},{1,5},{5... | collective-permute-start | bytes 172040 | tf_op jit(solution)/shard_map/ppermute | solution.py:232
  17.4 1.0 %copy-start = (bf16[16,16384]{1,0:T(8,128)(2,1)S(1)}, bf16[16,16384]{1,0:T(8,128)(2,1)}, u32[]{:S(2)}) copy-start(bf16[16,16384]{1,0:T(8,128)(2,1)} %refs_0_.3) | copy-start | bytes 1572868
  18.5 0.8 %copy-start.3 = (bf16[8,3584]{1,0:T(8,128)(2,1)S(1)}, bf16[8,3584]{1,0:T(8,128)(2,1)}, u32[]{:S(2)}) copy-start(bf16[8,3584]{1,0:T(8,128)(2,1)} %get-tuple-element.43.packed_ref) | copy-start | bytes 172036
  21.4 2.9 %copy-start.1 = (bf16[16,16384]{1,0:T(8,128)(2,1)S(1)}, bf16[16,16384]{1,0:T(8,128)(2,1)}, u32[]{:S(2)}) copy-start(bf16[16,16384]{1,0:T(8,128)(2,1)} %refs_0_.3) | copy-start | bytes 1572868
  22.1 2.3 %copy-start.2 = (bf16[8,16384]{1,0:T(8,128)(2,1)S(1)}, bf16[8,16384]{1,0:T(8,128)(2,1)}, u32[]{:S(2)}) copy-start(bf16[8,16384]{1,0:T(8,128)(2,1)} %part_ref.2) | copy-start | bytes 786436
  22.1 1.4 %collective-permute-start.9 = (f32[1,16,2048]{2,1,0:T(8,128)S(1)}, f32[1,16,2048]{2,1,0:T(8,128)S(1)}, u32[]{:S(2)}, u32[]{:S(2)}) collective-permute-start(f32[1,16,2048]{2,1,0:T(8,128)S(1)} %get-tuple-element.58), channel_id=1, source_target_pairs={{0,1},{1,0},{2,3},{3,2},{4,5},{5,4},{6,7},{7,6},{8,9},{9,8},{10,11... | collective-permute-start | bytes 393224 | tf_op jit(solution)/shard_map/ppermute | solution.py:203
  22.2 4.2 %collective-permute-start.10 = (f32[96,64]{1,0:T(8,128)S(1)}, f32[96,64]{1,0:T(8,128)S(1)}, u32[]{:S(2)}, u32[]{:S(2)}) collective-permute-start(f32[96,64]{1,0:T(8,128)S(1)} %get-tuple-element.61), channel_id=1, source_target_pairs={{0,2},{1,3},{2,0},{3,1},{4,6},{5,7},{6,4},{7,5},{8,10},{9,11},{10,... | collective-permute-start | bytes 73736 | tf_op jit(solution)/shard_map/ppermute | solution.py:203
  23.5 5.6 %collective-permute-start.12 = (f32[16,2048]{1,0:T(8,128)S(1)}, f32[16,2048]{1,0:T(8,128)S(1)}, u32[]{:S(2)}, u32[]{:S(2)}) collective-permute-start(f32[16,2048]{1,0:T(8,128)S(1)} %add_bitcast_fusion), channel_id=1, source_target_pairs={{0,2},{1,3},{2,0},{3,1},{4,6},{5,7},{6,4},{7,5},{8,10},{9,11},{10,... | collective-permute-start | bytes 393224 | tf_op jit(solution)/shard_map/ppermute | solution.py:203
  27.0 2.2 %collective-permute-start.11 = (f32[1,16,2048]{2,1,0:T(8,128)S(1)}, f32[1,16,2048]{2,1,0:T(8,128)S(1)}, u32[]{:S(2)}, u32[]{:S(2)}) collective-permute-start(f32[1,16,2048]{2,1,0:T(8,128)S(1)} %get-tuple-element.66), channel_id=1, source_target_pairs={{0,1},{1,0},{2,3},{3,2},{4,5},{5,4},{6,7},{7,6},{8,9},{9,8},{10,11... | collective-permute-start | bytes 393224 | tf_op jit(solution)/shard_map/ppermute | solution.py:203

commit v7 on v6

--- a/solution.py
+++ b/solution.py
@@ -18,7 +18,7 @@
 CHUNK = 4
 LANES = 128
 VMEM_BYTES = 48 * 1024 * 1024
-VMEM_MOST = 65900000
+VMEM_MOST = 56000000
 f32 = jnp.float32
 bf16 = jnp.bfloat16
 

time: 30.1 us -> 29.8 us (0.990)
  Pallas kernels: 8.37 us -> 7.61 us
  waiting for transfers between devices: 2.4 us -> 2.98 us
    pallas_call x1, Pallas kernels: 2.1 us -> 1.29 us  [on_device(): call(pack_kernel, 'pack', [((n, cols + ROT * k), bf16)] * dom, [vmem] * 3...]
    ppermute x7, waiting for transfers between devices: 0.57 us -> 1.2 us  [on_device(): got.append(lax.ppermute(x, 'dom', [(d, d ^ s) for d in range(dom)]))]
  transfers between devices with their start and end apart: 13 -> 13, of which waited for: 5 -> 6; matrix products, arithmetic and copies ran while one was open for 0% -> 0% of each run, Pallas kernels for 26% -> 24%
where the time goes in v7:
time: 29.8 us; the launch traced here: 29.6 us
  starting transfers between devices  15.8 us (53%)
  Pallas kernels  7.61 us (26%)
  waiting for transfers between devices  2.98 us (10%)
  local copies, waits for them, and re-layouts  1.74 us (6%)
  between operations  0.73 us (2%)
  other arithmetic  0.7 us (2%)
    ppermute x7, starting transfers between devices, on_device(): got.append(lax.ppermute(x, 'dom', [(d, d ^ s) for d in range(dom)]))  11.1 us
    ppermute x6, starting transfers between devices, across(): return lax.ppermute(x, 'cls', [(c, c ^ bit) for c in range(groups)])  4.65 us
    ppermute x6, waiting for transfers between devices, across(): return lax.ppermute(x, 'cls', [(c, c ^ bit) for c in range(groups)])  1.79 us
    pallas_call x1, Pallas kernels, on_device(): call(near_scores_kernel, 'near_scores', [((n, k // 2), f32)], [vmem] * (2...  1.75 us
    unnamed x8, local copies, waits for them, and re-layouts  1.74 us
    pallas_call x1, Pallas kernels, on_device(): call(guest_kernel, 'guest_scores', [((n * ROT // PAIR, PAIR * k // 2), f3...  1.56 us
    pallas_call x1, Pallas kernels, on_device(): call(pack_kernel, 'pack', [((n, cols + ROT * k), bf16)] * dom, [vmem] * 3...  1.29 us
    pallas_call x1, Pallas kernels, on_device(): call(scores_kernel, 'scores', [((n, k), f32)], [vmem] * 3)  1.29 us
  transfers between devices with their start and end apart: 13, of which 6 were waited for; matrix products, arithmetic and copies ran while one was open for 0% of the time, Pallas kernels for 24%

profile of v7, /device:TPU:0, one launch (start us, length us, event | category | flops | bytes accessed | tf_op | source)
XLA Modules:
  0.0 29.6 jit_solution(2114645496371641080)
XLA Ops:
  0.6 0.5 %collective-permute-start.1 = (bf16[16,16384]{1,0:T(8,128)(2,1)}, bf16[16,16384]{1,0:T(8,128)(2,1)S(1)}, u32[]{:S(2)}, u32[]{:S(2)}) collective-permute-start(bf16[16,16384]{1,0:T(8,128)(2,1)} %refs_0_.3), channel_id=1, source_target_pairs={{0,1},{1,0},{2,3},{3,2},{4,5},{5,4},{6,7},{7,6},{8,9},{9,8},{10,11... | collective-permute-start | bytes 1572872 | tf_op jit(solution)/shard_map/ppermute | solution.py:203
  1.1 2.6 %collective-permute-start = (bf16[8,16384]{1,0:T(8,128)(2,1)}, bf16[8,16384]{1,0:T(8,128)(2,1)S(1)}, u32[]{:S(2)}, u32[]{:S(2)}) collective-permute-start(bf16[8,16384]{1,0:T(8,128)(2,1)} %part_ref.2), channel_id=1, source_target_pairs={{0,2},{1,3},{2,0},{3,1},{4,6},{5,7},{6,4},{7,5},{8,10},{9,11},{10,... | collective-permute-start | bytes 786440 | tf_op jit(solution)/shard_map/ppermute | solution.py:203
  3.7 0.0 copy-start.3
  3.7 0.7 %copy-done.3 = s32[8,64]{1,0:T(8,128)S(1)} copy-done((s32[8,64]{1,0:T(8,128)S(1)}, s32[8,64]{1,0:T(8,128)}, u32[]{:S(2)}) %copy-start.3) | copy-done | bytes 2072
  4.4 1.3 %pack.1 = (bf16[8,3584]{1,0:T(8,128)(2,1)S(1)}, bf16[8,3584]{1,0:T(8,128)(2,1)S(1)}, bf16[8,3584]{1,0:T(8,128)(2,1)S(1)}, bf16[8,3584]{1,0:T(8,128)(2,1)S(1)}, b...) custom-call(bf16[8,16384]{1,0:T(8,128)(2,1)} %part_ref.2, ...), custom_call_target="tpu_custom_call" | custom-call | tf_op jit(solution)/shard_map/pack/pallas_call | solution.py:221
  5.7 0.0 collective-permute-done.1.refs_1_
  5.7 4.6 %collective-permute-start.2 = (bf16[8,3584]{1,0:T(8,128)(2,1)S(1)}, bf16[8,3584]{1,0:T(8,128)(2,1)S(1)}, u32[]{:S(2)}, u32[]{:S(2)}) collective-permute-start(bf16[8,3584]{1,0:T(8,128)(2,1)S(1)} %get-tuple-element.45), channel_id=1, source_target_pairs={{0,28},{4,24},{8,20},{12,16},{16,12},{20,8},{24,4},{28,0},{1,29},{... | collective-permute-start | bytes 172040 | tf_op jit(solution)/shard_map/ppermute | solution.py:232
  10.3 0.2 collective-permute-start.3
  10.6 0.8 %collective-permute-start.4 = (bf16[8,3584]{1,0:T(8,128)(2,1)S(1)}, bf16[8,3584]{1,0:T(8,128)(2,1)S(1)}, u32[]{:S(2)}, u32[]{:S(2)}) collective-permute-start(bf16[8,3584]{1,0:T(8,128)(2,1)S(1)} %get-tuple-element.47), channel_id=1, source_target_pairs={{0,20},{4,16},{8,28},{12,24},{16,4},{20,0},{24,12},{28,8},{1,21},{... | collective-permute-start | bytes 172040 | tf_op jit(solution)/shard_map/ppermute | solution.py:232
  11.3 2.1 %collective-permute-start.5 = (bf16[8,3584]{1,0:T(8,128)(2,1)S(1)}, bf16[8,3584]{1,0:T(8,128)(2,1)S(1)}, u32[]{:S(2)}, u32[]{:S(2)}) collective-permute-start(bf16[8,3584]{1,0:T(8,128)(2,1)S(1)} %get-tuple-element.49), channel_id=1, source_target_pairs={{0,16},{4,20},{8,24},{12,28},{16,0},{20,4},{24,8},{28,12},{1,17},{... | collective-permute-start | bytes 172040 | tf_op jit(solution)/shard_map/ppermute | solution.py:232
  13.5 0.0 collective-permute-done.part_ref
  13.5 2.2 %collective-permute-start.6 = (bf16[8,3584]{1,0:T(8,128)(2,1)S(1)}, bf16[8,3584]{1,0:T(8,128)(2,1)S(1)}, u32[]{:S(2)}, u32[]{:S(2)}) collective-permute-start(bf16[8,3584]{1,0:T(8,128)(2,1)S(1)} %get-tuple-element.50), channel_id=1, source_target_pairs={{0,12},{4,8},{8,4},{12,0},{16,28},{20,24},{24,20},{28,16},{1,13},{... | collective-permute-start | bytes 172040 | tf_op jit(solution)/shard_map/ppermute | solution.py:232
  15.6 0.0 collective-permute-done.2.refs_1_
  15.6 0.8 %collective-permute-start.7 = (bf16[8,3584]{1,0:T(8,128)(2,1)S(1)}, bf16[8,3584]{1,0:T(8,128)(2,1)S(1)}, u32[]{:S(2)}, u32[]{:S(2)}) collective-permute-start(bf16[8,3584]{1,0:T(8,128)(2,1)S(1)} %get-tuple-element.51), channel_id=1, source_target_pairs={{0,8},{4,12},{8,0},{12,4},{16,24},{20,28},{24,16},{28,20},{1,9},{5... | collective-permute-start | bytes 172040 | tf_op jit(solution)/shard_map/ppermute | solution.py:232
  16.4 0.2 collective-permute-done.3.refs_2_
  16.7 0.5 %collective-permute-start.8 = (bf16[8,3584]{1,0:T(8,128)(2,1)S(1)}, bf16[8,3584]{1,0:T(8,128)(2,1)S(1)}, u32[]{:S(2)}, u32[]{:S(2)}) collective-permute-start(bf16[8,3584]{1,0:T(8,128)(2,1)S(1)} %get-tuple-element.52), channel_id=1, source_target_pairs={{0,4},{4,0},{8,12},{12,8},{16,20},{20,16},{24,28},{28,24},{1,5},{5... | collective-permute-start | bytes 172040 | tf_op jit(solution)/shard_map/ppermute | solution.py:232
  17.1 0.0 copy-start
  17.1 1.0 %copy-done = bf16[16,16384]{1,0:T(8,128)(2,1)S(1)} copy-done((bf16[16,16384]{1,0:T(8,128)(2,1)S(1)}, bf16[16,16384]{1,0:T(8,128)(2,1)}, u32[]{:S(2)}) %copy-start) | copy-done | bytes 524312
  18.2 1.6 %guest_scores.1 = (f32[96,64]{1,0:T(8,128)S(1)}, bf16[8,3584]{1,0:T(8,128)(2,1)S(1)}) custom-call(bf16[8,16384]{1,0:T(8,128)(2,1)S(1)} %collective-permute-done.part_ref, bf16[8,3584]{1,0:T(8,128)(2,1)S(1)} %get-tuple-element.43.packed_ref, bf16[16,16384]{1,0:T(8,128)(2,1)S(1)} %copy-done, bf16[16,16384]{1,0:T(8,128)(2,1)S(1)} %collective-permute-done.1.refs_1_), custom_call_target="tpu_custom_call" | custom-call | tf_op jit(solution)/shard_map/guest_scores/pallas_call | solution.py:235
  19.7 0.0 collective-permute-done.4.refs_3_
  19.7 0.4 %early_sums.1 = (bf16[192,2048]{1,0:T(8,128)(2,1)S(1)}, f32[128,2048]{1,0:T(8,128)S(1)}) custom-call(bf16[8,3584]{1,0:T(8,128)(2,1)S(1)} %get-tuple-element.44.refs_0_.weights_ref, bf16[8,3584]{1,0:T(8,128)(2,1)S(1)} %collective-permute-done.2.refs_1_, bf16[8,3584]{1,0:T(8,128)(2,1)S(1)} %collective-permute-done.3.refs_2_, ...), custom_call_target="tpu_custom_call" | custom-call | tf_op jit(solution)/shard_map/early_sums/pallas_call | solution.py:243
  20.2 0.4 %collective-permute-done.5.refs_0_.refs_4_ = bf16[8,3584]{1,0:T(8,128)(2,1)S(1)} collective-permute-done((bf16[8,3584]{1,0:T(8,128)(2,1)S(1)}, bf16[8,3584]{1,0:T(8,128)(2,1)S(1)}, u32[]{:S(2)}, u32[]{:S(2)}) %collective-permute-start.5) | collective-permute-done | bytes 57376 | tf_op jit(solution)/shard_map/ppermute | solution.py:232
  20.6 0.0 collective-permute-done.6.refs_1_.refs_5_
  20.7 0.5 %collective-permute-done.7.refs_2_.refs_6_ = bf16[8,3584]{1,0:T(8,128)(2,1)S(1)} collective-permute-done((bf16[8,3584]{1,0:T(8,128)(2,1)S(1)}, bf16[8,3584]{1,0:T(8,128)(2,1)S(1)}, u32[]{:S(2)}, u32[]{:S(2)}) %collective-permute-start.7) | collective-permute-done | bytes 57376 | tf_op jit(solution)/shard_map/ppermute | solution.py:232
  21.1 0.0 collective-permute-done.8.refs_3_.refs_7_
  21.2 0.0 copy-start.1
  21.2 0.6 %far_sums.1 = (bf16[192,2048]{1,0:T(8,128)(2,1)S(1)}, f32[1,16,2048]{2,1,0:T(8,128)S(1)}, f32[1,16,2048]{2,1,0:T(8,128)S(1)}) custom-call(f32[128,2048]{1,0:T(8,128)S(1)} %get-tuple-element.48.early_ref, bf16[8,3584]{1,0:T(8,128)(2,1)S(1)} %collective-permute-done.5.refs_0_.refs_4_, bf16[8,3584]{1,0:T(8,128)(2,1)S(1)} %collective-permute-done.6.refs_1_.refs_5_, ...), custom_call_target="tpu_custom_call" | custom-call | tf_op jit(solution)/shard_map/far_sums/pallas_call | solution.py:250
  21.8 0.0 copy-start.2
  21.8 0.1 collective-permute-start.9
  21.9 0.6 %collective-permute-start.10 = (f32[96,64]{1,0:T(8,128)S(1)}, f32[96,64]{1,0:T(8,128)S(1)}, u32[]{:S(2)}, u32[]{:S(2)}) collective-permute-start(f32[96,64]{1,0:T(8,128)S(1)} %get-tuple-element.61), channel_id=1, source_target_pairs={{0,2},{1,3},{2,0},{3,1},{4,6},{5,7},{6,4},{7,5},{8,10},{9,11},{10,... | collective-permute-start | bytes 73736 | tf_op jit(solution)/shard_map/ppermute | solution.py:203
  22.5 0.8 %collective-permute-done.9 = f32[1,16,2048]{2,1,0:T(8,128)S(1)} collective-permute-done((f32[1,16,2048]{2,1,0:T(8,128)S(1)}, f32[1,16,2048]{2,1,0:T(8,128)S(1)}, u32[]{:S(2)}, u32[]{:S(2)}) %collective-permute-start.9) | collective-permute-done | bytes 131104 | tf_op jit(solution)/shard_map/ppermute | solution.py:203
  23.2 0.8 %collective-permute-start.12 = (f32[16,2048]{1,0:T(8,128)S(1)}, f32[16,2048]{1,0:T(8,128)S(1)}, u32[]{:S(2)}, u32[]{:S(2)}) collective-permute-start(f32[16,2048]{1,0:T(8,128)S(1)} %add_bitcast_fusion), channel_id=1, source_target_pairs={{0,2},{1,3},{2,0},{3,1},{4,6},{5,7},{6,4},{7,5},{8,10},{9,11},{10,... | collective-permute-start | bytes 393224 | tf_op jit(solution)/shard_map/ppermute | solution.py:203
  24.1 0.0 copy-done.1
  24.1 0.0 copy-done.2
  24.1 1.7 %near_scores.1.near_ref = f32[8,32]{1,0:T(8,128)S(1)} custom-call(bf16[8,16384]{1,0:T(8,128)(2,1)S(1)} %copy-done.2, bf16[8,3584]{1,0:T(8,128)(2,1)S(1)} %get-tuple-element.44.refs_0_.weights_ref, bf16[16,16384]{1,0:T(8,128)(2,1)S(1)} %copy-done.1, bf16[16,16384]{1,0:T(8,128)(2,1)S(1)} %collective-permute-done.1.refs_1_), custom_call_target="tpu_custom_call" | custom-call | tf_op jit(solution)/shard_map/near_scores/pallas_call | solution.py:259
  25.8 0.2 collective-permute-done.10.back_ref
  26.1 0.6 %near_sums.1 = (f32[1,16,2048]{2,1,0:T(8,128)S(1)}, f32[1,16,2048]{2,1,0:T(8,128)S(1)}) custom-call(bf16[192,2048]{1,0:T(8,128)(2,1)S(1)} %get-tuple-element.62.early_ref, bf16[192,2048]{1,0:T(8,128)(2,1)S(1)} %get-tuple-element.64.late_ref, bf16[8,3584]{1,0:T(8,128)(2,1)S(1)} %get-tuple-element.44.refs_0_.weights_ref, ...), custom_call_target="tpu_custom_call" | custom-call | tf_op jit(solution)/shard_map/near_sums/pallas_call | solution.py:264
  26.7 0.1 collective-permute-start.11
  26.8 1.3 %scores.1 = f32[8,64]{1,0:T(8,128)} custom-call(f32[8,32]{1,0:T(8,128)S(1)} %near_scores.1.near_ref, f32[96,64]{1,0:T(8,128)S(1)} %collective-permute-done.10.back_ref, bf16[8,3584]{1,0:T(8,128)(2,1)S(1)} %get-tuple-element.44.refs_0_.weights_ref), custom_call_target="tpu_custom_call" | custom-call | tf_op jit(solution)/shard_map/scores/pallas_call | solution.py:269
  28.1 0.8 %collective-permute-done.12 = f32[16,2048]{1,0:T(8,128)S(1)} collective-permute-done((f32[16,2048]{1,0:T(8,128)S(1)}, f32[16,2048]{1,0:T(8,128)S(1)}, u32[]{:S(2)}, u32[]{:S(2)}) %collective-permute-start.12) | collective-permute-done | bytes 131104 | tf_op jit(solution)/shard_map/ppermute | solution.py:203
  28.9 0.0 collective-permute-done.11
  28.9 0.7 %fusion = f32[16,2048]{1,0:T(8,128)} fusion(f32[16,2048]{1,0:T(8,128)S(1)} %collective-permute-done.12, f32[1,16,2048]{2,1,0:T(8,128)S(1)} %get-tuple-element.65, f32[1,16,2048]{2,1,0:T(8,128)S(1)} %collective-permute-done.11), kind=kLoop, calls=%fused_computation.1 | loop fusion | flops 98304 | bytes 524288 | tf_op jit(solution)/shard_map/div | solution.py:271
  (1 shorter events, 0.0 us)
Async XLA Ops:
  0.6 5.1 %collective-permute-start.1 = (bf16[16,16384]{1,0:T(8,128)(2,1)}, bf16[16,16384]{1,0:T(8,128)(2,1)S(1)}, u32[]{:S(2)}, u32[]{:S(2)}) collective-permute-start(bf16[16,16384]{1,0:T(8,128)(2,1)} %refs_0_.3), channel_id=1, source_target_pairs={{0,1},{1,0},{2,3},{3,2},{4,5},{5,4},{6,7},{7,6},{8,9},{9,8},{10,11... | collective-permute-start | bytes 1572872 | tf_op jit(solution)/shard_map/ppermute | solution.py:203
  1.1 12.3 %collective-permute-start = (bf16[8,16384]{1,0:T(8,128)(2,1)}, bf16[8,16384]{1,0:T(8,128)(2,1)S(1)}, u32[]{:S(2)}, u32[]{:S(2)}) collective-permute-start(bf16[8,16384]{1,0:T(8,128)(2,1)} %part_ref.2), channel_id=1, source_target_pairs={{0,2},{1,3},{2,0},{3,1},{4,6},{5,7},{6,4},{7,5},{8,10},{9,11},{10,... | collective-permute-start | bytes 786440 | tf_op jit(solution)/shard_map/ppermute | solution.py:203
  3.7 0.7 %copy-start.3 = (s32[8,64]{1,0:T(8,128)S(1)}, s32[8,64]{1,0:T(8,128)}, u32[]{:S(2)}) copy-start(s32[8,64]{1,0:T(8,128)} %mask_ref.1) | copy-start | bytes 6148
  5.7 9.9 %collective-permute-start.2 = (bf16[8,3584]{1,0:T(8,128)(2,1)S(1)}, bf16[8,3584]{1,0:T(8,128)(2,1)S(1)}, u32[]{:S(2)}, u32[]{:S(2)}) collective-permute-start(bf16[8,3584]{1,0:T(8,128)(2,1)S(1)} %get-tuple-element.45), channel_id=1, source_target_pairs={{0,28},{4,24},{8,20},{12,16},{16,12},{20,8},{24,4},{28,0},{1,29},{... | collective-permute-start | bytes 172040 | tf_op jit(solution)/shard_map/ppermute | solution.py:232
  10.3 6.3 %collective-permute-start.3 = (bf16[8,3584]{1,0:T(8,128)(2,1)S(1)}, bf16[8,3584]{1,0:T(8,128)(2,1)S(1)}, u32[]{:S(2)}, u32[]{:S(2)}) collective-permute-start(bf16[8,3584]{1,0:T(8,128)(2,1)S(1)} %get-tuple-element.46), channel_id=1, source_target_pairs={{0,24},{4,28},{8,16},{12,20},{16,8},{20,12},{24,0},{28,4},{1,25},{... | collective-permute-start | bytes 172040 | tf_op jit(solution)/shard_map/ppermute | solution.py:232
  10.6 9.2 %collective-permute-start.4 = (bf16[8,3584]{1,0:T(8,128)(2,1)S(1)}, bf16[8,3584]{1,0:T(8,128)(2,1)S(1)}, u32[]{:S(2)}, u32[]{:S(2)}) collective-permute-start(bf16[8,3584]{1,0:T(8,128)(2,1)S(1)} %get-tuple-element.47), channel_id=1, source_target_pairs={{0,20},{4,16},{8,28},{12,24},{16,4},{20,0},{24,12},{28,8},{1,21},{... | collective-permute-start | bytes 172040 | tf_op jit(solution)/shard_map/ppermute | solution.py:232
  11.3 9.3 %collective-permute-start.5 = (bf16[8,3584]{1,0:T(8,128)(2,1)S(1)}, bf16[8,3584]{1,0:T(8,128)(2,1)S(1)}, u32[]{:S(2)}, u32[]{:S(2)}) collective-permute-start(bf16[8,3584]{1,0:T(8,128)(2,1)S(1)} %get-tuple-element.49), channel_id=1, source_target_pairs={{0,16},{4,20},{8,24},{12,28},{16,0},{20,4},{24,8},{28,12},{1,17},{... | collective-permute-start | bytes 172040 | tf_op jit(solution)/shard_map/ppermute | solution.py:232
  13.5 7.2 %collective-permute-start.6 = (bf16[8,3584]{1,0:T(8,128)(2,1)S(1)}, bf16[8,3584]{1,0:T(8,128)(2,1)S(1)}, u32[]{:S(2)}, u32[]{:S(2)}) collective-permute-start(bf16[8,3584]{1,0:T(8,128)(2,1)S(1)} %get-tuple-element.50), channel_id=1, source_target_pairs={{0,12},{4,8},{8,4},{12,0},{16,28},{20,24},{24,20},{28,16},{1,13},{... | collective-permute-start | bytes 172040 | tf_op jit(solution)/shard_map/ppermute | solution.py:232
  15.6 5.5 %collective-permute-start.7 = (bf16[8,3584]{1,0:T(8,128)(2,1)S(1)}, bf16[8,3584]{1,0:T(8,128)(2,1)S(1)}, u32[]{:S(2)}, u32[]{:S(2)}) collective-permute-start(bf16[8,3584]{1,0:T(8,128)(2,1)S(1)} %get-tuple-element.51), channel_id=1, source_target_pairs={{0,8},{4,12},{8,0},{12,4},{16,24},{20,28},{24,16},{28,20},{1,9},{5... | collective-permute-start | bytes 172040 | tf_op jit(solution)/shard_map/ppermute | solution.py:232
  16.7 4.5 %collective-permute-start.8 = (bf16[8,3584]{1,0:T(8,128)(2,1)S(1)}, bf16[8,3584]{1,0:T(8,128)(2,1)S(1)}, u32[]{:S(2)}, u32[]{:S(2)}) collective-permute-start(bf16[8,3584]{1,0:T(8,128)(2,1)S(1)} %get-tuple-element.52), channel_id=1, source_target_pairs={{0,4},{4,0},{8,12},{12,8},{16,20},{20,16},{24,28},{28,24},{1,5},{5... | collective-permute-start | bytes 172040 | tf_op jit(solution)/shard_map/ppermute | solution.py:232
  17.1 1.0 %copy-start = (bf16[16,16384]{1,0:T(8,128)(2,1)S(1)}, bf16[16,16384]{1,0:T(8,128)(2,1)}, u32[]{:S(2)}) copy-start(bf16[16,16384]{1,0:T(8,128)(2,1)} %refs_0_.3) | copy-start | bytes 1572868
  21.2 2.9 %copy-start.1 = (bf16[16,16384]{1,0:T(8,128)(2,1)S(1)}, bf16[16,16384]{1,0:T(8,128)(2,1)}, u32[]{:S(2)}) copy-start(bf16[16,16384]{1,0:T(8,128)(2,1)} %refs_0_.3) | copy-start | bytes 1572868
  21.8 2.3 %copy-start.2 = (bf16[8,16384]{1,0:T(8,128)(2,1)S(1)}, bf16[8,16384]{1,0:T(8,128)(2,1)}, u32[]{:S(2)}) copy-start(bf16[8,16384]{1,0:T(8,128)(2,1)} %part_ref.2) | copy-start | bytes 786436
  21.8 1.4 %collective-permute-start.9 = (f32[1,16,2048]{2,1,0:T(8,128)S(1)}, f32[1,16,2048]{2,1,0:T(8,128)S(1)}, u32[]{:S(2)}, u32[]{:S(2)}) collective-permute-start(f32[1,16,2048]{2,1,0:T(8,128)S(1)} %get-tuple-element.58), channel_id=1, source_target_pairs={{0,1},{1,0},{2,3},{3,2},{4,5},{5,4},{6,7},{7,6},{8,9},{9,8},{10,11... | collective-permute-start | bytes 393224 | tf_op jit(solution)/shard_map/ppermute | solution.py:203
  21.9 4.2 %collective-permute-start.10 = (f32[96,64]{1,0:T(8,128)S(1)}, f32[96,64]{1,0:T(8,128)S(1)}, u32[]{:S(2)}, u32[]{:S(2)}) collective-permute-start(f32[96,64]{1,0:T(8,128)S(1)} %get-tuple-element.61), channel_id=1, source_target_pairs={{0,2},{1,3},{2,0},{3,1},{4,6},{5,7},{6,4},{7,5},{8,10},{9,11},{10,... | collective-permute-start | bytes 73736 | tf_op jit(solution)/shard_map/ppermute | solution.py:203
  23.2 5.6 %collective-permute-start.12 = (f32[16,2048]{1,0:T(8,128)S(1)}, f32[16,2048]{1,0:T(8,128)S(1)}, u32[]{:S(2)}, u32[]{:S(2)}) collective-permute-start(f32[16,2048]{1,0:T(8,128)S(1)} %add_bitcast_fusion), channel_id=1, source_target_pairs={{0,2},{1,3},{2,0},{3,1},{4,6},{5,7},{6,4},{7,5},{8,10},{9,11},{10,... | collective-permute-start | bytes 393224 | tf_op jit(solution)/shard_map/ppermute | solution.py:203
  26.7 2.2 %collective-permute-start.11 = (f32[1,16,2048]{2,1,0:T(8,128)S(1)}, f32[1,16,2048]{2,1,0:T(8,128)S(1)}, u32[]{:S(2)}, u32[]{:S(2)}) collective-permute-start(f32[1,16,2048]{2,1,0:T(8,128)S(1)} %get-tuple-element.66), channel_id=1, source_target_pairs={{0,1},{1,0},{2,3},{3,2},{4,5},{5,4},{6,7},{7,6},{8,9},{9,8},{10,11... | collective-permute-start | bytes 393224 | tf_op jit(solution)/shard_map/ppermute | solution.py:203

commit v8 on v7

--- a/solution.py
+++ b/solution.py
@@ -159,10 +159,9 @@
     return out
 
 
-def guest_kernel(part_ref, packed_ref, *refs):
-    *blocks, out_ref, own_ref = refs
+def guest_kernel(part_ref, *refs):
+    *blocks, out_ref = refs
     out_ref[...] = correlate(part_ref, blocks)
-    own_ref[...] = packed_ref[...]
 
 
 def near_scores_kernel(part_ref, weights_ref, *refs):
@@ -232,12 +231,12 @@
         got.append(lax.ppermute(x, "dom", [(d, d ^ s) for d in range(dom)]))
 
     guests = across(particles, last)
-    back, got[0] = call(
+    (back,) = call(
         guest_kernel,
         "guest_scores",
-        [((n * ROT // PAIR, PAIR * k // 2), f32), (packed[0].shape, bf16)],
-        [vmem] * (2 + last),
-    )(guests, packed[0], *near)
+        [((n * ROT // PAIR, PAIR * k // 2), f32)],
+        [vmem] * (1 + last),
+    )(guests, *near)
     send_shape = (max(last // 2, 1), per, cols)
     first = dom // 2
     early_stack, early = call(
@@ -246,7 +245,7 @@
         [((n * first * COARSE, cols), bf16), ((FINE * k // 2, cols), f32)],
         [vmem] * first,
     )(*got[:first])
-    got = got[:first] + after(got[first:], early)
+    got = got[:first] + after(got[first:], (early, back))
     late_stack, keep, send = call(
         far_sums_kernel,
         "far_sums",

time: 29.8 us -> 29.8 us (level)
  no operation moved by 1% of the time
where the time goes in v8:
time: 29.8 us; the launch traced here: 29.5 us
  starting transfers between devices  15.8 us (53%)
  Pallas kernels  7.58 us (25%)
  waiting for transfers between devices  3.01 us (10%)
  local copies, waits for them, and re-layouts  1.74 us (6%)
  between operations  0.73 us (2%)
  other arithmetic  0.7 us (2%)
    ppermute x7, starting transfers between devices, on_device(): got.append(lax.ppermute(x, 'dom', [(d, d ^ s) for d in range(dom)]))  11.1 us
    ppermute x6, starting transfers between devices, across(): return lax.ppermute(x, 'cls', [(c, c ^ bit) for c in range(groups)])  4.65 us
    ppermute x6, waiting for transfers between devices, across(): return lax.ppermute(x, 'cls', [(c, c ^ bit) for c in range(groups)])  1.81 us
    pallas_call x1, Pallas kernels, on_device(): call(near_scores_kernel, 'near_scores', [((n, k // 2), f32)], [vmem] * (2...  1.74 us
    unnamed x8, local copies, waits for them, and re-layouts  1.74 us
    pallas_call x1, Pallas kernels, on_device(): call(guest_kernel, 'guest_scores', [((n * ROT // PAIR, PAIR * k // 2), f3...  1.55 us
    pallas_call x1, Pallas kernels, on_device(): call(pack_kernel, 'pack', [((n, cols + ROT * k), bf16)] * dom, [vmem] * 3...  1.29 us
    pallas_call x1, Pallas kernels, on_device(): call(scores_kernel, 'scores', [((n, k), f32)], [vmem] * 3)  1.29 us
  transfers between devices with their start and end apart: 13, of which 6 were waited for; matrix products, arithmetic and copies ran while one was open for 0% of the time, Pallas kernels for 24%

profile of v8, /device:TPU:0, one launch (start us, length us, event | category | flops | bytes accessed | tf_op | source)
XLA Modules:
  0.0 29.5 jit_solution(17308351438485468716)
XLA Ops:
  0.6 0.5 %collective-permute-start = (bf16[16,16384]{1,0:T(8,128)(2,1)}, bf16[16,16384]{1,0:T(8,128)(2,1)S(1)}, u32[]{:S(2)}, u32[]{:S(2)}) collective-permute-start(bf16[16,16384]{1,0:T(8,128)(2,1)} %refs_0_.3), channel_id=1, source_target_pairs={{0,1},{1,0},{2,3},{3,2},{4,5},{5,4},{6,7},{7,6},{8,9},{9,8},{10,11... | collective-permute-start | bytes 1572872 | tf_op jit(solution)/shard_map/ppermute | solution.py:202
  1.1 2.6 %collective-permute-start.8 = (bf16[8,16384]{1,0:T(8,128)(2,1)}, bf16[8,16384]{1,0:T(8,128)(2,1)S(1)}, u32[]{:S(2)}, u32[]{:S(2)}) collective-permute-start(bf16[8,16384]{1,0:T(8,128)(2,1)} %part_ref.2), channel_id=1, source_target_pairs={{0,2},{1,3},{2,0},{3,1},{4,6},{5,7},{6,4},{7,5},{8,10},{9,11},{10,... | collective-permute-start | bytes 786440 | tf_op jit(solution)/shard_map/ppermute | solution.py:202
  3.7 0.0 copy-start.3
  3.7 0.7 %copy-done.3 = s32[8,64]{1,0:T(8,128)S(1)} copy-done((s32[8,64]{1,0:T(8,128)S(1)}, s32[8,64]{1,0:T(8,128)}, u32[]{:S(2)}) %copy-start.3) | copy-done | bytes 2072
  4.4 1.3 %pack.1 = (bf16[8,3584]{1,0:T(8,128)(2,1)S(1)}, bf16[8,3584]{1,0:T(8,128)(2,1)S(1)}, bf16[8,3584]{1,0:T(8,128)(2,1)S(1)}, bf16[8,3584]{1,0:T(8,128)(2,1)S(1)}, b...) custom-call(bf16[8,16384]{1,0:T(8,128)(2,1)} %part_ref.2, ...), custom_call_target="tpu_custom_call" | custom-call | tf_op jit(solution)/shard_map/pack/pallas_call | solution.py:220
  5.7 0.0 collective-permute-done.refs_1_
  5.7 4.6 %collective-permute-start.1 = (bf16[8,3584]{1,0:T(8,128)(2,1)S(1)}, bf16[8,3584]{1,0:T(8,128)(2,1)S(1)}, u32[]{:S(2)}, u32[]{:S(2)}) collective-permute-start(bf16[8,3584]{1,0:T(8,128)(2,1)S(1)} %get-tuple-element.42), channel_id=1, source_target_pairs={{0,28},{4,24},{8,20},{12,16},{16,12},{20,8},{24,4},{28,0},{1,29},{... | collective-permute-start | bytes 172040 | tf_op jit(solution)/shard_map/ppermute | solution.py:231
  10.3 0.2 collective-permute-start.2
  10.6 0.8 %collective-permute-start.3 = (bf16[8,3584]{1,0:T(8,128)(2,1)S(1)}, bf16[8,3584]{1,0:T(8,128)(2,1)S(1)}, u32[]{:S(2)}, u32[]{:S(2)}) collective-permute-start(bf16[8,3584]{1,0:T(8,128)(2,1)S(1)} %get-tuple-element.44), channel_id=1, source_target_pairs={{0,20},{4,16},{8,28},{12,24},{16,4},{20,0},{24,12},{28,8},{1,21},{... | collective-permute-start | bytes 172040 | tf_op jit(solution)/shard_map/ppermute | solution.py:231
  11.3 2.1 %collective-permute-start.4 = (bf16[8,3584]{1,0:T(8,128)(2,1)S(1)}, bf16[8,3584]{1,0:T(8,128)(2,1)S(1)}, u32[]{:S(2)}, u32[]{:S(2)}) collective-permute-start(bf16[8,3584]{1,0:T(8,128)(2,1)S(1)} %get-tuple-element.46), channel_id=1, source_target_pairs={{0,16},{4,20},{8,24},{12,28},{16,0},{20,4},{24,8},{28,12},{1,17},{... | collective-permute-start | bytes 172040 | tf_op jit(solution)/shard_map/ppermute | solution.py:231
  13.5 0.0 collective-permute-done.8.part_ref
  13.5 2.2 %collective-permute-start.5 = (bf16[8,3584]{1,0:T(8,128)(2,1)S(1)}, bf16[8,3584]{1,0:T(8,128)(2,1)S(1)}, u32[]{:S(2)}, u32[]{:S(2)}) collective-permute-start(bf16[8,3584]{1,0:T(8,128)(2,1)S(1)} %get-tuple-element.47), channel_id=1, source_target_pairs={{0,12},{4,8},{8,4},{12,0},{16,28},{20,24},{24,20},{28,16},{1,13},{... | collective-permute-start | bytes 172040 | tf_op jit(solution)/shard_map/ppermute | solution.py:231
  15.6 0.0 collective-permute-done.1.refs_1_
  15.6 0.8 %collective-permute-start.6 = (bf16[8,3584]{1,0:T(8,128)(2,1)S(1)}, bf16[8,3584]{1,0:T(8,128)(2,1)S(1)}, u32[]{:S(2)}, u32[]{:S(2)}) collective-permute-start(bf16[8,3584]{1,0:T(8,128)(2,1)S(1)} %get-tuple-element.48), channel_id=1, source_target_pairs={{0,8},{4,12},{8,0},{12,4},{16,24},{20,28},{24,16},{28,20},{1,9},{5... | collective-permute-start | bytes 172040 | tf_op jit(solution)/shard_map/ppermute | solution.py:231
  16.4 0.2 collective-permute-done.2.refs_2_
  16.7 0.5 %collective-permute-start.7 = (bf16[8,3584]{1,0:T(8,128)(2,1)S(1)}, bf16[8,3584]{1,0:T(8,128)(2,1)S(1)}, u32[]{:S(2)}, u32[]{:S(2)}) collective-permute-start(bf16[8,3584]{1,0:T(8,128)(2,1)S(1)} %get-tuple-element.49), channel_id=1, source_target_pairs={{0,4},{4,0},{8,12},{12,8},{16,20},{20,16},{24,28},{28,24},{1,5},{5... | collective-permute-start | bytes 172040 | tf_op jit(solution)/shard_map/ppermute | solution.py:231
  17.1 0.0 copy-start
  17.1 1.0 %copy-done = bf16[16,16384]{1,0:T(8,128)(2,1)S(1)} copy-done((bf16[16,16384]{1,0:T(8,128)(2,1)S(1)}, bf16[16,16384]{1,0:T(8,128)(2,1)}, u32[]{:S(2)}) %copy-start) | copy-done | bytes 524312
  18.2 1.5 %guest_scores.1 = f32[96,64]{1,0:T(8,128)S(1)} custom-call(bf16[8,16384]{1,0:T(8,128)(2,1)S(1)} %collective-permute-done.8.part_ref, bf16[16,16384]{1,0:T(8,128)(2,1)S(1)} %copy-done, bf16[16,16384]{1,0:T(8,128)(2,1)S(1)} %collective-permute-done.refs_1_), custom_call_target="tpu_custom_call" | custom-call | tf_op jit(solution)/shard_map/guest_scores/pallas_call | solution.py:234
  19.7 0.0 collective-permute-done.3.refs_3_
  19.7 0.4 %early_sums.1 = (bf16[192,2048]{1,0:T(8,128)(2,1)S(1)}, f32[128,2048]{1,0:T(8,128)S(1)}) custom-call(bf16[8,3584]{1,0:T(8,128)(2,1)S(1)} %get-tuple-element.41.refs_0_.weights_ref, bf16[8,3584]{1,0:T(8,128)(2,1)S(1)} %collective-permute-done.1.refs_1_, bf16[8,3584]{1,0:T(8,128)(2,1)S(1)} %collective-permute-done.2.refs_2_, ...), custom_call_target="tpu_custom_call" | custom-call | tf_op jit(solution)/shard_map/early_sums/pallas_call | solution.py:242
  20.2 0.4 %collective-permute-done.4.refs_0_.refs_4_ = bf16[8,3584]{1,0:T(8,128)(2,1)S(1)} collective-permute-done((bf16[8,3584]{1,0:T(8,128)(2,1)S(1)}, bf16[8,3584]{1,0:T(8,128)(2,1)S(1)}, u32[]{:S(2)}, u32[]{:S(2)}) %collective-permute-start.4) | collective-permute-done | bytes 57376 | tf_op jit(solution)/shard_map/ppermute | solution.py:231
  20.6 0.0 collective-permute-done.5.refs_1_.refs_5_
  20.7 0.5 %collective-permute-done.6.refs_2_.refs_6_ = bf16[8,3584]{1,0:T(8,128)(2,1)S(1)} collective-permute-done((bf16[8,3584]{1,0:T(8,128)(2,1)S(1)}, bf16[8,3584]{1,0:T(8,128)(2,1)S(1)}, u32[]{:S(2)}, u32[]{:S(2)}) %collective-permute-start.6) | collective-permute-done | bytes 57376 | tf_op jit(solution)/shard_map/ppermute | solution.py:231
  21.1 0.0 collective-permute-done.7.refs_3_.refs_7_
  21.2 0.0 copy-start.1
  21.2 0.6 %far_sums.1 = (bf16[192,2048]{1,0:T(8,128)(2,1)S(1)}, f32[1,16,2048]{2,1,0:T(8,128)S(1)}, f32[1,16,2048]{2,1,0:T(8,128)S(1)}) custom-call(f32[128,2048]{1,0:T(8,128)S(1)} %get-tuple-element.45.early_ref, bf16[8,3584]{1,0:T(8,128)(2,1)S(1)} %collective-permute-done.4.refs_0_.refs_4_, bf16[8,3584]{1,0:T(8,128)(2,1)S(1)} %collective-permute-done.5.refs_1_.refs_5_, ...), custom_call_target="tpu_custom_call" | custom-call | tf_op jit(solution)/shard_map/far_sums/pallas_call | solution.py:249
  21.8 0.0 copy-start.2
  21.8 0.1 collective-permute-start.9
  21.9 0.6 %collective-permute-start.10 = (f32[96,64]{1,0:T(8,128)S(1)}, f32[96,64]{1,0:T(8,128)S(1)}, u32[]{:S(2)}, u32[]{:S(2)}) collective-permute-start(f32[96,64]{1,0:T(8,128)S(1)} %guest_scores.1), channel_id=1, source_target_pairs={{0,2},{1,3},{2,0},{3,1},{4,6},{5,7},{6,4},{7,5},{8,10},{9,11},{10,... | collective-permute-start | bytes 73736 | tf_op jit(solution)/shard_map/ppermute | solution.py:202
  22.5 0.8 %collective-permute-done.9 = f32[1,16,2048]{2,1,0:T(8,128)S(1)} collective-permute-done((f32[1,16,2048]{2,1,0:T(8,128)S(1)}, f32[1,16,2048]{2,1,0:T(8,128)S(1)}, u32[]{:S(2)}, u32[]{:S(2)}) %collective-permute-start.9) | collective-permute-done | bytes 131104 | tf_op jit(solution)/shard_map/ppermute | solution.py:202
  23.2 0.8 %collective-permute-start.12 = (f32[16,2048]{1,0:T(8,128)S(1)}, f32[16,2048]{1,0:T(8,128)S(1)}, u32[]{:S(2)}, u32[]{:S(2)}) collective-permute-start(f32[16,2048]{1,0:T(8,128)S(1)} %add_bitcast_fusion), channel_id=1, source_target_pairs={{0,2},{1,3},{2,0},{3,1},{4,6},{5,7},{6,4},{7,5},{8,10},{9,11},{10,... | collective-permute-start | bytes 393224 | tf_op jit(solution)/shard_map/ppermute | solution.py:202
  24.1 0.0 copy-done.1
  24.1 0.0 copy-done.2
  24.1 1.7 %near_scores.1.near_ref = f32[8,32]{1,0:T(8,128)S(1)} custom-call(bf16[8,16384]{1,0:T(8,128)(2,1)S(1)} %copy-done.2, bf16[8,3584]{1,0:T(8,128)(2,1)S(1)} %get-tuple-element.41.refs_0_.weights_ref, bf16[16,16384]{1,0:T(8,128)(2,1)S(1)} %copy-done.1, bf16[16,16384]{1,0:T(8,128)(2,1)S(1)} %collective-permute-done.refs_1_), custom_call_target="tpu_custom_call" | custom-call | tf_op jit(solution)/shard_map/near_scores/pallas_call | solution.py:258
  25.8 0.2 collective-permute-done.10.back_ref
  26.1 0.6 %near_sums.1 = (f32[1,16,2048]{2,1,0:T(8,128)S(1)}, f32[1,16,2048]{2,1,0:T(8,128)S(1)}) custom-call(bf16[192,2048]{1,0:T(8,128)(2,1)S(1)} %get-tuple-element.58.early_ref, bf16[192,2048]{1,0:T(8,128)(2,1)S(1)} %get-tuple-element.60.late_ref, bf16[8,3584]{1,0:T(8,128)(2,1)S(1)} %get-tuple-element.41.refs_0_.weights_ref, ...), custom_call_target="tpu_custom_call" | custom-call | tf_op jit(solution)/shard_map/near_sums/pallas_call | solution.py:263
  26.7 0.1 collective-permute-start.11
  26.8 1.3 %scores.1 = f32[8,64]{1,0:T(8,128)} custom-call(f32[8,32]{1,0:T(8,128)S(1)} %near_scores.1.near_ref, f32[96,64]{1,0:T(8,128)S(1)} %collective-permute-done.10.back_ref, bf16[8,3584]{1,0:T(8,128)(2,1)S(1)} %get-tuple-element.41.refs_0_.weights_ref), custom_call_target="tpu_custom_call" | custom-call | tf_op jit(solution)/shard_map/scores/pallas_call | solution.py:268
  28.1 0.8 %collective-permute-done.12 = f32[16,2048]{1,0:T(8,128)S(1)} collective-permute-done((f32[16,2048]{1,0:T(8,128)S(1)}, f32[16,2048]{1,0:T(8,128)S(1)}, u32[]{:S(2)}, u32[]{:S(2)}) %collective-permute-start.12) | collective-permute-done | bytes 131104 | tf_op jit(solution)/shard_map/ppermute | solution.py:202
  28.9 0.0 collective-permute-done.11
  28.9 0.7 %fusion = f32[16,2048]{1,0:T(8,128)} fusion(f32[16,2048]{1,0:T(8,128)S(1)} %collective-permute-done.12, f32[1,16,2048]{2,1,0:T(8,128)S(1)} %get-tuple-element.61, f32[1,16,2048]{2,1,0:T(8,128)S(1)} %collective-permute-done.11), kind=kLoop, calls=%fused_computation.1 | loop fusion | flops 98304 | bytes 524288 | tf_op jit(solution)/shard_map/div | solution.py:270
  (1 shorter events, 0.0 us)
Async XLA Ops:
  0.6 5.1 %collective-permute-start = (bf16[16,16384]{1,0:T(8,128)(2,1)}, bf16[16,16384]{1,0:T(8,128)(2,1)S(1)}, u32[]{:S(2)}, u32[]{:S(2)}) collective-permute-start(bf16[16,16384]{1,0:T(8,128)(2,1)} %refs_0_.3), channel_id=1, source_target_pairs={{0,1},{1,0},{2,3},{3,2},{4,5},{5,4},{6,7},{7,6},{8,9},{9,8},{10,11... | collective-permute-start | bytes 1572872 | tf_op jit(solution)/shard_map/ppermute | solution.py:202
  1.1 12.3 %collective-permute-start.8 = (bf16[8,16384]{1,0:T(8,128)(2,1)}, bf16[8,16384]{1,0:T(8,128)(2,1)S(1)}, u32[]{:S(2)}, u32[]{:S(2)}) collective-permute-start(bf16[8,16384]{1,0:T(8,128)(2,1)} %part_ref.2), channel_id=1, source_target_pairs={{0,2},{1,3},{2,0},{3,1},{4,6},{5,7},{6,4},{7,5},{8,10},{9,11},{10,... | collective-permute-start | bytes 786440 | tf_op jit(solution)/shard_map/ppermute | solution.py:202
  3.7 0.7 %copy-start.3 = (s32[8,64]{1,0:T(8,128)S(1)}, s32[8,64]{1,0:T(8,128)}, u32[]{:S(2)}) copy-start(s32[8,64]{1,0:T(8,128)} %mask_ref.1) | copy-start | bytes 6148
  5.7 9.9 %collective-permute-start.1 = (bf16[8,3584]{1,0:T(8,128)(2,1)S(1)}, bf16[8,3584]{1,0:T(8,128)(2,1)S(1)}, u32[]{:S(2)}, u32[]{:S(2)}) collective-permute-start(bf16[8,3584]{1,0:T(8,128)(2,1)S(1)} %get-tuple-element.42), channel_id=1, source_target_pairs={{0,28},{4,24},{8,20},{12,16},{16,12},{20,8},{24,4},{28,0},{1,29},{... | collective-permute-start | bytes 172040 | tf_op jit(solution)/shard_map/ppermute | solution.py:231
  10.3 6.3 %collective-permute-start.2 = (bf16[8,3584]{1,0:T(8,128)(2,1)S(1)}, bf16[8,3584]{1,0:T(8,128)(2,1)S(1)}, u32[]{:S(2)}, u32[]{:S(2)}) collective-permute-start(bf16[8,3584]{1,0:T(8,128)(2,1)S(1)} %get-tuple-element.43), channel_id=1, source_target_pairs={{0,24},{4,28},{8,16},{12,20},{16,8},{20,12},{24,0},{28,4},{1,25},{... | collective-permute-start | bytes 172040 | tf_op jit(solution)/shard_map/ppermute | solution.py:231
  10.6 9.2 %collective-permute-start.3 = (bf16[8,3584]{1,0:T(8,128)(2,1)S(1)}, bf16[8,3584]{1,0:T(8,128)(2,1)S(1)}, u32[]{:S(2)}, u32[]{:S(2)}) collective-permute-start(bf16[8,3584]{1,0:T(8,128)(2,1)S(1)} %get-tuple-element.44), channel_id=1, source_target_pairs={{0,20},{4,16},{8,28},{12,24},{16,4},{20,0},{24,12},{28,8},{1,21},{... | collective-permute-start | bytes 172040 | tf_op jit(solution)/shard_map/ppermute | solution.py:231
  11.3 9.3 %collective-permute-start.4 = (bf16[8,3584]{1,0:T(8,128)(2,1)S(1)}, bf16[8,3584]{1,0:T(8,128)(2,1)S(1)}, u32[]{:S(2)}, u32[]{:S(2)}) collective-permute-start(bf16[8,3584]{1,0:T(8,128)(2,1)S(1)} %get-tuple-element.46), channel_id=1, source_target_pairs={{0,16},{4,20},{8,24},{12,28},{16,0},{20,4},{24,8},{28,12},{1,17},{... | collective-permute-start | bytes 172040 | tf_op jit(solution)/shard_map/ppermute | solution.py:231
  13.5 7.2 %collective-permute-start.5 = (bf16[8,3584]{1,0:T(8,128)(2,1)S(1)}, bf16[8,3584]{1,0:T(8,128)(2,1)S(1)}, u32[]{:S(2)}, u32[]{:S(2)}) collective-permute-start(bf16[8,3584]{1,0:T(8,128)(2,1)S(1)} %get-tuple-element.47), channel_id=1, source_target_pairs={{0,12},{4,8},{8,4},{12,0},{16,28},{20,24},{24,20},{28,16},{1,13},{... | collective-permute-start | bytes 172040 | tf_op jit(solution)/shard_map/ppermute | solution.py:231
  15.6 5.5 %collective-permute-start.6 = (bf16[8,3584]{1,0:T(8,128)(2,1)S(1)}, bf16[8,3584]{1,0:T(8,128)(2,1)S(1)}, u32[]{:S(2)}, u32[]{:S(2)}) collective-permute-start(bf16[8,3584]{1,0:T(8,128)(2,1)S(1)} %get-tuple-element.48), channel_id=1, source_target_pairs={{0,8},{4,12},{8,0},{12,4},{16,24},{20,28},{24,16},{28,20},{1,9},{5... | collective-permute-start | bytes 172040 | tf_op jit(solution)/shard_map/ppermute | solution.py:231
  16.7 4.5 %collective-permute-start.7 = (bf16[8,3584]{1,0:T(8,128)(2,1)S(1)}, bf16[8,3584]{1,0:T(8,128)(2,1)S(1)}, u32[]{:S(2)}, u32[]{:S(2)}) collective-permute-start(bf16[8,3584]{1,0:T(8,128)(2,1)S(1)} %get-tuple-element.49), channel_id=1, source_target_pairs={{0,4},{4,0},{8,12},{12,8},{16,20},{20,16},{24,28},{28,24},{1,5},{5... | collective-permute-start | bytes 172040 | tf_op jit(solution)/shard_map/ppermute | solution.py:231
  17.1 1.0 %copy-start = (bf16[16,16384]{1,0:T(8,128)(2,1)S(1)}, bf16[16,16384]{1,0:T(8,128)(2,1)}, u32[]{:S(2)}) copy-start(bf16[16,16384]{1,0:T(8,128)(2,1)} %refs_0_.3) | copy-start | bytes 1572868
  21.2 2.9 %copy-start.1 = (bf16[16,16384]{1,0:T(8,128)(2,1)S(1)}, bf16[16,16384]{1,0:T(8,128)(2,1)}, u32[]{:S(2)}) copy-start(bf16[16,16384]{1,0:T(8,128)(2,1)} %refs_0_.3) | copy-start | bytes 1572868
  21.8 2.3 %copy-start.2 = (bf16[8,16384]{1,0:T(8,128)(2,1)S(1)}, bf16[8,16384]{1,0:T(8,128)(2,1)}, u32[]{:S(2)}) copy-start(bf16[8,16384]{1,0:T(8,128)(2,1)} %part_ref.2) | copy-start | bytes 786436
  21.8 1.4 %collective-permute-start.9 = (f32[1,16,2048]{2,1,0:T(8,128)S(1)}, f32[1,16,2048]{2,1,0:T(8,128)S(1)}, u32[]{:S(2)}, u32[]{:S(2)}) collective-permute-start(f32[1,16,2048]{2,1,0:T(8,128)S(1)} %get-tuple-element.55), channel_id=1, source_target_pairs={{0,1},{1,0},{2,3},{3,2},{4,5},{5,4},{6,7},{7,6},{8,9},{9,8},{10,11... | collective-permute-start | bytes 393224 | tf_op jit(solution)/shard_map/ppermute | solution.py:202
  21.9 4.2 %collective-permute-start.10 = (f32[96,64]{1,0:T(8,128)S(1)}, f32[96,64]{1,0:T(8,128)S(1)}, u32[]{:S(2)}, u32[]{:S(2)}) collective-permute-start(f32[96,64]{1,0:T(8,128)S(1)} %guest_scores.1), channel_id=1, source_target_pairs={{0,2},{1,3},{2,0},{3,1},{4,6},{5,7},{6,4},{7,5},{8,10},{9,11},{10,... | collective-permute-start | bytes 73736 | tf_op jit(solution)/shard_map/ppermute | solution.py:202
  23.2 5.6 %collective-permute-start.12 = (f32[16,2048]{1,0:T(8,128)S(1)}, f32[16,2048]{1,0:T(8,128)S(1)}, u32[]{:S(2)}, u32[]{:S(2)}) collective-permute-start(f32[16,2048]{1,0:T(8,128)S(1)} %add_bitcast_fusion), channel_id=1, source_target_pairs={{0,2},{1,3},{2,0},{3,1},{4,6},{5,7},{6,4},{7,5},{8,10},{9,11},{10,... | collective-permute-start | bytes 393224 | tf_op jit(solution)/shard_map/ppermute | solution.py:202
  26.7 2.2 %collective-permute-start.11 = (f32[1,16,2048]{2,1,0:T(8,128)S(1)}, f32[1,16,2048]{2,1,0:T(8,128)S(1)}, u32[]{:S(2)}, u32[]{:S(2)}) collective-permute-start(f32[1,16,2048]{2,1,0:T(8,128)S(1)} %get-tuple-element.62), channel_id=1, source_target_pairs={{0,1},{1,0},{2,3},{3,2},{4,5},{5,4},{6,7},{7,6},{8,9},{9,8},{10,11... | collective-permute-start | bytes 393224 | tf_op jit(solution)/shard_map/ppermute | solution.py:202
